TPU v7x, 512 devices: a whole 4x4x16 slice. The times are simulated.
512 devices in a mesh: mem: 8 (over z_lo), hor: 64 (over z_hi, x, y, core).
Axes of the slice: x: 4, y: 4, z: 16 (z_hi: 2, z_lo: 8; z = z_hi * 8 + z_lo), core: 2. Of those that a mesh axis runs over, the one named last changes fastest.
Arguments:
- fine_increment: float32 [4, 4608, 768], P(None, 'hor', 'mem'), may hold values from -6 to 6
- row_taps: float32 [4, 2304], P(None, 'hor'), may hold values from 0 to 0.45, as said below
- col_weights: float32 [768, 384], replicated, may hold values from 0 to 0.45, as said below
- prior: bfloat16 [80, 4, 2304, 384], P('mem', None, 'hor'), may hold values from -6 to 6
- posterior: bfloat16 [80, 4, 2304, 384], P('mem', None, 'hor'), may hold values from -4 to 4
Outputs:
- recentred: bfloat16 [80, 4, 2304, 384], P('mem', None, 'hor')
Inputs may be any that keep to these rules, and one draw needn't show every extreme that they name: row_taps[t, g] is zero where control-grid row 2 g - 1 + t lies outside rows 0 to 4607. Column c of col_weights is zero outside rows 2 c - 1 to 2 c + 2.
All inputs are finite; a program needn't handle non-finite values.
Results may differ from a plain program's by a relative error of at most 0.001.
Values sent between devices are 32-bit elements; how exact they have to be, the bound alone decides.
No kernel may reach another device: no remote copies, remote signals or barrier semaphores. Data moves between devices by JAX's collectives and lax.ppermute only.
A program may use at most 64 MiB of HBM per device.

v0:
```python
import jax
import jax.numpy as jnp
from jax import lax
from jax.sharding import PartitionSpec as P


def extended(x, sides, width):
    for axis, dim in sides:
        count, length = (lax.axis_size(axis), x.shape[dim])
        up = [(i, (i + 1) % count) for i in range(count - 1)]
        down = [(j, i) for i, j in up]
        last = lax.slice_in_dim(x, length - width, length, axis=dim)
        leading = lax.slice_in_dim(x, 0, width, axis=dim)
        before = lax.ppermute(last, axis, up)
        after = lax.ppermute(leading, axis, down)
        x = jnp.concatenate([before, x, after], axis=dim)
    return x


def restrict_rows(padded_rows, taps):
    count = taps.shape[1]
    total = taps[0][None, :, None] * padded_rows[:, 0 : 2 * count : 2, :]
    for offset in range(1, 4):
        total = (
            total + taps[offset][None, :, None] * padded_rows[:, offset : offset + 2 * count : 2, :]
        )
    return total


def on_device(fine_increment, row_taps, col_weights, prior, posterior):
    colres = jnp.einsum(
        "lrj,jc->lrc",
        lax.all_gather(fine_increment, "mem", axis=2, tiled=True),
        col_weights,
        precision=lax.Precision.HIGHEST,
    )
    rimmed = extended(colres, (("hor", 1),), 1)
    increment = restrict_rows(rimmed, row_taps)
    before = prior.astype(jnp.float32)
    after = posterior.astype(jnp.float32)
    count = prior.shape[0] * lax.axis_size("mem")
    prior_total, post_total = lax.psum((jnp.sum(before, axis=0), jnp.sum(after, axis=0)), "mem")
    prior_mean = prior_total / count
    post_mean = post_total / count
    prior_dev = before - prior_mean
    post_dev = after - post_mean
    prior_square, post_square = lax.psum(
        (jnp.sum(prior_dev * prior_dev, axis=0), jnp.sum(post_dev * post_dev, axis=0)), "mem"
    )
    prior_var = prior_square / (count - 1)
    post_var = post_square / (count - 1)
    prior_spread = jnp.sqrt(prior_var + 1e-06)
    post_spread = jnp.sqrt(post_var + 1e-06)
    factor = 1.0 + 0.9 * (prior_spread - post_spread) / post_spread
    return (prior_mean + increment + factor * post_dev).astype(jnp.bfloat16)


def solution(mesh):
    return jax.shard_map(
        on_device,
        mesh=mesh,
        in_specs=(
            P(None, "hor", "mem"),
            P(None, "hor"),
            P(),
            P("mem", None, "hor", None),
            P("mem", None, "hor", None),
        ),
        out_specs=P("mem", None, "hor", None),
        check_vma=False,
    )
```

profile of v0, /device:TPU:2, one launch (start us, length us, event | category | flops | bytes accessed | tf_op | source)
XLA Modules:
  0.0 273.7 jit_solution(3497087549695168484)
XLA Ops:
  6.5 1.9 convert_reduce_fusion
  8.5 0.7 copy.14
  9.2 0.5 convert_reduce_fusion.1
  9.7 0.7 copy.9
  10.5 0.1 copy.10
  10.6 60.8 %all_gather.3 = f32[4,72,768]{1,0,2:T(4,128)S(1)} all-gather(f32[4,72,96]{1,0,2:T(4,128)S(1)} %copy.10), channel_id=1, replica_groups=mesh['mem'=8,'hor'=64] {'mem'}, dimensions={2}, use_global_device_ids=true | all-gather | bytes 995328 | tf_op jit(solution)/shard_map/all_gather | solution.py:33
  71.4 3.1 %fusion.7 = f32[4,72,384]{2,1,0:T(8,128)S(1)} fusion(f32[4,72,768]{1,0,2:T(4,128)S(1)} %all_gather.3, f32[768,384]{1,0:T(8,128)S(1)} %copy-done), kind=kOutput, calls=%fused_computation.11 | convolution fusion | flops 1019215872 | bytes 2506752 | tf_op jit(solution)/shard_map/lrj,jc->lrc/dot_general | solution.py:31
  74.6 1.9 collective-permute-start
  76.5 5.8 %collective-permute-start.1 = (f32[4,1,384]{2,1,0:T(1,128)S(1)}, f32[4,1,384]{2,1,0:T(1,128)S(1)}, u32[]{:S(2)}, u32[]{:S(2)}) collective-permute-start(f32[4,1,384]{2,1,0:T(1,128)S(1)} %get-tuple-element.10), channel_id=1, source_target_pairs={{1,0},{2,1},{3,2},{4,3},{5,4},{6,5},{7,6},{8,7},{9,8},{10,9},{11,1... | collective-permute-start | bytes 18440 | tf_op jit(solution)/shard_map/ppermute | solution.py:15
  82.3 0.8 slice.35
  83.1 0.5 collective-permute-done.1
  83.6 0.8 slice.33
  84.5 0.8 slice.37
  85.3 1.8 slice.39
  87.1 53.4 %all-reduce.7.cloned.1.call-done = (f32[4,36,384]{2,1,0:T(8,128)}, f32[4,36,384]{2,1,0:T(8,128)}) async-done(((f32[4,36,384]{2,1,0:T(8,128)}, f32[4,36,384]{2,1,0:T(8,128)}), (f32[4,36,384]{2,1,0:T(8,128)}, f32[4,36,384]{2,1,0:T(8,128)})) %all-reduce.7.cloned.1.call-update) | async-done | bytes 442384 | tf_op jit(solution)/shard_map/psum | solution.py:42
  140.5 2.3 add_add_fusion
  142.8 0.1 copy.15
  142.9 0.7 copy-done.4
  143.5 1.5 fusion.2
  145.1 1.5 fusion.6
  146.6 1.1 copy.12
  147.6 116.1 %all-reduce.5.cloned.1.call-done = (f32[4,36,384]{2,0,1:T(4,128)}, f32[4,36,384]{2,0,1:T(4,128)}) async-done(((f32[4,36,384]{2,0,1:T(4,128)}, f32[4,36,384]{2,0,1:T(4,128)}), (f32[4,36,384]{2,0,1:T(4,128)}, f32[4,36,384]{2,0,1:T(4,128)})) %all-reduce.5.cloned.1.call-update) | async-done | bytes 442384 | tf_op jit(solution)/shard_map/psum | solution.py:47
  263.7 1.4 fusion.10
  265.1 1.7 fusion.4
  (24 shorter events, 0.2 us)
Async XLA Ops:
  6.5 64.9 %copy-start = (f32[768,384]{1,0:T(8,128)S(1)}, f32[768,384]{1,0:T(8,128)}, u32[]{:S(2)}) copy-start(f32[768,384]{1,0:T(8,128)} %param.7) | copy-start | bytes 3538948
  6.5 2.7 copy-start.2
  6.5 133.9 %all-reduce.7.cloned.1.call-start = ((), (), s32[]{:S(2)}) async-start(), calls=%async_computation.1 | async-start | bytes 983040 | tf_op jit(solution)/shard_map/psum | solution.py:42
  8.5 2.0 copy-start.6
  10.4 253.3 %all-reduce.5.cloned.1.call-start = ((), (), s32[]{:S(2)}) async-start(), calls=%async_computation | async-start | bytes 884736 | tf_op jit(solution)/shard_map/psum | solution.py:47
  71.4 10.8 %copy-start.7 = (f32[4,36]{1,0:T(4,128)S(1)}, f32[4,36]{1,0:T(4,128)}, u32[]{:S(2)}) copy-start(f32[4,36]{1,0:T(4,128)} %param.6) | copy-start | bytes 1732
  74.6 8.5 %collective-permute-start = (f32[4,1,384]{2,1,0:T(1,128)S(1)}, f32[4,1,384]{2,1,0:T(1,128)S(1)}, u32[]{:S(2)}, u32[]{:S(2)}) collective-permute-start(f32[4,1,384]{2,1,0:T(1,128)S(1)} %get-tuple-element.9), channel_id=1, source_target_pairs={{0,1},{1,2},{2,3},{3,4},{4,5},{5,6},{6,7},{7,8},{8,9},{9,10},{10,1... | collective-permute-start | bytes 18440 | tf_op jit(solution)/shard_map/ppermute | solution.py:14
  76.5 7.1 %collective-permute-start.1 = (f32[4,1,384]{2,1,0:T(1,128)S(1)}, f32[4,1,384]{2,1,0:T(1,128)S(1)}, u32[]{:S(2)}, u32[]{:S(2)}) collective-permute-start(f32[4,1,384]{2,1,0:T(1,128)S(1)} %get-tuple-element.10), channel_id=1, source_target_pairs={{1,0},{2,1},{3,2},{4,3},{5,4},{6,5},{7,6},{8,7},{9,8},{10,9},{11,1... | collective-permute-start | bytes 18440 | tf_op jit(solution)/shard_map/ppermute | solution.py:15
  83.6 0.9 copy-start.3
  85.3 58.3 %copy-start.1 = (bf16[10,4,36,384]{3,1,2,0:T(4,128)(2,1)S(1)}, bf16[10,4,36,384]{3,1,2,0:T(4,128)(2,1)}, u32[]{:S(2)}) copy-start(bf16[10,4,36,384]{3,1,2,0:T(4,128)(2,1)} %param.9) | copy-start | bytes 3317764
  142.9 0.7 copy-start.4
  146.5 118.6 %copy-start.5 = (f32[4,36,384]{2,0,1:T(4,128)S(1)}, f32[4,36,384]{2,0,1:T(4,128)}, u32[]{:S(2)}) copy-start(f32[4,36,384]{2,0,1:T(4,128)} %copy-done.4) | copy-start | bytes 663556
Sparse Core Ops, SparseCore 0:
  10.5 129.9 all-reduce.6
  146.7 116.9 all-reduce.4
where the time goes:
time: 274 us
  waiting for transfers between devices  170 us (62%)
  blocking collectives  60.8 us (22%)
  between operations  13.5 us (5%)
  other arithmetic  10.8 us (4%)
  starting transfers between devices  7.72 us (3%)
  local copies, waits for them, and re-layouts  7.66 us (3%)
  matrix products  3.11 us (1%)
    psum x1, waiting for transfers between devices, on_device(): lax.psum((jnp.sum(prior_dev * prior_dev, axis=0), jnp.sum(post_dev * post...  116 us
    all_gather x1, blocking collectives, on_device(): lax.all_gather(fine_increment, 'mem', axis=2, tiled=True)  60.8 us
    psum x1, waiting for transfers between devices, on_device(): lax.psum((jnp.sum(before, axis=0), jnp.sum(after, axis=0)), 'mem')  53.4 us
    ppermute x1, starting transfers between devices, extended(): after = lax.ppermute(leading, axis, down)  5.75 us
  transfers between devices with their start and end apart: 4, of which 3 were waited for; matrix products, arithmetic and copies ran while one was open for 3% of the time, Pallas kernels for 0%

commit v1 on v0

v1 whole, which is shorter than its diff:
```python
import functools

import jax
import jax.numpy as jnp
from jax import lax
from jax.experimental import pallas as pl
from jax.experimental.pallas import tpu as pltpu
from jax.sharding import PartitionSpec as P

CHUNK = 56
ORDER = (0, 4, 2, 6, 1, 5, 3, 7)
F32 = jnp.float32
HIGHEST = lax.Precision.HIGHEST


def pack(ref, which, level, value):
    for e in range(2):
        base = (2 * level + e) * CHUNK
        for rt in range(2):
            for ct in range(3):
                at = base + (3 * rt + ct) * 8
                row = 16 * e + 8 * rt
                ref[which, at : at + 8, :] = value[row : row + 8, 128 * ct : 128 * ct + 128]
        for ct in range(3):
            at = base + 48 + 2 * ct
            ref[which, at : at + 2, :] = value[32 + 2 * e : 34 + 2 * e, 128 * ct : 128 * ct + 128]
        ref[which, base + 54 : base + 56, :] = jnp.zeros((2, 128), F32)


def stats_kernel(m_ref, x_ref, keep_ref, send_ref, all_ref):
    m = m_ref[0]
    members = x_ref.shape[0]
    for level in range(4):
        total = x_ref[0, level].astype(F32)
        for i in range(1, members):
            total = total + x_ref[i, level].astype(F32)
        mean = total / members
        square = jnp.zeros_like(total)
        for i in range(members):
            dev = x_ref[i, level].astype(F32) - mean
            square = square + dev * dev
        pack(all_ref, 0, level, total)
        pack(all_ref, 1, level, square)
    for p in range(8):
        at = pl.multiple_of((m ^ ORDER[p]) * CHUNK, 8)
        out, to = (keep_ref, p * CHUNK) if p < 4 else (send_ref, (p - 4) * CHUNK)
        for which in range(2):
            out[which, to : to + CHUNK, :] = all_ref[which, pl.ds(at, CHUNK), :]


def stats(m, x):
    shape = jax.ShapeDtypeStruct((2, 4 * CHUNK, 128), F32)
    return pl.pallas_call(
        stats_kernel,
        out_shape=(shape, shape),
        in_specs=[pl.BlockSpec(memory_space=pltpu.SMEM), pl.BlockSpec(memory_space=pltpu.VMEM)],
        out_specs=(pl.BlockSpec(memory_space=pltpu.VMEM),) * 2,
        scratch_shapes=[pltpu.VMEM((2, 8 * CHUNK, 128), F32)],
        compiler_params=pltpu.CompilerParams(vmem_limit_bytes=16 * 2**20),
        cost_estimate=pl.CostEstimate(flops=4_000_000, bytes_accessed=2_500_000, transcendentals=0),
        name="stats",
    )(m, x)


def fine_kernel(m_ref, fine_ref, up_ref, down_ref, taps_ref, weights_ref, keep_ref, send_ref, rows_ref, all_ref):
    m = m_ref[0]
    weights = weights_ref[pl.ds(pl.multiple_of(m * 96, 32), 96), :]
    local = pltpu.roll(weights, lax.rem(385 - 48 * m, 384), 1)[:, :128]
    for level in range(4):
        rows_ref[level, 8:80, :] = fine_ref[level]
        rows_ref[level, 7:8, :] = up_ref[level]
        rows_ref[level, 80:81, :] = down_ref[level]
        total = taps_ref[:, 0:1] * rows_ref[level, pl.ds(7, 36, stride=2), :]
        for t in range(1, 4):
            total = total + taps_ref[:, t : t + 1] * rows_ref[level, pl.ds(7 + t, 36, stride=2), :]
        part = jnp.dot(total, local, precision=HIGHEST, preferred_element_type=F32)
        for e in range(2):
            k = 2 * level + e
            all_ref[10 * k : 10 * k + 8, :] = part[16 * e : 16 * e + 8] + pltpu.roll(
                part[16 * e + 8 : 16 * e + 16], 64, 1
            )
            all_ref[10 * k + 8 : 10 * k + 10, :] = part[32 + 2 * e : 34 + 2 * e]
    for p in range(8):
        k = m ^ ORDER[p]
        block = all_ref[pl.ds(k * 10, 10), :]
        out, q = (keep_ref, p) if p < 4 else (send_ref, p - 4)
        out[8 * q : 8 * q + 8, :] = block[0:8]
        out[32 + 2 * q : 34 + 2 * q, :] = block[8:10]


def fine_part(m, fine, up, down, taps, weights):
    shape = jax.ShapeDtypeStruct((40, 128), F32)
    return pl.pallas_call(
        fine_kernel,
        out_shape=(shape, shape),
        in_specs=[pl.BlockSpec(memory_space=pltpu.SMEM)] + [pl.BlockSpec(memory_space=pltpu.VMEM)] * 5,
        out_specs=(pl.BlockSpec(memory_space=pltpu.VMEM),) * 2,
        scratch_shapes=[pltpu.VMEM((4, 88, 96), F32), pltpu.VMEM((80, 128), F32)],
        compiler_params=pltpu.CompilerParams(vmem_limit_bytes=16 * 2**20),
        cost_estimate=pl.CostEstimate(flops=4_000_000, bytes_accessed=1_500_000, transcendentals=0),
        name="fine",
    )(m, fine, up, down, taps, weights)


def merged(keep, recv, count):
    diff = keep[0] - recv[0]
    return keep[0] + recv[0], keep[1] + recv[1] + diff * diff * (0.5 / count)


def factor_kernel(count, m_ref, ka_ref, ra_ref, kb_ref, rb_ref, ik_ref, ir_ref, out_ref, wide_ref):
    m = m_ref[0]
    prior_total, prior_square = merged((ka_ref[0], ka_ref[1]), (ra_ref[0], ra_ref[1]), count // 2)
    post_total, post_square = merged(
        (kb_ref[0], kb_ref[1]), (rb_ref[:CHUNK], rb_ref[CHUNK : 2 * CHUNK]), count // 2
    )
    prior_mean = prior_total / count
    post_mean = post_total / count
    prior_spread = jnp.sqrt(prior_square / (count - 1) + 1e-06)
    post_spread = jnp.sqrt(post_square / (count - 1) + 1e-06)
    factor = 1.0 + 0.9 * (prior_spread - post_spread) / post_spread
    base = prior_mean - factor * post_mean
    wide = jnp.zeros((24, 384), F32)
    lane = lax.broadcasted_iota(jnp.int32, (24, 384), 1)
    for s in range(8):
        ref, q, at = (ik_ref, s, 0) if s < 4 else (ir_ref, s - 4, 0)
        tile = ref[8 * q : 8 * q + 8, :]
        rest = ref[32 + 2 * q : 34 + 2 * q, :]
        rows = jnp.concatenate([tile, pltpu.roll(tile, 64, 1), rest, jnp.zeros((6, 128), F32)], axis=0)
        rows = jnp.concatenate([rows, jnp.zeros((24, 256), F32)], axis=1)
        rows = jnp.where(lane < 50, rows, 0.0)
        wide = wide + pltpu.roll(rows, lax.rem(48 * (m ^ s) + 383, 384), 1)
    out_ref[0] = factor
    for rt in range(2):
        for ct in range(3):
            at = (3 * rt + ct) * 8
            out_ref[1, at : at + 8, :] = base[at : at + 8] + wide[8 * rt : 8 * rt + 8, 128 * ct : 128 * ct + 128]
    for ct in range(3):
        at = 48 + 2 * ct
        out_ref[1, at : at + 2, :] = base[at : at + 2] + wide[16:18, 128 * ct : 128 * ct + 128]
    out_ref[1, 54:56, :] = base[54:56]


def factor_part(count, m, *args):
    return pl.pallas_call(
        functools.partial(factor_kernel, count),
        out_shape=jax.ShapeDtypeStruct((2, CHUNK, 128), F32),
        in_specs=[pl.BlockSpec(memory_space=pltpu.SMEM)] + [pl.BlockSpec(memory_space=pltpu.VMEM)] * 6,
        out_specs=pl.BlockSpec(memory_space=pltpu.VMEM),
        scratch_shapes=[pltpu.VMEM((24, 384), F32)],
        cost_estimate=pl.CostEstimate(flops=1_000_000, bytes_accessed=400_000, transcendentals=20_000),
        name="factor",
    )(m, *args)


def output_kernel(m_ref, near_ref, far_ref, x_ref, out_ref, all_ref, full_ref):
    m = m_ref[0]

    @pl.when(pl.program_id(0) == 0)
    def _():
        for p in range(8):
            at = pl.multiple_of((m ^ ORDER[p]) * CHUNK, 8)
            ref, q = (near_ref, p * CHUNK) if p < 4 else (far_ref, (p - 4) * CHUNK)
            for which in range(2):
                all_ref[which, pl.ds(at, CHUNK), :] = ref[which, q : q + CHUNK, :]
        for which in range(2):
            for k in range(8):
                level, e = k // 2, k % 2
                base = k * CHUNK
                for rt in range(2):
                    for ct in range(3):
                        at = base + (3 * rt + ct) * 8
                        row = 16 * e + 8 * rt
                        full_ref[which, level, row : row + 8, 128 * ct : 128 * ct + 128] = all_ref[
                            which, at : at + 8, :
                        ]
                for ct in range(3):
                    at = base + 48 + 2 * ct
                    full_ref[which, level, 32 + 2 * e : 34 + 2 * e, 128 * ct : 128 * ct + 128] = all_ref[
                        which, at : at + 2, :
                    ]

    for level in range(4):
        factor = full_ref[0, level]
        base = full_ref[1, level]
        for i in range(x_ref.shape[0]):
            out_ref[i, level] = (base + factor * x_ref[i, level].astype(F32)).astype(jnp.bfloat16)


def output(m, near, far, x):
    members = x.shape[0]
    step = 2
    block = pl.BlockSpec((step, 4, 36, 384), lambda i: (i, 0, 0, 0))
    whole = pl.BlockSpec((2, 4 * CHUNK, 128), lambda i: (0, 0, 0))
    return pl.pallas_call(
        output_kernel,
        grid=(members // step,),
        out_shape=jax.ShapeDtypeStruct(x.shape, jnp.bfloat16),
        in_specs=[pl.BlockSpec(memory_space=pltpu.SMEM), whole, whole, block],
        out_specs=block,
        scratch_shapes=[pltpu.VMEM((2, 8 * CHUNK, 128), F32), pltpu.VMEM((2, 4, 36, 384), F32)],
        compiler_params=pltpu.CompilerParams(vmem_limit_bytes=16 * 2**20),
        cost_estimate=pl.CostEstimate(flops=2_000_000, bytes_accessed=3_000_000, transcendentals=0),
        name="output",
    )(m, near, far, x)


def on_device(fine_increment, row_taps, col_weights, prior, posterior):
    count = prior.shape[0] * lax.axis_size("mem")
    hor = lax.axis_size("hor")
    m = lax.axis_index("mem").astype(jnp.int32).reshape(1)

    def swap(x, distance):
        return lax.ppermute(x, "mem", [(i, i ^ distance) for i in range(8)])

    half, quarter = 2 * CHUNK, CHUNK
    keep_a, send_a = stats(m, prior)
    recv_a = swap(send_a, 1)
    keep_b, send_b = stats(m, posterior)
    recv_b = swap(send_b, 1)

    last = fine_increment[:, -1:, :]
    first = fine_increment[:, :1, :]
    up = lax.ppermute(last, "hor", [(i, i + 1) for i in range(hor - 1)])
    down = lax.ppermute(first, "hor", [(i + 1, i) for i in range(hor - 1)])
    inc_keep, inc_send = fine_part(m, fine_increment, up, down, row_taps.T, col_weights)
    inc_recv = swap(inc_send, 1)

    total, square = merged(keep_a, recv_a, count // 8)
    a = jnp.stack([total, square])
    keep_a, send_a = a[:, :half], a[:, half:]
    recv_a = swap(send_a, 2)

    total, square = merged(keep_b, recv_b, count // 8)
    keep_b = jnp.stack([total[:half], square[:half]])
    send = jnp.concatenate(
        [total[half:], square[half:], inc_keep[16:32], inc_recv[16:32], inc_keep[36:40], inc_recv[36:40]]
    )
    inc_keep = jnp.concatenate([inc_keep[:16], inc_recv[:16], inc_keep[32:36], inc_recv[32:36]])
    recv = swap(send, 2)
    recv_b = recv[: 2 * half].reshape(2, half, 128)
    inc_recv = recv[2 * half :]

    total, square = merged(keep_a, recv_a, count // 4)
    a = jnp.stack([total, square])
    keep_a, send_a = a[:, :quarter], a[:, quarter:]
    recv_a = swap(send_a, 4)

    total, square = merged(keep_b, recv_b, count // 4)
    keep_b = jnp.stack([total[:quarter], square[:quarter]])

    def of(position):
        tiles = [x[16 * s + 8 * position : 16 * s + 8 * position + 8] for x in (inc_keep, inc_recv) for s in range(2)]
        rests = [
            x[32 + 4 * s + 2 * position : 34 + 4 * s + 2 * position] for x in (inc_keep, inc_recv) for s in range(2)
        ]
        return tiles + rests

    send = jnp.concatenate([total[quarter:], square[quarter:]] + of(1))
    inc_keep = jnp.concatenate(of(0))
    recv = swap(send, 4)
    own = factor_part(count, m, keep_a, recv_a, keep_b, recv[: 2 * quarter], inc_keep, recv[2 * quarter :])

    near = jnp.concatenate([own, swap(own, 4)], axis=1)
    near = jnp.concatenate([near, swap(near, 2)], axis=1)
    far = swap(near, 1)
    return output(m, near, far, posterior)


def solution(mesh):
    return jax.shard_map(
        on_device,
        mesh=mesh,
        in_specs=(
            P(None, "hor", "mem"),
            P(None, "hor"),
            P(),
            P("mem", None, "hor", None),
            P("mem", None, "hor", None),
        ),
        out_specs=P("mem", None, "hor", None),
        check_vma=False,
    )
```

time: 274 us -> 96.5 us (0.35)
  the two profiles are of different devices: /device:TPU:2 before, /device:TPU:256 now
where the time goes in v1:
time: 96.5 us; the launch traced here: 95.8 us
  starting transfers between devices  51 us (53%)
  waiting for transfers between devices  26.9 us (28%)
  local copies, waits for them, and re-layouts  8.8 us (9%)
  other arithmetic  4.94 us (5%)
  Pallas kernels  3.81 us (4%)
    ppermute x10, starting transfers between devices, swap(): return lax.ppermute(x, 'mem', [(i, i ^ distance) for i in range(8)])  32.5 us
    ppermute x10, waiting for transfers between devices, swap(): return lax.ppermute(x, 'mem', [(i, i ^ distance) for i in range(8)])  26.9 us
    ppermute x1, starting transfers between devices, on_device(): down = lax.ppermute(first, 'hor', [(i + 1, i) for i in range(hor - 1)])  16.6 us
    concatenate x1, local copies, waits for them, and re-layouts, on_device(): inc_keep = jnp.concatenate(of(0))  2.94 us
    unnamed x13, local copies, waits for them, and re-layouts  2.33 us
    add x4, other arithmetic, merged(): return (keep[0] + recv[0], keep[1] + recv[1] + diff * diff * (0.5 / count))  2.01 us
  transfers between devices with their start and end apart: 12, of which 6 were waited for; matrix products, arithmetic and copies ran while one was open for 10% of the time, Pallas kernels for 2%

profile of v1, /device:TPU:256, one launch (start us, length us, event | category | flops | bytes accessed | tf_op | source)
XLA Modules:
  0.0 95.8 jit_solution(8996363767528955648)
XLA Ops:
  0.7 1.9 %collective-permute-start.4 = (f32[4,1,96]{2,1,0:T(1,128)S(1)}, f32[4,1,96]{2,1,0:T(1,128)S(1)}, u32[]{:S(2)}, u32[]{:S(2)}) collective-permute-start(f32[4,1,96]{2,1,0:T(1,128)S(1)} %get-tuple-element.26), channel_id=1, source_target_pairs={{0,1},{1,2},{2,3},{3,4},{4,5},{5,6},{6,7},{7,8},{8,9},{9,10},{10,1... | collective-permute-start | bytes 4616 | tf_op jit(solution)/shard_map/ppermute | solution.py:223
  2.7 16.6 %collective-permute-start.5 = (f32[4,1,96]{2,1,0:T(1,128)S(1)}, f32[4,1,96]{2,1,0:T(1,128)S(1)}, u32[]{:S(2)}, u32[]{:S(2)}) collective-permute-start(f32[4,1,96]{2,1,0:T(1,128)S(1)} %get-tuple-element.25), channel_id=1, source_target_pairs={{1,0},{2,1},{3,2},{4,3},{5,4},{6,5},{7,6},{8,7},{9,8},{10,9},{11,1... | collective-permute-start | bytes 4616 | tf_op jit(solution)/shard_map/ppermute | solution.py:224
  19.2 1.4 %copy.6.x_ref = bf16[10,4,36,384]{3,2,1,0:T(8,128)(2,1)S(1)} copy(bf16[10,4,36,384]{3,1,2,0:T(4,128)(2,1)} %param.8) | data formatting | bytes 2211840 | tf_op args[3]
  21.3 2.9 %collective-permute-start = (f32[2,224,128]{2,1,0:T(8,128)S(1)}, f32[2,224,128]{2,1,0:T(8,128)}, u32[]{:S(2)}, u32[]{:S(2)}) collective-permute-start(f32[2,224,128]{2,1,0:T(8,128)S(1)} %get-tuple-element.12), channel_id=1, source_target_pairs={{0,64},{64,0},{128,192},{192,128},{256,320},{320,256},{384,448},{4... | collective-permute-start | bytes 688136 | tf_op jit(solution)/shard_map/ppermute | solution.py:213
  25.0 2.9 %collective-permute-start.3 = (f32[2,224,128]{2,1,0:T(8,128)S(1)}, f32[2,224,128]{2,1,0:T(8,128)}, u32[]{:S(2)}, u32[]{:S(2)}) collective-permute-start(f32[2,224,128]{2,1,0:T(8,128)S(1)} %get-tuple-element.14), channel_id=1, source_target_pairs={{0,64},{64,0},{128,192},{192,128},{256,320},{320,256},{384,448},{4... | collective-permute-start | bytes 688136 | tf_op jit(solution)/shard_map/ppermute | solution.py:213
  28.6 2.9 %collective-permute-start.6 = (f32[40,128]{1,0:T(8,128)S(1)}, f32[40,128]{1,0:T(8,128)S(1)}, u32[]{:S(2)}, u32[]{:S(2)}) collective-permute-start(f32[40,128]{1,0:T(8,128)S(1)} %get-tuple-element.16), channel_id=1, source_target_pairs={{0,64},{64,0},{128,192},{192,128},{256,320},{320,256},{384,448},{4... | collective-permute-start | bytes 61448 | tf_op jit(solution)/shard_map/ppermute | solution.py:213
  31.6 2.7 %collective-permute-done.6 = f32[40,128]{1,0:T(8,128)S(1)} collective-permute-done((f32[40,128]{1,0:T(8,128)S(1)}, f32[40,128]{1,0:T(8,128)S(1)}, u32[]{:S(2)}, u32[]{:S(2)}) %collective-permute-start.6) | collective-permute-done | bytes 20512 | tf_op jit(solution)/shard_map/ppermute | solution.py:213
  34.3 1.0 %slice_add_fusion.3 = (f32[1,224,128]{2,1,0:T(8,128)S(1)}, f32[1,224,128]{2,1,0:T(8,128)S(1)}) fusion(f32[2,224,128]{2,1,0:T(8,128)} %collective-permute-done, f32[2,224,128]{2,1,0:T(8,128)S(1)} %get-tuple-element.11), kind=kLoop, calls=%fused_computation.10 | loop fusion | flops 172032 | bytes 688128 | tf_op jit(solution)/shard_map/add | solution.py:107
  35.3 3.4 %collective-permute-start.1 = (f32[2,112,128]{2,1,0:T(8,128)S(1)}, f32[2,112,128]{2,1,0:T(8,128)S(1)}, u32[]{:S(2)}, u32[]{:S(2)}) collective-permute-start(f32[2,112,128]{2,1,0:T(8,128)S(1)} %pad_maximum_fusion.1), channel_id=1, source_target_pairs={{0,128},{64,192},{128,0},{192,64},{256,384},{320,448},{384,256},{4... | collective-permute-start | bytes 344072 | tf_op jit(solution)/shard_map/ppermute | solution.py:213
  38.7 1.0 %fusion = (f32[1,224,128]{2,1,0:T(8,128)S(1)}, f32[1,224,128]{2,1,0:T(8,128)S(1)}) fusion(f32[2,224,128]{2,1,0:T(8,128)} %collective-permute-done.3, f32[2,224,128]{2,1,0:T(8,128)S(1)} %get-tuple-element.13), kind=kLoop, calls=%fused_computation.2 | loop fusion | flops 172032 | bytes 688128 | tf_op jit(solution)/shard_map/add | solution.py:107
  39.8 3.4 %collective-permute-start.7 = (f32[264,128]{1,0:T(8,128)S(1)}, f32[264,128]{1,0:T(8,128)S(1)}, u32[]{:S(2)}, u32[]{:S(2)}) collective-permute-start(f32[264,128]{1,0:T(8,128)S(1)} %concatenate.16), channel_id=1, source_target_pairs={{0,128},{64,192},{128,0},{192,64},{256,384},{320,448},{384,256},{4... | collective-permute-start | bytes 405512 | tf_op jit(solution)/shard_map/ppermute | solution.py:213
  43.1 2.5 %collective-permute-done.1 = f32[2,112,128]{2,1,0:T(8,128)S(1)} collective-permute-done((f32[2,112,128]{2,1,0:T(8,128)S(1)}, f32[2,112,128]{2,1,0:T(8,128)S(1)}, u32[]{:S(2)}, u32[]{:S(2)}) %collective-permute-start.1) | collective-permute-done | bytes 114720 | tf_op jit(solution)/shard_map/ppermute | solution.py:213
  46.3 3.1 %collective-permute-start.2 = (f32[2,56,128]{2,1,0:T(8,128)S(1)}, f32[2,56,128]{2,1,0:T(8,128)S(1)}, u32[]{:S(2)}, u32[]{:S(2)}) collective-permute-start(f32[2,56,128]{2,1,0:T(8,128)S(1)} %get-tuple-element.35), channel_id=1, source_target_pairs={{0,256},{64,320},{128,384},{192,448},{256,0},{320,64},{384,128},{4... | collective-permute-start | bytes 172040 | tf_op jit(solution)/shard_map/ppermute | solution.py:213
  49.5 6.7 %collective-permute-start.8 = (f32[152,128]{1,0:T(8,128)S(1)}, f32[152,128]{1,0:T(8,128)S(1)}, u32[]{:S(2)}, u32[]{:S(2)}) collective-permute-start(f32[152,128]{1,0:T(8,128)S(1)} %concatenate.17), channel_id=1, source_target_pairs={{0,256},{64,320},{128,384},{192,448},{256,0},{320,64},{384,128},{4... | collective-permute-start | bytes 233480 | tf_op jit(solution)/shard_map/ppermute | solution.py:213
  56.2 2.9 %concatenate.18.ik_ref = f32[40,128]{1,0:T(8,128)} concatenate(f32[8,128]{1,0:T(8,128)S(1)} %get-tuple-element.47, f32[8,128]{1,0:T(8,128)S(1)} %get-tuple-element.45, f32[8,128]{1,0:T(8,128)S(1)} %get-tuple-element.32, f32[8,128]{1,0:T(8,128)S(1)} %get-tuple-element.31, f32[2,128]{1,0:T(2,128)S(1)} %get-tuple-element.43, f32[2,128]{1,0:T(2,128)S(1)} %get-tuple-element.41, ...), dimensions={0} | concatenate | bytes 40960 | tf_op jit(solution)/shard_map/concatenate | solution.py:259
  59.7 3.2 %collective-permute-done.8 = f32[152,128]{1,0:T(8,128)S(1)} collective-permute-done((f32[152,128]{1,0:T(8,128)S(1)}, f32[152,128]{1,0:T(8,128)S(1)}, u32[]{:S(2)}, u32[]{:S(2)}) %collective-permute-start.8) | collective-permute-done | bytes 77856 | tf_op jit(solution)/shard_map/ppermute | solution.py:213
  64.8 1.7 %factor.1 = f32[2,56,128]{2,1,0:T(8,128)} custom-call(s32[1]{0:T(128)} %bitcast.m_ref, f32[2,56,128]{2,1,0:T(8,128)} %get-tuple-element.36.ka_ref, f32[2,56,128]{2,1,0:T(8,128)} %copy-done.3, f32[2,56,128]{2,1,0:T(8,128)} %pad_maximum_fusion.4.kb_ref, f32[112,128]{1,0:T(8,128)} %slice.278.rb_ref, f32[40,128]{1,0:T(8,128)} %concatenate.18.ik_ref, ...), custom_call_target="tpu_custom_call" | custom-call | flops 1000000 | bytes 400000 | tf_op jit(solution)/shard_map/factor/pallas_call | solution.py:144
  66.5 3.4 %collective-permute-start.9 = (f32[2,56,128]{2,1,0:T(8,128)}, f32[2,56,128]{2,1,0:T(8,128)S(1)}, u32[]{:S(2)}, u32[]{:S(2)}) collective-permute-start(f32[2,56,128]{2,1,0:T(8,128)} %factor.1), channel_id=1, source_target_pairs={{0,256},{64,320},{128,384},{192,448},{256,0},{320,64},{384,128},{4... | collective-permute-start | bytes 172040 | tf_op jit(solution)/shard_map/ppermute | solution.py:213
  69.9 6.9 %collective-permute-done.9 = f32[2,56,128]{2,1,0:T(8,128)S(1)} collective-permute-done((f32[2,56,128]{2,1,0:T(8,128)}, f32[2,56,128]{2,1,0:T(8,128)S(1)}, u32[]{:S(2)}, u32[]{:S(2)}) %collective-permute-start.9) | collective-permute-done | bytes 57376 | tf_op jit(solution)/shard_map/ppermute | solution.py:213
  77.6 1.9 %collective-permute-start.10 = (f32[2,112,128]{2,1,0:T(8,128)S(1)}, f32[2,112,128]{2,1,0:T(8,128)S(1)}, u32[]{:S(2)}, u32[]{:S(2)}) collective-permute-start(f32[2,112,128]{2,1,0:T(8,128)S(1)} %pad_maximum_fusion.2), channel_id=1, source_target_pairs={{0,128},{64,192},{128,0},{192,64},{256,384},{320,448},{384,256},{4... | collective-permute-start | bytes 344072 | tf_op jit(solution)/shard_map/ppermute | solution.py:213
  79.5 5.7 %collective-permute-done.10 = f32[2,112,128]{2,1,0:T(8,128)S(1)} collective-permute-done((f32[2,112,128]{2,1,0:T(8,128)S(1)}, f32[2,112,128]{2,1,0:T(8,128)S(1)}, u32[]{:S(2)}, u32[]{:S(2)}) %collective-permute-start.10) | collective-permute-done | bytes 114720 | tf_op jit(solution)/shard_map/ppermute | solution.py:213
  86.0 1.9 %collective-permute-start.11 = (f32[2,224,128]{2,1,0:T(8,128)S(1)}, f32[2,224,128]{2,1,0:T(8,128)S(1)}, u32[]{:S(2)}, u32[]{:S(2)}) collective-permute-start(f32[2,224,128]{2,1,0:T(8,128)S(1)} %pad_maximum_fusion.near_ref), channel_id=1, source_target_pairs={{0,64},{64,0},{128,192},{192,128},{256,320},{320,256},{384,448},{4... | collective-permute-start | bytes 688136 | tf_op jit(solution)/shard_map/ppermute | solution.py:213
  88.0 6.0 %collective-permute-done.11.far_ref = f32[2,224,128]{2,1,0:T(8,128)S(1)} collective-permute-done((f32[2,224,128]{2,1,0:T(8,128)S(1)}, f32[2,224,128]{2,1,0:T(8,128)S(1)}, u32[]{:S(2)}, u32[]{:S(2)}) %collective-permute-start.11) | collective-permute-done | bytes 229408 | tf_op jit(solution)/shard_map/ppermute | solution.py:213
  94.4 1.4 %copy.10 = bf16[10,4,36,384]{3,1,2,0:T(4,128)(2,1)} copy(bf16[10,4,36,384]{3,2,1,0:T(8,128)(2,1)S(1)} %output.1) | data formatting | bytes 2211840 | tf_op jit(solution)/shard_map/output/pallas_call | solution.py:194
  (47 shorter events, 8.1 us)
Async XLA Ops:
  0.7 27.3 %collective-permute-start.4 = (f32[4,1,96]{2,1,0:T(1,128)S(1)}, f32[4,1,96]{2,1,0:T(1,128)S(1)}, u32[]{:S(2)}, u32[]{:S(2)}) collective-permute-start(f32[4,1,96]{2,1,0:T(1,128)S(1)} %get-tuple-element.26), channel_id=1, source_target_pairs={{0,1},{1,2},{2,3},{3,4},{4,5},{5,6},{6,7},{7,8},{8,9},{9,10},{10,1... | collective-permute-start | bytes 4616 | tf_op jit(solution)/shard_map/ppermute | solution.py:223
  2.7 25.4 %collective-permute-start.5 = (f32[4,1,96]{2,1,0:T(1,128)S(1)}, f32[4,1,96]{2,1,0:T(1,128)S(1)}, u32[]{:S(2)}, u32[]{:S(2)}) collective-permute-start(f32[4,1,96]{2,1,0:T(1,128)S(1)} %get-tuple-element.25), channel_id=1, source_target_pairs={{1,0},{2,1},{3,2},{4,3},{5,4},{6,5},{7,6},{8,7},{9,8},{10,9},{11,1... | collective-permute-start | bytes 4616 | tf_op jit(solution)/shard_map/ppermute | solution.py:224
  20.7 3.5 %copy-start.2 = (bf16[10,4,36,384]{3,1,2,0:T(4,128)(2,1)S(1)}, bf16[10,4,36,384]{3,1,2,0:T(4,128)(2,1)}, u32[]{:S(2)}) copy-start(bf16[10,4,36,384]{3,1,2,0:T(4,128)(2,1)} %param.9) | copy-start | bytes 3317764
  21.3 13.1 %collective-permute-start = (f32[2,224,128]{2,1,0:T(8,128)S(1)}, f32[2,224,128]{2,1,0:T(8,128)}, u32[]{:S(2)}, u32[]{:S(2)}) collective-permute-start(f32[2,224,128]{2,1,0:T(8,128)S(1)} %get-tuple-element.12), channel_id=1, source_target_pairs={{0,64},{64,0},{128,192},{192,128},{256,320},{320,256},{384,448},{4... | collective-permute-start | bytes 688136 | tf_op jit(solution)/shard_map/ppermute | solution.py:213
  24.2 3.8 %copy-start.1 = (f32[4,72,96]{2,1,0:T(8,128)S(1)}, f32[4,72,96]{2,1,0:T(8,128)}, u32[]{:S(2)}) copy-start(f32[4,72,96]{2,1,0:T(8,128)} %fine_ref.1) | copy-start | bytes 331780
  24.4 3.5 %copy-start.4 = (f32[4,36]{1,0:T(4,128)S(1)}, f32[4,36]{1,0:T(4,128)}, u32[]{:S(2)}) copy-start(f32[4,36]{1,0:T(4,128)} %param.6) | copy-start | bytes 1732
  24.4 3.6 %copy-start = (f32[768,384]{1,0:T(8,128)S(1)}, f32[768,384]{1,0:T(8,128)}, u32[]{:S(2)}) copy-start(f32[768,384]{1,0:T(8,128)} %weights_ref.1) | copy-start | bytes 3538948
  25.0 13.7 %collective-permute-start.3 = (f32[2,224,128]{2,1,0:T(8,128)S(1)}, f32[2,224,128]{2,1,0:T(8,128)}, u32[]{:S(2)}, u32[]{:S(2)}) collective-permute-start(f32[2,224,128]{2,1,0:T(8,128)S(1)} %get-tuple-element.14), channel_id=1, source_target_pairs={{0,64},{64,0},{128,192},{192,128},{256,320},{320,256},{384,448},{4... | collective-permute-start | bytes 688136 | tf_op jit(solution)/shard_map/ppermute | solution.py:213
  28.6 5.7 %collective-permute-start.6 = (f32[40,128]{1,0:T(8,128)S(1)}, f32[40,128]{1,0:T(8,128)S(1)}, u32[]{:S(2)}, u32[]{:S(2)}) collective-permute-start(f32[40,128]{1,0:T(8,128)S(1)} %get-tuple-element.16), channel_id=1, source_target_pairs={{0,64},{64,0},{128,192},{192,128},{256,320},{320,256},{384,448},{4... | collective-permute-start | bytes 61448 | tf_op jit(solution)/shard_map/ppermute | solution.py:213
  35.3 10.3 %collective-permute-start.1 = (f32[2,112,128]{2,1,0:T(8,128)S(1)}, f32[2,112,128]{2,1,0:T(8,128)S(1)}, u32[]{:S(2)}, u32[]{:S(2)}) collective-permute-start(f32[2,112,128]{2,1,0:T(8,128)S(1)} %pad_maximum_fusion.1), channel_id=1, source_target_pairs={{0,128},{64,192},{128,0},{192,64},{256,384},{320,448},{384,256},{4... | collective-permute-start | bytes 344072 | tf_op jit(solution)/shard_map/ppermute | solution.py:213
  39.8 9.6 %collective-permute-start.7 = (f32[264,128]{1,0:T(8,128)S(1)}, f32[264,128]{1,0:T(8,128)S(1)}, u32[]{:S(2)}, u32[]{:S(2)}) collective-permute-start(f32[264,128]{1,0:T(8,128)S(1)} %concatenate.16), channel_id=1, source_target_pairs={{0,128},{64,192},{128,0},{192,64},{256,384},{320,448},{384,256},{4... | collective-permute-start | bytes 405512 | tf_op jit(solution)/shard_map/ppermute | solution.py:213
  46.3 17.9 %collective-permute-start.2 = (f32[2,56,128]{2,1,0:T(8,128)S(1)}, f32[2,56,128]{2,1,0:T(8,128)S(1)}, u32[]{:S(2)}, u32[]{:S(2)}) collective-permute-start(f32[2,56,128]{2,1,0:T(8,128)S(1)} %get-tuple-element.35), channel_id=1, source_target_pairs={{0,256},{64,320},{128,384},{192,448},{256,0},{320,64},{384,128},{4... | collective-permute-start | bytes 172040 | tf_op jit(solution)/shard_map/ppermute | solution.py:213
  49.5 13.4 %collective-permute-start.8 = (f32[152,128]{1,0:T(8,128)S(1)}, f32[152,128]{1,0:T(8,128)S(1)}, u32[]{:S(2)}, u32[]{:S(2)}) collective-permute-start(f32[152,128]{1,0:T(8,128)S(1)} %concatenate.17), channel_id=1, source_target_pairs={{0,256},{64,320},{128,384},{192,448},{256,0},{320,64},{384,128},{4... | collective-permute-start | bytes 233480 | tf_op jit(solution)/shard_map/ppermute | solution.py:213
  64.2 0.6 copy-start.3
  66.5 10.3 %collective-permute-start.9 = (f32[2,56,128]{2,1,0:T(8,128)}, f32[2,56,128]{2,1,0:T(8,128)S(1)}, u32[]{:S(2)}, u32[]{:S(2)}) collective-permute-start(f32[2,56,128]{2,1,0:T(8,128)} %factor.1), channel_id=1, source_target_pairs={{0,256},{64,320},{128,384},{192,448},{256,0},{320,64},{384,128},{4... | collective-permute-start | bytes 172040 | tf_op jit(solution)/shard_map/ppermute | solution.py:213
  77.6 7.6 %collective-permute-start.10 = (f32[2,112,128]{2,1,0:T(8,128)S(1)}, f32[2,112,128]{2,1,0:T(8,128)S(1)}, u32[]{:S(2)}, u32[]{:S(2)}) collective-permute-start(f32[2,112,128]{2,1,0:T(8,128)S(1)} %pad_maximum_fusion.2), channel_id=1, source_target_pairs={{0,128},{64,192},{128,0},{192,64},{256,384},{320,448},{384,256},{4... | collective-permute-start | bytes 344072 | tf_op jit(solution)/shard_map/ppermute | solution.py:213
  86.0 7.9 %collective-permute-start.11 = (f32[2,224,128]{2,1,0:T(8,128)S(1)}, f32[2,224,128]{2,1,0:T(8,128)S(1)}, u32[]{:S(2)}, u32[]{:S(2)}) collective-permute-start(f32[2,224,128]{2,1,0:T(8,128)S(1)} %pad_maximum_fusion.near_ref), channel_id=1, source_target_pairs={{0,64},{64,0},{128,192},{192,128},{256,320},{320,256},{384,448},{4... | collective-permute-start | bytes 688136 | tf_op jit(solution)/shard_map/ppermute | solution.py:213

commit v2 on v0

v2 whole, which is shorter than its diff:
```python
import functools

import jax
import jax.numpy as jnp
from jax import lax
from jax.experimental import pallas as pl
from jax.experimental.layout import Layout, with_layout_constraint
from jax.experimental.pallas import tpu as pltpu
from jax.sharding import PartitionSpec as P

ROWS = 54
HALF = 2 * ROWS
STATS = 4 * ROWS
ORDER = (0, 4, 2, 6, 1, 5, 3, 7)
INC = 40
EDGE = 4
GATHER = HALF + EDGE
F32 = jnp.float32
HIGHEST = lax.Precision.HIGHEST
VMEM = pl.BlockSpec(memory_space=pltpu.VMEM)
SMEM = pl.BlockSpec(memory_space=pltpu.SMEM)


def call(kernel, name, ids, args, out, scratch=(), mib=4, flops=200_000, after=()):
    many = isinstance(out, tuple)
    moved = sum(a.size * a.dtype.itemsize for a in args) + sum(
        o.size * o.dtype.itemsize for o in (out if many else (out,))
    )
    count = len(args)

    def body(ids, *refs):
        kernel(ids, *refs[:count], *refs[count + len(after) :])

    return pl.pallas_call(
        body,
        out_shape=out,
        in_specs=[SMEM] + [VMEM] * count + [pl.BlockSpec(memory_space=pl.ANY)] * len(after),
        out_specs=(VMEM,) * len(out) if many else VMEM,
        scratch_shapes=list(scratch),
        compiler_params=pltpu.CompilerParams(vmem_limit_bytes=mib * 2**20),
        cost_estimate=pl.CostEstimate(flops=flops, bytes_accessed=moved, transcendentals=0),
        name=name,
    )(ids, *args, *after)


def rows_of(*counts):
    shapes = tuple(jax.ShapeDtypeStruct((count, 128), F32) for count in counts)
    return shapes if len(shapes) > 1 else shapes[0]


def stats_kernel(ids, prior, post, keep, send, full, block):
    step = 144
    for which, ref in enumerate((prior, post)):
        members = ref.shape[0]
        for at in range(0, 432, step):
            total = ref[0, at : at + step, :].astype(F32)
            for i in range(1, members):
                total = total + ref[i, at : at + step, :].astype(F32)
            mean = total / members
            square = jnp.zeros_like(total)
            for i in range(members):
                dev = ref[i, at : at + step, :].astype(F32) - mean
                square = square + dev * dev
            full[which, at : at + step, :] = total
            full[2 + which, at : at + step, :] = square
    for k in range(8):
        for j in range(4):
            at = k * STATS + j * ROWS
            block[at : at + ROWS, :] = full[j, pl.ds(4 * ROWS * (k >> 2) + (k & 3), ROWS, stride=4), :]
    for p in range(8):
        at = pl.multiple_of((ids[0] ^ ORDER[p]) * STATS, 8)
        out, to = (keep, p * STATS) if p < 4 else (send, (p - 4) * STATS)
        out[to : to + STATS, :] = block[pl.ds(at, STATS), :]


def local_weights(weights, device):
    own = weights[pl.ds(pl.multiple_of(device * 96, 32), 96), :]
    return pltpu.roll(own, lax.rem(385 - 48 * device, 384), 1)[:, :128]


def column(taps, t):
    size = taps.shape[1]
    diagonal = lax.broadcasted_iota(jnp.int32, (size, size), 0) == lax.broadcasted_iota(jnp.int32, (size, size), 1)
    return jnp.sum(jnp.where(diagonal, taps[t : t + 1, :], 0.0), axis=1, keepdims=True)


def fine_kernel(ids, fine, near, taps, weights, keep, send, rows, block):
    odd = ids[1] & 1
    local = local_weights(weights, ids[0])
    other = near[...]
    up = jnp.where(odd == 1, other, 0.0)
    down = jnp.where(odd == 1, 0.0, other)
    weight = [column(taps, t) for t in range(4)]
    for level in range(4):
        rows[8:80, :] = fine[level]
        rows[7:8, :] = up[level : level + 1]
        rows[80:81, :] = down[level : level + 1]
        total = weight[0] * rows[pl.ds(7, 36, stride=2), :]
        for t in range(1, 4):
            total = total + weight[t] * rows[pl.ds(7 + t, 36, stride=2), :]
        part = jnp.dot(total, local, precision=HIGHEST, preferred_element_type=F32)
        for e in range(2):
            at, row = 16 * (level + 4 * e), 18 * e
            block[at : at + 8, :] = part[row : row + 8] + pltpu.roll(part[row + 8 : row + 16], 64, 1)
            block[at + 8 : at + 9, :] = part[row + 16 : row + 17] + pltpu.roll(part[row + 17 : row + 18], 64, 1)
    for p in range(8):
        at = pl.multiple_of((ids[0] ^ ORDER[p]) * 16, 8)
        out, q = (keep, p) if p < 4 else (send, p - 4)
        out[8 * q : 8 * q + 8, :] = block[pl.ds(at, 8), :]
        out[32 + q : 33 + q, :] = block[pl.ds(at + 8, 8), :][0:1]
    for out in (keep, send):
        out[36:40, :] = jnp.zeros((4, 128), F32)


def merged(a, at, b, bt, count):
    one, two = a[at : at + HALF, :], b[bt : bt + HALF, :]
    diff = one - two
    squares = a[at + HALF : at + STATS, :] + b[bt + HALF : bt + STATS, :]
    return one + two, squares + diff * diff * (0.5 / count)


def merge_kernel(count, ids, keep, recv, *refs):
    *inc, keep_out, send_out = refs
    chunks = keep_out.shape[0] // STATS
    for p in range(2 * chunks):
        out, to = (keep_out, p * STATS) if p < chunks else (send_out, (p - chunks) * STATS)
        total, square = merged(keep, p * STATS, recv, p * STATS, count)
        out[to : to + HALF, :] = total
        out[to + HALF : to + STATS, :] = square
    old = 2 * chunks * STATS
    pairs = [(inc[0], 0), (inc[1], 0)] if inc else [(keep, old), (recv, old)]
    each = 4 // chunks // 2
    for half, out in enumerate((keep_out, send_out)):
        to = chunks * STATS
        for i, (ref, at) in enumerate(pairs):
            for s in range(each):
                for q in range(chunks):
                    new = (i * each + s) * chunks + q
                    old_place = s * 2 * chunks + half * chunks + q
                    out[to + 8 * new : to + 8 * new + 8, :] = ref[at + 8 * old_place : at + 8 * old_place + 8, :]
                    out[to + 32 + new : to + 33 + new, :] = ref[at + 32 + old_place : at + 33 + old_place, :]
        out[to + 36 : to + 40, :] = jnp.zeros((4, 128), F32)


def placed(ref, device):
    lane = lax.broadcasted_iota(jnp.int32, (18, 128), 1)
    wide = jnp.zeros((18, 384), F32)
    for s in range(4):
        most = ref[STATS + 8 * s : STATS + 8 * s + 8, :]
        rest = ref[STATS + 32 + s : STATS + 33 + s, :]
        share = jnp.concatenate([most, pltpu.roll(most, 64, 1), rest, pltpu.roll(rest, 64, 1)], axis=0)
        share = jnp.where(lane < 50, share, 0.0)
        share = jnp.concatenate([share, jnp.zeros((18, 256), F32)], axis=1)
        wide = wide + pltpu.roll(share, lax.rem(48 * (device ^ s) + 383, 384), 1)
    return wide


def own_kernel(ids, mine, out):
    out[...] = placed(mine, ids[0])


def edge_kernel(ids, late, taps, weights, out):
    tap = jnp.where(ids[1] & 1 == 1, taps[3:4, 35:36], taps[0:1, 0:1])
    out[...] = jnp.dot(
        late[...] * tap, local_weights(weights, ids[0] ^ ids[2]), precision=HIGHEST, preferred_element_type=F32
    )


def factor_kernel(count, ids, mine, recv, own, edge, out, scratch):
    total, square = merged(mine, 0, recv, 0, count // 2)
    mean = total / count
    spread = jnp.sqrt(square / (count - 1) + 1e-06)
    prior_spread, post_spread = spread[0:ROWS], spread[ROWS:HALF]
    factor = 1.0 + 0.9 * (prior_spread - post_spread) / post_spread
    wide = own[...] + placed(recv, ids[0] ^ 4)
    for ct in range(3):
        scratch[pl.ds(ct, 18, stride=3), :] = wide[:, 128 * ct : 128 * ct + 128]
    out[0:ROWS, :] = factor
    out[ROWS:HALF, :] = mean[0:ROWS] - factor * mean[ROWS:HALF] + scratch[...]
    out[HALF:GATHER, :] = edge[...]


def join_kernel(ids, a, b, out):
    size = a.shape[0]
    out[0:size, :] = a[...]
    out[size : 2 * size, :] = b[...]


def output_kernel(ids, near, far, post, out, block, factor, base):
    lane = lax.broadcasted_iota(jnp.int32, (EDGE, 128), 1)
    edge = jnp.zeros((EDGE, 384), F32)
    for p in range(8):
        ref, at = (near, p * GATHER) if p < 4 else (far, (p - 4) * GATHER)
        chunk = ids[0] ^ ORDER[p]
        block[pl.ds(pl.multiple_of(chunk * GATHER, 8), GATHER), :] = ref[at : at + GATHER, :]
        share = jnp.where(lane < 50, ref[at + HALF : at + GATHER, :], 0.0)
        share = jnp.concatenate([share, jnp.zeros((EDGE, 256), F32)], axis=1)
        edge = edge + pltpu.roll(share, lax.rem(48 * (chunk ^ ids[2]) + 383, 384), 1)
    for k in range(8):
        at = k * GATHER
        to = pl.ds(4 * ROWS * (k >> 2) + (k & 3), ROWS, stride=4)
        factor[to, :] = block[at : at + ROWS, :]
        base[to, :] = block[at + ROWS : at + HALF, :]
    odd = ids[1] & 1
    for ct in range(3):
        share = edge[:, 128 * ct : 128 * ct + 128]
        for at, part in ((0, jnp.where(odd == 1, 0.0, share)), (420, jnp.where(odd == 1, share, 0.0))):
            at = at + 4 * ct
            base[at : at + 4, :] = base[at : at + 4, :] + part
    step = 144
    for at in range(0, 432, step):
        scale = factor[at : at + step, :]
        shift = base[at : at + step, :]
        for i in range(post.shape[0]):
            out[i, at : at + step, :] = (shift + scale * post[i, at : at + step, :].astype(F32)).astype(jnp.bfloat16)


def viewed(x):
    members = x.shape[0]
    x = with_layout_constraint(x.reshape(members, 4, 36, 3, 128), Layout(major_to_minor=(0, 2, 3, 1, 4)))
    return x.transpose(0, 2, 3, 1, 4).reshape(members, 432, 128)


def on_device(fine_increment, row_taps, col_weights, prior, posterior):
    mem, hor = lax.axis_size("mem"), lax.axis_size("hor")
    share = prior.shape[0]
    count = share * mem
    m, h = lax.axis_index("mem"), lax.axis_index("hor")
    middle = hor // 2
    apart = jnp.where((h == middle - 1) | (h == middle), 4, 0)
    ids = jnp.stack([m, h, apart]).astype(jnp.int32)

    def swap(x, distance):
        return lax.ppermute(x, "mem", [(i, i ^ distance) for i in range(mem)])

    def swap_rows(x, first, far=None):
        pairs = [(i, i + 1) for i in range(first, hor - 1, 2)]
        pairs = pairs + [(j, i) for i, j in pairs]
        return lax.ppermute(
            x,
            ("mem", "hor"),
            [
                (i * hor + a, (i ^ (4 if a + b == 2 * middle - 1 and far else 0)) * hor + b)
                for i in range(mem)
                for a, b in pairs
            ],
        )

    prior, posterior = viewed(prior), viewed(posterior)
    last, first = fine_increment[:, -1, :], fine_increment[:, 0, :]
    odd = h % 2 == 1

    keep, send = call(
        stats_kernel,
        "stats",
        ids,
        (prior, posterior),
        rows_of(4 * STATS, 4 * STATS),
        [pltpu.VMEM((4, 432, 128), F32), pltpu.VMEM((8 * STATS, 128), F32)],
        mib=10,
        flops=8_000_000,
    )
    recv = swap(send, 1)
    now = swap_rows(jnp.where(odd, first, last), 0)
    inc_keep, inc_send = call(
        fine_kernel,
        "fine",
        ids,
        (fine_increment, now, row_taps, col_weights),
        rows_of(INC, INC),
        [pltpu.VMEM((88, 96), F32), pltpu.VMEM((128, 128), F32)],
        flops=4_000_000,
    )
    inc_recv = swap(inc_send, 1)
    keep, send = call(
        functools.partial(merge_kernel, share),
        "merge1",
        ids,
        (keep, recv, inc_keep, inc_recv),
        rows_of(2 * STATS + INC, 2 * STATS + INC),
    )
    recv = swap(send, 2)
    late, _ = lax.optimization_barrier((jnp.where(odd, last, first), keep))
    late = swap_rows(late, 1, True)
    edge = call(
        edge_kernel, "edge", ids, (late, row_taps, col_weights), rows_of(EDGE)
    )
    keep, send = call(
        functools.partial(merge_kernel, 2 * share), "merge2", ids, (keep, recv), rows_of(STATS + INC, STATS + INC)
    )
    recv = swap(send, 4)
    own = call(own_kernel, "own", ids, (keep,), jax.ShapeDtypeStruct((18, 384), F32))
    near = call(
        functools.partial(factor_kernel, count),
        "factor",
        ids,
        (keep, recv, own, edge),
        rows_of(GATHER),
        [pltpu.VMEM((ROWS, 128), F32)],
    )
    for distance in (4, 2):
        near = call(join_kernel, "join", ids, (near, swap(near, distance)), rows_of(2 * near.shape[0]))
    far = swap(near, 1)
    out = call(
        output_kernel,
        "output",
        ids,
        (near, far, posterior),
        jax.ShapeDtypeStruct(posterior.shape, jnp.bfloat16),
        [pltpu.VMEM((8 * GATHER, 128), F32)] + [pltpu.VMEM((432, 128), F32)] * 2,
        mib=10,
        flops=2_000_000,
    )
    out = out.reshape(share, 36, 3, 4, 128).transpose(0, 1, 3, 2, 4)
    return out.reshape(share, 36, 4, 384).transpose(0, 2, 1, 3)


def solution(mesh):
    return jax.shard_map(
        on_device,
        mesh=mesh,
        in_specs=(
            P(None, "hor", "mem"),
            P(None, "hor"),
            P(),
            P("mem", None, "hor", None),
            P("mem", None, "hor", None),
        ),
        out_specs=P("mem", None, "hor", None),
        check_vma=False,
    )
```

time: 274 us -> 87 us (0.32)
  the two profiles are of different devices: /device:TPU:2 before, /device:TPU:6 now
where the time goes in v2:
time: 87 us; the launch traced here: 86.6 us
  waiting for transfers between devices  43.2 us (50%)
  starting transfers between devices  31.4 us (36%)
  Pallas kernels  9.21 us (11%)
  local copies, waits for them, and re-layouts  2.51 us (3%)
    ppermute x7, waiting for transfers between devices, swap(): return lax.ppermute(x, 'mem', [(i, i ^ distance) for i in range(mem)])  38.6 us
    ppermute x7, starting transfers between devices, swap(): return lax.ppermute(x, 'mem', [(i, i ^ distance) for i in range(mem)])  25.9 us
    pallas_call x10, Pallas kernels, call(): pl.pallas_call(body, out_shape=out, in_specs=[SMEM] + [VMEM] * count + [p...  9.21 us
    ppermute x2, starting transfers between devices, swap_rows(): lax.ppermute(x, ('mem', 'hor'), [(i * hor + a, (i ^ (4 if a + b == 2 * mi...  5.55 us
    ppermute x2, waiting for transfers between devices, swap_rows(): lax.ppermute(x, ('mem', 'hor'), [(i * hor + a, (i ^ (4 if a + b == 2 * mi...  4.63 us
    unnamed x12, local copies, waits for them, and re-layouts  2.51 us
  transfers between devices with their start and end apart: 9, of which 8 were waited for; matrix products, arithmetic and copies ran while one was open for 0% of the time, Pallas kernels for 3%

profile of v2, /device:TPU:6, one launch (start us, length us, event | category | flops | bytes accessed | tf_op | source)
XLA Modules:
  0.0 86.6 jit_solution(2386747296665948209)
XLA Ops:
  0.1 1.2 %copy-done.1 = bf16[10,4,36,384]{3,1,2,0:T(4,128)(2,1)S(1)} copy-done((bf16[10,4,36,384]{3,1,2,0:T(4,128)(2,1)S(1)}, bf16[10,4,36,384]{3,1,2,0:T(4,128)(2,1)}, u32[]{:S(2)}) %copy-start.1) | copy-done | bytes 1105944
  1.3 1.2 %copy-done.3 = bf16[10,4,36,384]{3,1,2,0:T(4,128)(2,1)S(1)} copy-done((bf16[10,4,36,384]{3,1,2,0:T(4,128)(2,1)S(1)}, bf16[10,4,36,384]{3,1,2,0:T(4,128)(2,1)}, u32[]{:S(2)}) %copy-start.3) | copy-done | bytes 1105944
  2.6 1.6 %stats.1 = (f32[864,128]{1,0:T(8,128)S(1)}, f32[864,128]{1,0:T(8,128)S(1)}) custom-call(s32[3]{0:T(128)S(1)} %pad_add_fusion.ids, bf16[10,432,128]{2,1,0:T(8,128)(2,1)S(1)} %bitcast.28, bf16[10,432,128]{2,1,0:T(8,128)(2,1)S(1)} %bitcast.26), custom_call_target="tpu_custom_call" | custom-call | flops 8000000 | bytes 3096576 | tf_op jit(solution)/shard_map/stats/pallas_call | solution.py:34
  4.2 3.8 %collective-permute-start = (f32[864,128]{1,0:T(8,128)S(1)}, f32[864,128]{1,0:T(8,128)S(1)}, u32[]{:S(2)}, u32[]{:S(2)}) collective-permute-start(f32[864,128]{1,0:T(8,128)S(1)} %get-tuple-element.15), channel_id=1, source_target_pairs={{0,64},{64,0},{128,192},{192,128},{256,320},{320,256},{384,448},{4... | collective-permute-start | bytes 1327112 | tf_op jit(solution)/shard_map/ppermute | solution.py:234
  8.1 1.9 %collective-permute-start.1 = (f32[4,96]{1,0:T(4,128)S(1)}, f32[4,96]{1,0:T(4,128)S(1)}, u32[]{:S(2)}, u32[]{:S(2)}) collective-permute-start(f32[4,96]{1,0:T(4,128)S(1)} %get-tuple-element.26), channel_id=1, source_target_pairs={{0,1},{2,3},{4,5},{6,7},{8,9},{10,11},{12,13},{14,15},{16,17},{18,... | collective-permute-start | bytes 4616 | tf_op jit(solution)/shard_map/ppermute | solution.py:239
  10.0 1.1 %collective-permute-done.1.refs_1_ = f32[4,96]{1,0:T(4,128)S(1)} collective-permute-done((f32[4,96]{1,0:T(4,128)S(1)}, f32[4,96]{1,0:T(4,128)S(1)}, u32[]{:S(2)}, u32[]{:S(2)}) %collective-permute-start.1) | collective-permute-done | bytes 1568 | tf_op jit(solution)/shard_map/ppermute | solution.py:239
  11.1 1.1 %fine.1 = (f32[40,128]{1,0:T(8,128)S(1)}, f32[40,128]{1,0:T(8,128)S(1)}) custom-call(s32[3]{0:T(128)S(1)} %pad_add_fusion.ids, f32[4,72,96]{2,1,0:T(8,128)S(1)} %copy-done.4, f32[4,96]{1,0:T(4,128)S(1)} %collective-permute-done.1.refs_1_, f32[4,36]{1,0:T(4,128)S(1)} %copy-done.5, f32[768,384]{1,0:T(8,128)S(1)} %copy-done), custom_call_target="tpu_custom_call" | custom-call | flops 4000000 | bytes 1333312 | tf_op jit(solution)/shard_map/fine/pallas_call | solution.py:34
  12.3 2.0 %collective-permute-start.2 = (f32[40,128]{1,0:T(8,128)S(1)}, f32[40,128]{1,0:T(8,128)S(1)}, u32[]{:S(2)}, u32[]{:S(2)}) collective-permute-start(f32[40,128]{1,0:T(8,128)S(1)} %get-tuple-element.17), channel_id=1, source_target_pairs={{0,64},{64,0},{128,192},{192,128},{256,320},{320,256},{384,448},{4... | collective-permute-start | bytes 61448 | tf_op jit(solution)/shard_map/ppermute | solution.py:234
  14.3 4.3 %collective-permute-done.2.refs_3_ = f32[40,128]{1,0:T(8,128)S(1)} collective-permute-done((f32[40,128]{1,0:T(8,128)S(1)}, f32[40,128]{1,0:T(8,128)S(1)}, u32[]{:S(2)}, u32[]{:S(2)}) %collective-permute-start.2) | collective-permute-done | bytes 20512 | tf_op jit(solution)/shard_map/ppermute | solution.py:234
  19.2 5.2 %collective-permute-start.3 = (f32[472,128]{1,0:T(8,128)S(1)}, f32[472,128]{1,0:T(8,128)S(1)}, u32[]{:S(2)}, u32[]{:S(2)}) collective-permute-start(f32[472,128]{1,0:T(8,128)S(1)} %get-tuple-element.19), channel_id=1, source_target_pairs={{0,128},{64,192},{128,0},{192,64},{256,384},{320,448},{384,256},{4... | collective-permute-start | bytes 725000 | tf_op jit(solution)/shard_map/ppermute | solution.py:234
  24.4 10.4 %collective-permute-done.3.refs_1_ = f32[472,128]{1,0:T(8,128)S(1)} collective-permute-done((f32[472,128]{1,0:T(8,128)S(1)}, f32[472,128]{1,0:T(8,128)S(1)}, u32[]{:S(2)}, u32[]{:S(2)}) %collective-permute-start.3) | collective-permute-done | bytes 241696 | tf_op jit(solution)/shard_map/ppermute | solution.py:234
  35.4 9.1 %collective-permute-start.4 = (f32[256,128]{1,0:T(8,128)S(1)}, f32[256,128]{1,0:T(8,128)S(1)}, u32[]{:S(2)}, u32[]{:S(2)}) collective-permute-start(f32[256,128]{1,0:T(8,128)S(1)} %get-tuple-element.21), channel_id=1, source_target_pairs={{0,256},{64,320},{128,384},{192,448},{256,0},{320,64},{384,128},{4... | collective-permute-start | bytes 393224 | tf_op jit(solution)/shard_map/ppermute | solution.py:234
  44.5 3.6 %collective-permute-start.5 = (f32[4,96]{1,0:T(4,128)S(1)}, f32[4,96]{1,0:T(4,128)S(1)}, u32[]{:S(2)}, u32[]{:S(2)}) collective-permute-start(f32[4,96]{1,0:T(4,128)S(1)} %get-tuple-element.22), channel_id=1, source_target_pairs={{1,2},{3,4},{5,6},{7,8},{9,10},{11,12},{13,14},{15,16},{17,18},{19... | collective-permute-start | bytes 4616 | tf_op jit(solution)/shard_map/ppermute | solution.py:239
  48.1 3.5 %collective-permute-done.5.refs_0_ = f32[4,96]{1,0:T(4,128)S(1)} collective-permute-done((f32[4,96]{1,0:T(4,128)S(1)}, f32[4,96]{1,0:T(4,128)S(1)}, u32[]{:S(2)}, u32[]{:S(2)}) %collective-permute-start.5) | collective-permute-done | bytes 1568 | tf_op jit(solution)/shard_map/ppermute | solution.py:239
  51.6 0.8 edge.1.refs_3_
  53.2 1.3 %collective-permute-done.4.refs_1_ = f32[256,128]{1,0:T(8,128)S(1)} collective-permute-done((f32[256,128]{1,0:T(8,128)S(1)}, f32[256,128]{1,0:T(8,128)S(1)}, u32[]{:S(2)}, u32[]{:S(2)}) %collective-permute-start.4) | collective-permute-done | bytes 131104 | tf_op jit(solution)/shard_map/ppermute | solution.py:234
  54.5 0.7 factor.1.refs_0_
  55.2 1.9 %collective-permute-start.6 = (f32[112,128]{1,0:T(8,128)S(1)}, f32[112,128]{1,0:T(8,128)S(1)}, u32[]{:S(2)}, u32[]{:S(2)}) collective-permute-start(f32[112,128]{1,0:T(8,128)S(1)} %factor.1.refs_0_), channel_id=1, source_target_pairs={{0,256},{64,320},{128,384},{192,448},{256,0},{320,64},{384,128},{4... | collective-permute-start | bytes 172040 | tf_op jit(solution)/shard_map/ppermute | solution.py:234
  57.1 8.1 %collective-permute-done.6.refs_1_ = f32[112,128]{1,0:T(8,128)S(1)} collective-permute-done((f32[112,128]{1,0:T(8,128)S(1)}, f32[112,128]{1,0:T(8,128)S(1)}, u32[]{:S(2)}, u32[]{:S(2)}) %collective-permute-start.6) | collective-permute-done | bytes 57376 | tf_op jit(solution)/shard_map/ppermute | solution.py:234
  65.8 1.9 %collective-permute-start.7 = (f32[224,128]{1,0:T(8,128)S(1)}, f32[224,128]{1,0:T(8,128)S(1)}, u32[]{:S(2)}, u32[]{:S(2)}) collective-permute-start(f32[224,128]{1,0:T(8,128)S(1)} %join.2.refs_0_), channel_id=1, source_target_pairs={{0,128},{64,192},{128,0},{192,64},{256,384},{320,448},{384,256},{4... | collective-permute-start | bytes 344072 | tf_op jit(solution)/shard_map/ppermute | solution.py:234
  67.7 7.2 %collective-permute-done.7.refs_1_ = f32[224,128]{1,0:T(8,128)S(1)} collective-permute-done((f32[224,128]{1,0:T(8,128)S(1)}, f32[224,128]{1,0:T(8,128)S(1)}, u32[]{:S(2)}, u32[]{:S(2)}) %collective-permute-start.7) | collective-permute-done | bytes 114720 | tf_op jit(solution)/shard_map/ppermute | solution.py:234
  75.5 1.9 %collective-permute-start.8 = (f32[448,128]{1,0:T(8,128)S(1)}, f32[448,128]{1,0:T(8,128)S(1)}, u32[]{:S(2)}, u32[]{:S(2)}) collective-permute-start(f32[448,128]{1,0:T(8,128)S(1)} %join.3.refs_0_), channel_id=1, source_target_pairs={{0,64},{64,0},{128,192},{192,128},{256,320},{320,256},{384,448},{4... | collective-permute-start | bytes 688136 | tf_op jit(solution)/shard_map/ppermute | solution.py:234
  77.4 7.3 %collective-permute-done.8.refs_1_ = f32[448,128]{1,0:T(8,128)S(1)} collective-permute-done((f32[448,128]{1,0:T(8,128)S(1)}, f32[448,128]{1,0:T(8,128)S(1)}, u32[]{:S(2)}, u32[]{:S(2)}) %collective-permute-start.8) | collective-permute-done | bytes 229408 | tf_op jit(solution)/shard_map/ppermute | solution.py:234
  84.7 1.9 %output.1 = bf16[10,432,128]{2,1,0:T(8,128)(2,1)} custom-call(s32[3]{0:T(128)S(1)} %pad_add_fusion.ids, f32[448,128]{1,0:T(8,128)S(1)} %join.3.refs_0_, f32[448,128]{1,0:T(8,128)S(1)} %collective-permute-done.8.refs_1_, bf16[10,432,128]{2,1,0:T(8,128)(2,1)S(1)} %bitcast.27), custom_call_target="tpu_custom_call" | custom-call | flops 2000000 | bytes 2670592 | tf_op jit(solution)/shard_map/output/pallas_call | solution.py:34
  (19 shorter events, 3.1 us)
Async XLA Ops:
  0.1 1.2 %copy-start.1 = (bf16[10,4,36,384]{3,1,2,0:T(4,128)(2,1)S(1)}, bf16[10,4,36,384]{3,1,2,0:T(4,128)(2,1)}, u32[]{:S(2)}) copy-start(bf16[10,4,36,384]{3,1,2,0:T(4,128)(2,1)} %param.9) | copy-start | bytes 3317764
  1.3 1.2 %copy-start.3 = (bf16[10,4,36,384]{3,1,2,0:T(4,128)(2,1)S(1)}, bf16[10,4,36,384]{3,1,2,0:T(4,128)(2,1)}, u32[]{:S(2)}) copy-start(bf16[10,4,36,384]{3,1,2,0:T(4,128)(2,1)} %param.8) | copy-start | bytes 3317764
  2.6 5.5 %copy-start.4 = (f32[4,72,96]{2,1,0:T(8,128)S(1)}, f32[4,72,96]{2,1,0:T(8,128)}, u32[]{:S(2)}) copy-start(f32[4,72,96]{2,1,0:T(8,128)} %refs_0_.1) | copy-start | bytes 331780
  2.6 8.6 %copy-start = (f32[768,384]{1,0:T(8,128)S(1)}, f32[768,384]{1,0:T(8,128)}, u32[]{:S(2)}) copy-start(f32[768,384]{1,0:T(8,128)} %refs_2_.3) | copy-start | bytes 3538948
  2.6 8.6 %copy-start.5 = (f32[4,36]{1,0:T(4,128)S(1)}, f32[4,36]{1,0:T(4,128)}, u32[]{:S(2)}) copy-start(f32[4,36]{1,0:T(4,128)} %refs_1_.1) | copy-start | bytes 1732
  4.2 14.4 %collective-permute-start = (f32[864,128]{1,0:T(8,128)S(1)}, f32[864,128]{1,0:T(8,128)S(1)}, u32[]{:S(2)}, u32[]{:S(2)}) collective-permute-start(f32[864,128]{1,0:T(8,128)S(1)} %get-tuple-element.15), channel_id=1, source_target_pairs={{0,64},{64,0},{128,192},{192,128},{256,320},{320,256},{384,448},{4... | collective-permute-start | bytes 1327112 | tf_op jit(solution)/shard_map/ppermute | solution.py:234
  8.1 3.1 %collective-permute-start.1 = (f32[4,96]{1,0:T(4,128)S(1)}, f32[4,96]{1,0:T(4,128)S(1)}, u32[]{:S(2)}, u32[]{:S(2)}) collective-permute-start(f32[4,96]{1,0:T(4,128)S(1)} %get-tuple-element.26), channel_id=1, source_target_pairs={{0,1},{2,3},{4,5},{6,7},{8,9},{10,11},{12,13},{14,15},{16,17},{18,... | collective-permute-start | bytes 4616 | tf_op jit(solution)/shard_map/ppermute | solution.py:239
  12.3 6.3 %collective-permute-start.2 = (f32[40,128]{1,0:T(8,128)S(1)}, f32[40,128]{1,0:T(8,128)S(1)}, u32[]{:S(2)}, u32[]{:S(2)}) collective-permute-start(f32[40,128]{1,0:T(8,128)S(1)} %get-tuple-element.17), channel_id=1, source_target_pairs={{0,64},{64,0},{128,192},{192,128},{256,320},{320,256},{384,448},{4... | collective-permute-start | bytes 61448 | tf_op jit(solution)/shard_map/ppermute | solution.py:234
  19.2 15.6 %collective-permute-start.3 = (f32[472,128]{1,0:T(8,128)S(1)}, f32[472,128]{1,0:T(8,128)S(1)}, u32[]{:S(2)}, u32[]{:S(2)}) collective-permute-start(f32[472,128]{1,0:T(8,128)S(1)} %get-tuple-element.19), channel_id=1, source_target_pairs={{0,128},{64,192},{128,0},{192,64},{256,384},{320,448},{384,256},{4... | collective-permute-start | bytes 725000 | tf_op jit(solution)/shard_map/ppermute | solution.py:234
  35.4 19.1 %collective-permute-start.4 = (f32[256,128]{1,0:T(8,128)S(1)}, f32[256,128]{1,0:T(8,128)S(1)}, u32[]{:S(2)}, u32[]{:S(2)}) collective-permute-start(f32[256,128]{1,0:T(8,128)S(1)} %get-tuple-element.21), channel_id=1, source_target_pairs={{0,256},{64,320},{128,384},{192,448},{256,0},{320,64},{384,128},{4... | collective-permute-start | bytes 393224 | tf_op jit(solution)/shard_map/ppermute | solution.py:234
  44.5 40.2 %copy-start.2 = (bf16[10,4,36,384]{3,1,2,0:T(4,128)(2,1)S(1)}, bf16[10,4,36,384]{3,1,2,0:T(4,128)(2,1)}, u32[]{:S(2)}) copy-start(bf16[10,4,36,384]{3,1,2,0:T(4,128)(2,1)} %param.9) | copy-start | bytes 3317764
  44.5 7.1 %collective-permute-start.5 = (f32[4,96]{1,0:T(4,128)S(1)}, f32[4,96]{1,0:T(4,128)S(1)}, u32[]{:S(2)}, u32[]{:S(2)}) collective-permute-start(f32[4,96]{1,0:T(4,128)S(1)} %get-tuple-element.22), channel_id=1, source_target_pairs={{1,2},{3,4},{5,6},{7,8},{9,10},{11,12},{13,14},{15,16},{17,18},{19... | collective-permute-start | bytes 4616 | tf_op jit(solution)/shard_map/ppermute | solution.py:239
  55.2 10.0 %collective-permute-start.6 = (f32[112,128]{1,0:T(8,128)S(1)}, f32[112,128]{1,0:T(8,128)S(1)}, u32[]{:S(2)}, u32[]{:S(2)}) collective-permute-start(f32[112,128]{1,0:T(8,128)S(1)} %factor.1.refs_0_), channel_id=1, source_target_pairs={{0,256},{64,320},{128,384},{192,448},{256,0},{320,64},{384,128},{4... | collective-permute-start | bytes 172040 | tf_op jit(solution)/shard_map/ppermute | solution.py:234
  65.8 9.1 %collective-permute-start.7 = (f32[224,128]{1,0:T(8,128)S(1)}, f32[224,128]{1,0:T(8,128)S(1)}, u32[]{:S(2)}, u32[]{:S(2)}) collective-permute-start(f32[224,128]{1,0:T(8,128)S(1)} %join.2.refs_0_), channel_id=1, source_target_pairs={{0,128},{64,192},{128,0},{192,64},{256,384},{320,448},{384,256},{4... | collective-permute-start | bytes 344072 | tf_op jit(solution)/shard_map/ppermute | solution.py:234
  75.5 9.2 %collective-permute-start.8 = (f32[448,128]{1,0:T(8,128)S(1)}, f32[448,128]{1,0:T(8,128)S(1)}, u32[]{:S(2)}, u32[]{:S(2)}) collective-permute-start(f32[448,128]{1,0:T(8,128)S(1)} %join.3.refs_0_), channel_id=1, source_target_pairs={{0,64},{64,0},{128,192},{192,128},{256,320},{320,256},{384,448},{4... | collective-permute-start | bytes 688136 | tf_op jit(solution)/shard_map/ppermute | solution.py:234

commit v3 on v2

v3 whole, which is shorter than its diff:
```python
import functools

import jax
import jax.numpy as jnp
from jax import lax
from jax.experimental import pallas as pl
from jax.experimental.layout import Layout, with_layout_constraint
from jax.experimental.pallas import tpu as pltpu
from jax.sharding import PartitionSpec as P

ROWS = 54
HALF = 2 * ROWS
STATS = 4 * ROWS
SENT = 2 * STATS + 24
KEPT = STATS + 40
EDGE = 4
GATHER = HALF + EDGE
F32 = jnp.float32
HIGHEST = lax.Precision.HIGHEST
VMEM = pl.BlockSpec(memory_space=pltpu.VMEM)
SMEM = pl.BlockSpec(memory_space=pltpu.SMEM)


def call(kernel, name, ids, args, out, scratch=(), mib=4, flops=200_000, specs=None):
    many = isinstance(out, tuple)
    moved = sum(a.size * a.dtype.itemsize for a in args) + sum(
        o.size * o.dtype.itemsize for o in (out if many else (out,))
    )
    return pl.pallas_call(
        kernel,
        out_shape=out,
        in_specs=[SMEM] + (specs or [VMEM] * len(args)),
        out_specs=(VMEM,) * len(out) if many else VMEM,
        scratch_shapes=list(scratch),
        compiler_params=pltpu.CompilerParams(vmem_limit_bytes=mib * 2**20),
        cost_estimate=pl.CostEstimate(flops=flops, bytes_accessed=moved, transcendentals=0),
        name=name,
    )(ids, *args)


def rows_of(*counts):
    shapes = tuple(jax.ShapeDtypeStruct((count, 128), F32) for count in counts)
    return shapes if len(shapes) > 1 else shapes[0]


def local_weights(own, device):
    return pltpu.roll(own, lax.rem(385 - 48 * device, 384), 1)[:, :128]


def column(taps, t):
    size = taps.shape[1]
    diagonal = lax.broadcasted_iota(jnp.int32, (size, size), 0) == lax.broadcasted_iota(jnp.int32, (size, size), 1)
    return jnp.sum(jnp.where(diagonal, taps[t : t + 1, :], 0.0), axis=1, keepdims=True)


def first_kernel(ids, prior, post, fine, taps, weights, *refs):
    outs, (members, rows, tap, weight, sems, full, block) = refs[:4], refs[4:]
    m = ids[0]
    copies = [
        pltpu.make_async_copy(src, dst, sems.at[i])
        for i, (src, dst) in enumerate(
            (
                (fine, rows.at[:, pl.ds(8, 72), :]),
                (weights.at[pl.ds(pl.multiple_of(96 * m, 32), 96), :], weight),
                (taps, tap),
                (prior, members.at[0]),
                (post, members.at[1]),
            )
        )
    ]
    for copy in copies:
        copy.start()
    for copy in copies[:3]:
        copy.wait()
    local = local_weights(weight[...], m)
    columns = [column(tap, t) for t in range(4)]
    for level in range(4):
        rows[level, 0:8, :] = jnp.zeros((8, 96), F32)
        rows[level, 80:88, :] = jnp.zeros((8, 96), F32)
        total = columns[0] * rows[level, pl.ds(7, 36, stride=2), :]
        for t in range(1, 4):
            total = total + columns[t] * rows[level, pl.ds(7 + t, 36, stride=2), :]
        part = jnp.dot(total, local, precision=HIGHEST, preferred_element_type=F32)
        for e in range(2):
            at, row = (level + 4 * e) * SENT // 2 + STATS, 18 * e
            block[at : at + 8, :] = part[row : row + 8] + pltpu.roll(part[row + 8 : row + 16], 64, 1)
            block[at + 8 : at + 9, :] = part[row + 16 : row + 17] + pltpu.roll(part[row + 17 : row + 18], 64, 1)
    step = 144
    for which in range(2):
        copies[3 + which].wait()
        count = members.shape[1]
        for at in range(0, 432, step):
            total = members[which, 0, at : at + step, :].astype(F32)
            for i in range(1, count):
                total = total + members[which, i, at : at + step, :].astype(F32)
            mean = total / count
            square = jnp.zeros_like(total)
            for i in range(count):
                dev = members[which, i, at : at + step, :].astype(F32) - mean
                square = square + dev * dev
            full[which, at : at + step, :] = total
            full[2 + which, at : at + step, :] = square
    for k in range(8):
        for j in range(4):
            at = k * SENT // 2 + j * ROWS
            block[at : at + ROWS, :] = full[j, pl.ds(4 * ROWS * (k >> 2) + (k & 3), ROWS, stride=4), :]
    for d, out in enumerate(outs):
        for i in range(2):
            at = pl.multiple_of((m ^ d ^ (4 * i)) * (SENT // 2), 4)
            out[i * STATS : (i + 1) * STATS, :] = block[pl.ds(at, STATS), :]
            out[2 * STATS + 8 * i : 2 * STATS + 8 * i + 8, :] = block[pl.ds(at + STATS, 8), :]
            out[2 * STATS + 16 + i : 2 * STATS + 17 + i, :] = block[pl.ds(at + STATS + 8, 1), :]
        out[2 * STATS + 18 : SENT, :] = jnp.zeros((6, 128), F32)


def merge_kernel(members, ids, *refs):
    edge, keep, send, edge_out = refs[4:]
    edge_out[...] = edge[...]
    for i, out in enumerate((keep, send)):
        at = i * STATS
        sums = [ref[at : at + HALF, :] for ref in refs[:4]]
        total = (sums[0] + sums[1]) + (sums[2] + sums[3])
        mean = total / (4 * members)
        square = jnp.zeros_like(total)
        for one, ref in zip(sums, refs[:4]):
            dev = one / members - mean
            square = square + (ref[at + HALF : at + STATS, :] + members * (dev * dev))
        out[0:HALF, :] = total
        out[HALF:STATS, :] = square
        for s, ref in enumerate(refs[:4]):
            share = 2 * STATS + 8 * i
            out[STATS + 8 * s : STATS + 8 * s + 8, :] = ref[share : share + 8, :]
            share = 2 * STATS + 16 + i
            out[STATS + 32 + s : STATS + 33 + s, :] = ref[share : share + 1, :]
        out[STATS + 36 : KEPT, :] = jnp.zeros((4, 128), F32)


def placed(share, source):
    lane = lax.broadcasted_iota(jnp.int32, share.shape, 1)
    share = jnp.where(lane < 50, share, 0.0)
    share = jnp.concatenate([share, jnp.zeros((share.shape[0], 256), F32)], axis=1)
    return pltpu.roll(share, lax.rem(48 * source + 383, 384), 1)


def placed_chunk(ref, device):
    wide = jnp.zeros((18, 384), F32)
    for s in range(4):
        most = ref[STATS + 8 * s : STATS + 8 * s + 8, :]
        rest = ref[STATS + 32 + s : STATS + 33 + s, :]
        share = jnp.concatenate([most, pltpu.roll(most, 64, 1), rest, pltpu.roll(rest, 64, 1)], axis=0)
        wide = wide + placed(share, device ^ s)
    return wide


def own_kernel(ids, mine, out):
    out[...] = placed_chunk(mine, ids[0])


def edge_kernel(ids, near, late, taps, weights, out):
    odd = ids[1] & 1
    above, below = taps[0:1, 0:1], taps[3:4, 35:36]
    share = []
    for rows, tap, source in (
        (near, jnp.where(odd == 1, above, below), ids[0]),
        (late, jnp.where(odd == 1, below, above), ids[0] ^ ids[2]),
    ):
        local = local_weights(weights[pl.ds(pl.multiple_of(96 * source, 32), 96), :], source)
        share.append(jnp.dot(rows[...] * tap, local, precision=HIGHEST, preferred_element_type=F32))
    out[...] = share[0] + pltpu.roll(share[1], 64, 1)


def merged(a, b, count):
    one, two = a[0:HALF, :], b[0:HALF, :]
    diff = one - two
    squares = a[HALF:STATS, :] + b[HALF:STATS, :]
    return one + two, squares + diff * diff * (0.5 / count)


def factor_kernel(count, ids, mine, recv, own, edge, out, scratch):
    total, square = merged(mine, recv, count // 2)
    mean = total / count
    spread = jnp.sqrt(square / (count - 1) + 1e-06)
    prior_spread, post_spread = spread[0:ROWS], spread[ROWS:HALF]
    factor = 1.0 + 0.9 * (prior_spread - post_spread) / post_spread
    wide = own[...] + placed_chunk(recv, ids[0] ^ 4)
    for ct in range(3):
        scratch[pl.ds(ct, 18, stride=3), :] = wide[:, 128 * ct : 128 * ct + 128]
    out[0:ROWS, :] = factor
    out[ROWS:HALF, :] = mean[0:ROWS] - factor * mean[ROWS:HALF] + scratch[...]
    out[HALF:GATHER, :] = edge[...]


def join_kernel(ids, a, b, out):
    size = a.shape[0]
    out[0:size, :] = a[...]
    out[size : 2 * size, :] = b[...]


def output_kernel(ids, own, one, two, three, post, out, block, factor, base):
    near = jnp.zeros((EDGE, 384), F32)
    late = near
    for d, ref in enumerate((own, one, two, three)):
        for i in range(2):
            at = i * GATHER
            chunk = ids[0] ^ d ^ (4 * i)
            block[pl.ds(pl.multiple_of(chunk * GATHER, 8), GATHER), :] = ref[at : at + GATHER, :]
            share = ref[at + HALF : at + GATHER, :]
            near = near + placed(share, chunk)
            late = late + placed(pltpu.roll(share, 64, 1), chunk ^ ids[2])
    for k in range(8):
        at = k * GATHER
        to = pl.ds(4 * ROWS * (k >> 2) + (k & 3), ROWS, stride=4)
        factor[to, :] = block[at : at + ROWS, :]
        base[to, :] = block[at + ROWS : at + HALF, :]
    odd = ids[1] & 1
    above = jnp.where(odd == 1, near, late)
    below = jnp.where(odd == 1, late, near)
    for ct in range(3):
        for at, part in ((4 * ct, above), (420 + 4 * ct, below)):
            base[at : at + 4, :] = base[at : at + 4, :] + part[:, 128 * ct : 128 * ct + 128]
    step = 144
    for at in range(0, 432, step):
        scale = factor[at : at + step, :]
        shift = base[at : at + step, :]
        for i in range(post.shape[0]):
            out[i, at : at + step, :] = (shift + scale * post[i, at : at + step, :].astype(F32)).astype(jnp.bfloat16)


def viewed(x):
    members = x.shape[0]
    x = with_layout_constraint(x.reshape(members, 4, 36, 3, 128), Layout(major_to_minor=(0, 2, 3, 1, 4)))
    return x.transpose(0, 2, 3, 1, 4).reshape(members, 432, 128)


def on_device(fine_increment, row_taps, col_weights, prior, posterior):
    mem, hor = lax.axis_size("mem"), lax.axis_size("hor")
    share = prior.shape[0]
    count = share * mem
    m, h = lax.axis_index("mem"), lax.axis_index("hor")
    middle = hor // 2
    apart = jnp.where((h == middle - 1) | (h == middle), 4, 0)
    ids = jnp.stack([m, h, apart]).astype(jnp.int32)

    def swap(x, distance):
        return lax.ppermute(x, "mem", [(i, i ^ distance) for i in range(mem)])

    def swap_rows(x, first, far=None):
        pairs = [(i, i + 1) for i in range(first, hor - 1, 2)]
        pairs = pairs + [(j, i) for i, j in pairs]
        return lax.ppermute(
            x,
            ("mem", "hor"),
            [
                (i * hor + a, (i ^ (4 if a + b == 2 * middle - 1 and far else 0)) * hor + b)
                for i in range(mem)
                for a, b in pairs
            ],
        )

    prior, posterior = viewed(prior), viewed(posterior)
    last, first = fine_increment[:, -1, :], fine_increment[:, 0, :]
    odd = h % 2 == 1

    own, *sent = call(
        first_kernel,
        "first",
        ids,
        (prior, posterior, fine_increment, row_taps, col_weights),
        rows_of(SENT, SENT, SENT, SENT),
        [
            pltpu.VMEM((2, share, 432, 128), jnp.bfloat16),
            pltpu.VMEM((4, 88, 96), F32),
            pltpu.VMEM((4, 36), F32),
            pltpu.VMEM((96, 384), F32),
            pltpu.SemaphoreType.DMA((5,)),
            pltpu.VMEM((4, 432, 128), F32),
            pltpu.VMEM((4 * SENT, 128), F32),
        ],
        mib=60,
        flops=12_000_000,
        specs=[pl.BlockSpec(memory_space=pltpu.HBM)] * 5,
    )
    got = [swap(x, d) for d, x in enumerate(sent, 1)]
    near = swap_rows(jnp.where(odd, first, last), 0)
    late = swap_rows(jnp.where(odd, last, first), 1, True)
    edge = call(edge_kernel, "edge", ids, (near, late, row_taps, col_weights), rows_of(EDGE))
    keep, send, edge = call(
        functools.partial(merge_kernel, share), "merge", ids, [own, *got, edge], rows_of(KEPT, KEPT, EDGE)
    )
    recv = swap(send, 4)
    own = call(own_kernel, "own", ids, (keep,), jax.ShapeDtypeStruct((18, 384), F32))
    near = call(
        functools.partial(factor_kernel, count),
        "factor",
        ids,
        (keep, recv, own, edge),
        rows_of(GATHER),
        [pltpu.VMEM((ROWS, 128), F32)],
    )
    near = call(join_kernel, "join", ids, (near, swap(near, 4)), rows_of(2 * GATHER))
    gathered = [near] + [swap(near, distance) for distance in (1, 2, 3)]
    out = call(
        output_kernel,
        "output",
        ids,
        (*gathered, posterior),
        jax.ShapeDtypeStruct(posterior.shape, jnp.bfloat16),
        [pltpu.VMEM((8 * GATHER, 128), F32)] + [pltpu.VMEM((432, 128), F32)] * 2,
        mib=10,
        flops=2_000_000,
    )
    out = out.reshape(share, 36, 3, 4, 128).transpose(0, 1, 3, 2, 4)
    return out.reshape(share, 36, 4, 384).transpose(0, 2, 1, 3)


def solution(mesh):
    return jax.shard_map(
        on_device,
        mesh=mesh,
        in_specs=(
            P(None, "hor", "mem"),
            P(None, "hor"),
            P(),
            P("mem", None, "hor", None),
            P("mem", None, "hor", None),
        ),
        out_specs=P("mem", None, "hor", None),
        check_vma=False,
    )
```

time: 87 us -> 81.2 us (0.933)
  the two profiles are of different devices: /device:TPU:6 before, /device:TPU:30 now
where the time goes in v3:
time: 81.2 us; the launch traced here: 80.7 us
  starting transfers between devices  57.7 us (71%)
  waiting for transfers between devices  11.7 us (14%)
  Pallas kernels  9.84 us (12%)
    ppermute x8, starting transfers between devices, swap(): return lax.ppermute(x, 'mem', [(i, i ^ distance) for i in range(mem)])  44.2 us
    ppermute x2, starting transfers between devices, swap_rows(): lax.ppermute(x, ('mem', 'hor'), [(i * hor + a, (i ^ (4 if a + b == 2 * mi...  13.5 us
    ppermute x8, waiting for transfers between devices, swap(): return lax.ppermute(x, 'mem', [(i, i ^ distance) for i in range(mem)])  10.9 us
    pallas_call x7, Pallas kernels, call(): pl.pallas_call(kernel, out_shape=out, in_specs=[SMEM] + (specs or [VMEM]...  9.84 us
  transfers between devices with their start and end apart: 10, of which 5 were waited for; matrix products, arithmetic and copies ran while one was open for 1% of the time, Pallas kernels for 2%

profile of v3, /device:TPU:30, one launch (start us, length us, event | category | flops | bytes accessed | tf_op | source)
XLA Modules:
  0.0 80.7 jit_solution(10941002789522678589)
XLA Ops:
  0.0 0.6 pad_add_fusion.ids
  0.6 4.3 %first.1 = (f32[456,128]{1,0:T(8,128)}, f32[456,128]{1,0:T(8,128)}, f32[456,128]{1,0:T(8,128)}, f32[456,128]{1,0:T(8,128)}) custom-call(s32[3]{0:T(128)} %pad_add_fusion.ids, bf16[10,432,128]{2,1,0:T(8,128)(2,1)} %bitcast.28, bf16[10,432,128]{2,1,0:T(8,128)(2,1)} %bitcast.26, f32[4,72,96]{2,1,0:T(8,128)} %fine.1, f32[4,36]{1,0:T(4,128)} %taps.3, ...), custom_call_target="tpu_custom_call" | custom-call | flops 12000000 | bytes 4436544 | tf_op jit(solution)/shard_map/first/pallas_call | solution.py:29
  4.9 4.0 %collective-permute-start = (f32[456,128]{1,0:T(8,128)}, f32[456,128]{1,0:T(8,128)S(1)}, u32[]{:S(2)}, u32[]{:S(2)}) collective-permute-start(f32[456,128]{1,0:T(8,128)} %get-tuple-element.13), channel_id=1, source_target_pairs={{0,64},{64,0},{128,192},{192,128},{256,320},{320,256},{384,448},{4... | collective-permute-start | bytes 700424 | tf_op jit(solution)/shard_map/ppermute | solution.py:245
  8.8 5.2 %collective-permute-start.1 = (f32[456,128]{1,0:T(8,128)}, f32[456,128]{1,0:T(8,128)S(1)}, u32[]{:S(2)}, u32[]{:S(2)}) collective-permute-start(f32[456,128]{1,0:T(8,128)} %get-tuple-element.14), channel_id=1, source_target_pairs={{0,128},{64,192},{128,0},{192,64},{256,384},{320,448},{384,256},{4... | collective-permute-start | bytes 700424 | tf_op jit(solution)/shard_map/ppermute | solution.py:245
  14.0 1.9 %collective-permute-start.2 = (f32[456,128]{1,0:T(8,128)}, f32[456,128]{1,0:T(8,128)S(1)}, u32[]{:S(2)}, u32[]{:S(2)}) collective-permute-start(f32[456,128]{1,0:T(8,128)} %get-tuple-element.15), channel_id=1, source_target_pairs={{0,192},{64,128},{128,64},{192,0},{256,448},{320,384},{384,320},{4... | collective-permute-start | bytes 700424 | tf_op jit(solution)/shard_map/ppermute | solution.py:245
  16.0 0.7 fusion
  16.7 1.9 %collective-permute-start.4 = (f32[4,96]{1,0:T(4,128)S(1)}, f32[4,96]{1,0:T(4,128)S(1)}, u32[]{:S(2)}, u32[]{:S(2)}) collective-permute-start(f32[4,96]{1,0:T(4,128)S(1)} %get-tuple-element.21), channel_id=1, source_target_pairs={{1,2},{3,4},{5,6},{7,8},{9,10},{11,12},{13,14},{15,16},{17,18},{19... | collective-permute-start | bytes 4616 | tf_op jit(solution)/shard_map/ppermute | solution.py:250
  18.6 11.6 %collective-permute-start.3 = (f32[4,96]{1,0:T(4,128)S(1)}, f32[4,96]{1,0:T(4,128)S(1)}, u32[]{:S(2)}, u32[]{:S(2)}) collective-permute-start(f32[4,96]{1,0:T(4,128)S(1)} %get-tuple-element.22), channel_id=1, source_target_pairs={{0,1},{2,3},{4,5},{6,7},{8,9},{10,11},{12,13},{14,15},{16,17},{18,... | collective-permute-start | bytes 4616 | tf_op jit(solution)/shard_map/ppermute | solution.py:250
  30.3 0.8 collective-permute-done.3.near
  31.0 0.9 %edge.1.refs_4_ = f32[4,128]{1,0:T(4,128)S(1)} custom-call(s32[3]{0:T(128)S(1)} %copy-done.3, f32[4,96]{1,0:T(4,128)S(1)} %collective-permute-done.3.near, f32[4,96]{1,0:T(4,128)S(1)} %collective-permute-done.4.late, f32[4,36]{1,0:T(4,128)S(1)} %copy-done.4, f32[768,384]{1,0:T(8,128)S(1)} %copy-done), custom_call_target="tpu_custom_call" | custom-call | flops 200000 | bytes 1185344 | tf_op jit(solution)/shard_map/edge/pallas_call | solution.py:29
  32.0 0.7 merge.1
  32.7 7.8 %collective-permute-start.5 = (f32[256,128]{1,0:T(8,128)S(1)}, f32[256,128]{1,0:T(8,128)S(1)}, u32[]{:S(2)}, u32[]{:S(2)}) collective-permute-start(f32[256,128]{1,0:T(8,128)S(1)} %get-tuple-element.17), channel_id=1, source_target_pairs={{0,256},{64,320},{128,384},{192,448},{256,0},{320,64},{384,128},{4... | collective-permute-start | bytes 393224 | tf_op jit(solution)/shard_map/ppermute | solution.py:245
  40.6 0.7 own.1
  41.3 2.2 %collective-permute-done.5.recv = f32[256,128]{1,0:T(8,128)S(1)} collective-permute-done((f32[256,128]{1,0:T(8,128)S(1)}, f32[256,128]{1,0:T(8,128)S(1)}, u32[]{:S(2)}, u32[]{:S(2)}) %collective-permute-start.5) | collective-permute-done | bytes 131104 | tf_op jit(solution)/shard_map/ppermute | solution.py:245
  43.5 0.7 factor.1.a
  44.2 7.8 %collective-permute-start.6 = (f32[112,128]{1,0:T(8,128)S(1)}, f32[112,128]{1,0:T(8,128)S(1)}, u32[]{:S(2)}, u32[]{:S(2)}) collective-permute-start(f32[112,128]{1,0:T(8,128)S(1)} %factor.1.a), channel_id=1, source_target_pairs={{0,256},{64,320},{128,384},{192,448},{256,0},{320,64},{384,128},{4... | collective-permute-start | bytes 172040 | tf_op jit(solution)/shard_map/ppermute | solution.py:245
  52.1 2.5 %collective-permute-done.6.b = f32[112,128]{1,0:T(8,128)S(1)} collective-permute-done((f32[112,128]{1,0:T(8,128)S(1)}, f32[112,128]{1,0:T(8,128)S(1)}, u32[]{:S(2)}, u32[]{:S(2)}) %collective-permute-start.6) | collective-permute-done | bytes 57376 | tf_op jit(solution)/shard_map/ppermute | solution.py:245
  54.5 0.5 join.1.own
  55.1 13.0 %collective-permute-start.9 = (f32[224,128]{1,0:T(8,128)S(1)}, f32[224,128]{1,0:T(8,128)S(1)}, u32[]{:S(2)}, u32[]{:S(2)}) collective-permute-start(f32[224,128]{1,0:T(8,128)S(1)} %join.1.own), channel_id=1, source_target_pairs={{0,192},{64,128},{128,64},{192,0},{256,448},{320,384},{384,320},{4... | collective-permute-start | bytes 344072 | tf_op jit(solution)/shard_map/ppermute | solution.py:245
  68.1 1.9 %collective-permute-start.8 = (f32[224,128]{1,0:T(8,128)S(1)}, f32[224,128]{1,0:T(8,128)S(1)}, u32[]{:S(2)}, u32[]{:S(2)}) collective-permute-start(f32[224,128]{1,0:T(8,128)S(1)} %join.1.own), channel_id=1, source_target_pairs={{0,128},{64,192},{128,0},{192,64},{256,384},{320,448},{384,256},{4... | collective-permute-start | bytes 344072 | tf_op jit(solution)/shard_map/ppermute | solution.py:245
  70.1 2.5 %collective-permute-start.7 = (f32[224,128]{1,0:T(8,128)S(1)}, f32[224,128]{1,0:T(8,128)S(1)}, u32[]{:S(2)}, u32[]{:S(2)}) collective-permute-start(f32[224,128]{1,0:T(8,128)S(1)} %join.1.own), channel_id=1, source_target_pairs={{0,64},{64,0},{128,192},{192,128},{256,320},{320,256},{384,448},{4... | collective-permute-start | bytes 344072 | tf_op jit(solution)/shard_map/ppermute | solution.py:245
  72.6 4.6 %collective-permute-done.8.two = f32[224,128]{1,0:T(8,128)S(1)} collective-permute-done((f32[224,128]{1,0:T(8,128)S(1)}, f32[224,128]{1,0:T(8,128)S(1)}, u32[]{:S(2)}, u32[]{:S(2)}) %collective-permute-start.8) | collective-permute-done | bytes 114720 | tf_op jit(solution)/shard_map/ppermute | solution.py:245
  77.1 1.6 %collective-permute-done.7.one = f32[224,128]{1,0:T(8,128)S(1)} collective-permute-done((f32[224,128]{1,0:T(8,128)S(1)}, f32[224,128]{1,0:T(8,128)S(1)}, u32[]{:S(2)}, u32[]{:S(2)}) %collective-permute-start.7) | collective-permute-done | bytes 114720 | tf_op jit(solution)/shard_map/ppermute | solution.py:245
  78.7 2.0 %output.1 = bf16[10,432,128]{2,1,0:T(8,128)(2,1)} custom-call(s32[3]{0:T(128)S(1)} %copy-done.3, f32[224,128]{1,0:T(8,128)S(1)} %join.1.own, f32[224,128]{1,0:T(8,128)S(1)} %collective-permute-done.7.one, f32[224,128]{1,0:T(8,128)S(1)} %collective-permute-done.8.two, f32[224,128]{1,0:T(8,128)S(1)} %collective-permute-done.9.three, ...), custom_call_target="tpu_custom_call" | custom-call | flops 2000000 | bytes 2670592 | tf_op jit(solution)/shard_map/output/pallas_call | solution.py:29
  (16 shorter events, 0.1 us)
Async XLA Ops:
  0.6 30.5 %copy-start = (f32[768,384]{1,0:T(8,128)S(1)}, f32[768,384]{1,0:T(8,128)}, u32[]{:S(2)}) copy-start(f32[768,384]{1,0:T(8,128)} %weights.3) | copy-start | bytes 3538948
  0.6 30.5 %copy-start.3 = (s32[3]{0:T(128)S(1)}, s32[3]{0:T(128)}, u32[]{:S(2)}) copy-start(s32[3]{0:T(128)} %pad_add_fusion.ids) | copy-start | bytes 40
  0.6 30.5 %copy-start.4 = (f32[4,36]{1,0:T(4,128)S(1)}, f32[4,36]{1,0:T(4,128)}, u32[]{:S(2)}) copy-start(f32[4,36]{1,0:T(4,128)} %taps.3) | copy-start | bytes 1732
  4.9 27.2 %copy-start.2 = (f32[456,128]{1,0:T(8,128)S(1)}, f32[456,128]{1,0:T(8,128)}, u32[]{:S(2)}) copy-start(f32[456,128]{1,0:T(8,128)} %get-tuple-element.12.refs_0_) | copy-start | bytes 700420
  4.9 27.1 %collective-permute-start = (f32[456,128]{1,0:T(8,128)}, f32[456,128]{1,0:T(8,128)S(1)}, u32[]{:S(2)}, u32[]{:S(2)}) collective-permute-start(f32[456,128]{1,0:T(8,128)} %get-tuple-element.13), channel_id=1, source_target_pairs={{0,64},{64,0},{128,192},{192,128},{256,320},{320,256},{384,448},{4... | collective-permute-start | bytes 700424 | tf_op jit(solution)/shard_map/ppermute | solution.py:245
  8.8 23.2 %collective-permute-start.1 = (f32[456,128]{1,0:T(8,128)}, f32[456,128]{1,0:T(8,128)S(1)}, u32[]{:S(2)}, u32[]{:S(2)}) collective-permute-start(f32[456,128]{1,0:T(8,128)} %get-tuple-element.14), channel_id=1, source_target_pairs={{0,128},{64,192},{128,0},{192,64},{256,384},{320,448},{384,256},{4... | collective-permute-start | bytes 700424 | tf_op jit(solution)/shard_map/ppermute | solution.py:245
  14.0 18.0 %collective-permute-start.2 = (f32[456,128]{1,0:T(8,128)}, f32[456,128]{1,0:T(8,128)S(1)}, u32[]{:S(2)}, u32[]{:S(2)}) collective-permute-start(f32[456,128]{1,0:T(8,128)} %get-tuple-element.15), channel_id=1, source_target_pairs={{0,192},{64,128},{128,64},{192,0},{256,448},{320,384},{384,320},{4... | collective-permute-start | bytes 700424 | tf_op jit(solution)/shard_map/ppermute | solution.py:245
  16.7 13.5 %collective-permute-start.4 = (f32[4,96]{1,0:T(4,128)S(1)}, f32[4,96]{1,0:T(4,128)S(1)}, u32[]{:S(2)}, u32[]{:S(2)}) collective-permute-start(f32[4,96]{1,0:T(4,128)S(1)} %get-tuple-element.21), channel_id=1, source_target_pairs={{1,2},{3,4},{5,6},{7,8},{9,10},{11,12},{13,14},{15,16},{17,18},{19... | collective-permute-start | bytes 4616 | tf_op jit(solution)/shard_map/ppermute | solution.py:250
  18.6 12.4 %collective-permute-start.3 = (f32[4,96]{1,0:T(4,128)S(1)}, f32[4,96]{1,0:T(4,128)S(1)}, u32[]{:S(2)}, u32[]{:S(2)}) collective-permute-start(f32[4,96]{1,0:T(4,128)S(1)} %get-tuple-element.22), channel_id=1, source_target_pairs={{0,1},{2,3},{4,5},{6,7},{8,9},{10,11},{12,13},{14,15},{16,17},{18,... | collective-permute-start | bytes 4616 | tf_op jit(solution)/shard_map/ppermute | solution.py:250
  32.0 46.8 %copy-start.1 = (bf16[10,4,36,384]{3,1,2,0:T(4,128)(2,1)S(1)}, bf16[10,4,36,384]{3,1,2,0:T(4,128)(2,1)}, u32[]{:S(2)}) copy-start(bf16[10,4,36,384]{3,1,2,0:T(4,128)(2,1)} %param.9) | copy-start | bytes 3317764
  32.7 10.8 %collective-permute-start.5 = (f32[256,128]{1,0:T(8,128)S(1)}, f32[256,128]{1,0:T(8,128)S(1)}, u32[]{:S(2)}, u32[]{:S(2)}) collective-permute-start(f32[256,128]{1,0:T(8,128)S(1)} %get-tuple-element.17), channel_id=1, source_target_pairs={{0,256},{64,320},{128,384},{192,448},{256,0},{320,64},{384,128},{4... | collective-permute-start | bytes 393224 | tf_op jit(solution)/shard_map/ppermute | solution.py:245
  44.2 10.3 %collective-permute-start.6 = (f32[112,128]{1,0:T(8,128)S(1)}, f32[112,128]{1,0:T(8,128)S(1)}, u32[]{:S(2)}, u32[]{:S(2)}) collective-permute-start(f32[112,128]{1,0:T(8,128)S(1)} %factor.1.a), channel_id=1, source_target_pairs={{0,256},{64,320},{128,384},{192,448},{256,0},{320,64},{384,128},{4... | collective-permute-start | bytes 172040 | tf_op jit(solution)/shard_map/ppermute | solution.py:245
  55.1 17.5 %collective-permute-start.9 = (f32[224,128]{1,0:T(8,128)S(1)}, f32[224,128]{1,0:T(8,128)S(1)}, u32[]{:S(2)}, u32[]{:S(2)}) collective-permute-start(f32[224,128]{1,0:T(8,128)S(1)} %join.1.own), channel_id=1, source_target_pairs={{0,192},{64,128},{128,64},{192,0},{256,448},{320,384},{384,320},{4... | collective-permute-start | bytes 344072 | tf_op jit(solution)/shard_map/ppermute | solution.py:245
  68.1 9.0 %collective-permute-start.8 = (f32[224,128]{1,0:T(8,128)S(1)}, f32[224,128]{1,0:T(8,128)S(1)}, u32[]{:S(2)}, u32[]{:S(2)}) collective-permute-start(f32[224,128]{1,0:T(8,128)S(1)} %join.1.own), channel_id=1, source_target_pairs={{0,128},{64,192},{128,0},{192,64},{256,384},{320,448},{384,256},{4... | collective-permute-start | bytes 344072 | tf_op jit(solution)/shard_map/ppermute | solution.py:245
  70.1 8.7 %collective-permute-start.7 = (f32[224,128]{1,0:T(8,128)S(1)}, f32[224,128]{1,0:T(8,128)S(1)}, u32[]{:S(2)}, u32[]{:S(2)}) collective-permute-start(f32[224,128]{1,0:T(8,128)S(1)} %join.1.own), channel_id=1, source_target_pairs={{0,64},{64,0},{128,192},{192,128},{256,320},{320,256},{384,448},{4... | collective-permute-start | bytes 344072 | tf_op jit(solution)/shard_map/ppermute | solution.py:245

commit v4 on v3

--- a/solution.py
+++ b/solution.py
@@ -11,7 +11,8 @@
 ROWS = 54
 HALF = 2 * ROWS
 STATS = 4 * ROWS
-SENT = 2 * STATS + 24
+SENT = STATS + 16
+PAIR = STATS + 24
 KEPT = STATS + 40
 EDGE = 4
 GATHER = HALF + EDGE
@@ -21,7 +22,7 @@
 SMEM = pl.BlockSpec(memory_space=pltpu.SMEM)
 
 
-def call(kernel, name, ids, args, out, scratch=(), mib=4, flops=200_000, specs=None):
+def call(kernel, name, ids, args, out, scratch=(), mib=4, flops=200_000, specs=None, outs=None, aliases=None):
     many = isinstance(out, tuple)
     moved = sum(a.size * a.dtype.itemsize for a in args) + sum(
         o.size * o.dtype.itemsize for o in (out if many else (out,))
@@ -30,8 +31,9 @@
         kernel,
         out_shape=out,
         in_specs=[SMEM] + (specs or [VMEM] * len(args)),
-        out_specs=(VMEM,) * len(out) if many else VMEM,
+        out_specs=tuple(outs or (VMEM,) * len(out)) if many else VMEM,
         scratch_shapes=list(scratch),
+        input_output_aliases=aliases or {},
         compiler_params=pltpu.CompilerParams(vmem_limit_bytes=mib * 2**20),
         cost_estimate=pl.CostEstimate(flops=flops, bytes_accessed=moved, transcendentals=0),
         name=name,
@@ -54,14 +56,15 @@
 
 
 def first_kernel(ids, prior, post, fine, taps, weights, *refs):
-    outs, (members, rows, tap, weight, sems, full, block) = refs[:4], refs[4:]
+    outs, (near, late, edge), (members, rows, tap, weight, sems, full, block) = refs[:5], refs[5:8], refs[8:]
     m = ids[0]
     copies = [
         pltpu.make_async_copy(src, dst, sems.at[i])
         for i, (src, dst) in enumerate(
             (
                 (fine, rows.at[:, pl.ds(8, 72), :]),
-                (weights.at[pl.ds(pl.multiple_of(96 * m, 32), 96), :], weight),
+                (weights.at[pl.ds(pl.multiple_of(96 * m, 32), 96), :], weight.at[0]),
+                (weights.at[pl.ds(pl.multiple_of(96 * (m ^ ids[2]), 32), 96), :], weight.at[1]),
                 (taps, tap),
                 (prior, members.at[0]),
                 (post, members.at[1]),
@@ -70,9 +73,17 @@
     ]
     for copy in copies:
         copy.start()
-    for copy in copies[:3]:
+    for copy in copies[:4]:
         copy.wait()
-    local = local_weights(weight[...], m)
+    odd = ids[1] & 1
+    for level in range(4):
+        first, last = rows[level, 8:9, :], rows[level, 79:80, :]
+        near[level : level + 1, :] = jnp.where(odd == 1, first, last)
+        late[level : level + 1, :] = jnp.where(odd == 1, last, first)
+    local = local_weights(weight[0], m)
+    above, below = tap[0:1, 0:1], tap[3:4, 35:36]
+    edge[0] = local * jnp.where(odd == 1, above, below)
+    edge[1] = local_weights(weight[1], m ^ ids[2]) * jnp.where(odd == 1, below, above)
     columns = [column(tap, t) for t in range(4)]
     for level in range(4):
         rows[level, 0:8, :] = jnp.zeros((8, 96), F32)
@@ -82,12 +93,13 @@
             total = total + columns[t] * rows[level, pl.ds(7 + t, 36, stride=2), :]
         part = jnp.dot(total, local, precision=HIGHEST, preferred_element_type=F32)
         for e in range(2):
-            at, row = (level + 4 * e) * SENT // 2 + STATS, 18 * e
+            at, row = (level + 4 * e) * SENT + STATS, 18 * e
             block[at : at + 8, :] = part[row : row + 8] + pltpu.roll(part[row + 8 : row + 16], 64, 1)
             block[at + 8 : at + 9, :] = part[row + 16 : row + 17] + pltpu.roll(part[row + 17 : row + 18], 64, 1)
+            block[at + 9 : at + 16, :] = jnp.zeros((7, 128), F32)
     step = 144
     for which in range(2):
-        copies[3 + which].wait()
+        copies[4 + which].wait()
         count = members.shape[1]
         for at in range(0, 432, step):
             total = members[which, 0, at : at + step, :].astype(F32)
@@ -102,37 +114,66 @@
             full[2 + which, at : at + step, :] = square
     for k in range(8):
         for j in range(4):
-            at = k * SENT // 2 + j * ROWS
+            at = k * SENT + j * ROWS
             block[at : at + ROWS, :] = full[j, pl.ds(4 * ROWS * (k >> 2) + (k & 3), ROWS, stride=4), :]
-    for d, out in enumerate(outs):
-        for i in range(2):
-            at = pl.multiple_of((m ^ d ^ (4 * i)) * (SENT // 2), 4)
-            out[i * STATS : (i + 1) * STATS, :] = block[pl.ds(at, STATS), :]
-            out[2 * STATS + 8 * i : 2 * STATS + 8 * i + 8, :] = block[pl.ds(at + STATS, 8), :]
-            out[2 * STATS + 16 + i : 2 * STATS + 17 + i, :] = block[pl.ds(at + STATS + 8, 1), :]
-        out[2 * STATS + 18 : SENT, :] = jnp.zeros((6, 128), F32)
-
-
-def merge_kernel(members, ids, *refs):
-    edge, keep, send, edge_out = refs[4:]
-    edge_out[...] = edge[...]
-    for i, out in enumerate((keep, send)):
-        at = i * STATS
-        sums = [ref[at : at + HALF, :] for ref in refs[:4]]
-        total = (sums[0] + sums[1]) + (sums[2] + sums[3])
-        mean = total / (4 * members)
-        square = jnp.zeros_like(total)
-        for one, ref in zip(sums, refs[:4]):
-            dev = one / members - mean
-            square = square + (ref[at + HALF : at + STATS, :] + members * (dev * dev))
+    for out, distances in zip(outs, ((4,), (0, 2), (5, 1, 3), (6,), (7,))):
+        for i, d in enumerate(distances):
+            out[i * SENT : (i + 1) * SENT, :] = block[pl.ds(pl.multiple_of((m ^ d) * SENT, 8), SENT), :]
+
+
+def merge(members, refs, out):
+    sums = [ref[0:HALF, :] for ref in refs]
+    total = (sums[0] + sums[1]) + (sums[2] + sums[3])
+    mean = total / (4 * members)
+    square = jnp.zeros_like(total)
+    for one, ref in zip(sums, refs):
+        dev = one / members - mean
+        square = square + (ref[HALF:STATS, :] + members * (dev * dev))
+    out[0:HALF, :] = total
+    out[HALF:STATS, :] = square
+    for s, ref in enumerate(refs):
+        out[STATS + 8 * s : STATS + 8 * s + 8, :] = ref[STATS : STATS + 8, :]
+        out[STATS + 32 + s : STATS + 33 + s, :] = ref[STATS + 8 : STATS + 9, :]
+    out[STATS + 36 : KEPT, :] = jnp.zeros((4, 128), F32)
+
+
+def merged(a, at, b, bt, count):
+    one, two = a[at : at + HALF, :], b[bt : bt + HALF, :]
+    diff = one - two
+    squares = a[at + HALF : at + STATS, :] + b[bt + HALF : bt + STATS, :]
+    return one + two, squares + diff * diff * (0.5 / count)
+
+
+def merge_pair_kernel(members, ids, mine, recv, near, own, on):
+    for i, out in enumerate((own, on)):
+        at, bt = i * SENT, (1 + i) * SENT
+        total, square = merged(mine, at, recv, bt, members)
         out[0:HALF, :] = total
         out[HALF:STATS, :] = square
-        for s, ref in enumerate(refs[:4]):
-            share = 2 * STATS + 8 * i
-            out[STATS + 8 * s : STATS + 8 * s + 8, :] = ref[share : share + 8, :]
-            share = 2 * STATS + 16 + i
-            out[STATS + 32 + s : STATS + 33 + s, :] = ref[share : share + 1, :]
-        out[STATS + 36 : KEPT, :] = jnp.zeros((4, 128), F32)
+        for s, (ref, to) in enumerate(((mine, at + STATS), (recv, bt + STATS))):
+            out[STATS + 8 * s : STATS + 8 * s + 8, :] = ref[to : to + 8, :]
+            out[STATS + 16 + s : STATS + 17 + s, :] = ref[to + 8 : to + 9, :]
+        out[STATS + 18 : PAIR, :] = jnp.zeros((6, 128), F32)
+
+
+def merge_on_kernel(members, ids, *refs):
+    merge(members, refs[:4], refs[6])
+
+
+def merge_own_kernel(members, ids, mine, recv, near, late, weights, keep, wide, edge):
+    total, square = merged(mine, 0, recv, 0, 2 * members)
+    keep[0:HALF, :] = total
+    keep[HALF:STATS, :] = square
+    for s, ref in enumerate((mine, recv)):
+        keep[STATS + 16 * s : STATS + 16 * s + 16, :] = ref[STATS : STATS + 16, :]
+        keep[STATS + 32 + 2 * s : STATS + 34 + 2 * s, :] = ref[STATS + 16 : STATS + 18, :]
+    keep[STATS + 36 : KEPT, :] = jnp.zeros((4, 128), F32)
+    wide[...] = placed_chunk(keep, ids[0])
+    shares = [
+        jnp.dot(rows[...], weights[i], precision=HIGHEST, preferred_element_type=F32)
+        for i, rows in enumerate((near, late))
+    ]
+    edge[...] = shares[0] + pltpu.roll(shares[1], 64, 1)
 
 
 def placed(share, source):
@@ -152,32 +193,8 @@
     return wide
 
 
-def own_kernel(ids, mine, out):
-    out[...] = placed_chunk(mine, ids[0])
-
-
-def edge_kernel(ids, near, late, taps, weights, out):
-    odd = ids[1] & 1
-    above, below = taps[0:1, 0:1], taps[3:4, 35:36]
-    share = []
-    for rows, tap, source in (
-        (near, jnp.where(odd == 1, above, below), ids[0]),
-        (late, jnp.where(odd == 1, below, above), ids[0] ^ ids[2]),
-    ):
-        local = local_weights(weights[pl.ds(pl.multiple_of(96 * source, 32), 96), :], source)
-        share.append(jnp.dot(rows[...] * tap, local, precision=HIGHEST, preferred_element_type=F32))
-    out[...] = share[0] + pltpu.roll(share[1], 64, 1)
-
-
-def merged(a, b, count):
-    one, two = a[0:HALF, :], b[0:HALF, :]
-    diff = one - two
-    squares = a[HALF:STATS, :] + b[HALF:STATS, :]
-    return one + two, squares + diff * diff * (0.5 / count)
-
-
 def factor_kernel(count, ids, mine, recv, own, edge, out, scratch):
-    total, square = merged(mine, recv, count // 2)
+    total, square = merged(mine, 0, recv, 0, count // 2)
     mean = total / count
     spread = jnp.sqrt(square / (count - 1) + 1e-06)
     prior_spread, post_spread = spread[0:ROWS], spread[ROWS:HALF]
@@ -258,37 +275,51 @@
         )
 
     prior, posterior = viewed(prior), viewed(posterior)
-    last, first = fine_increment[:, -1, :], fine_increment[:, 0, :]
-    odd = h % 2 == 1
-
-    own, *sent = call(
+
+    row = jax.ShapeDtypeStruct((4, 96), F32)
+    on, own, *sent, near, late, weights = call(
         first_kernel,
         "first",
         ids,
         (prior, posterior, fine_increment, row_taps, col_weights),
-        rows_of(SENT, SENT, SENT, SENT),
+        rows_of(SENT, 2 * SENT, 3 * SENT, SENT, SENT) + (row, row, jax.ShapeDtypeStruct((2, 96, 128), F32)),
         [
             pltpu.VMEM((2, share, 432, 128), jnp.bfloat16),
             pltpu.VMEM((4, 88, 96), F32),
             pltpu.VMEM((4, 36), F32),
-            pltpu.VMEM((96, 384), F32),
-            pltpu.SemaphoreType.DMA((5,)),
+            pltpu.VMEM((2, 96, 384), F32),
+            pltpu.SemaphoreType.DMA((6,)),
             pltpu.VMEM((4, 432, 128), F32),
-            pltpu.VMEM((4 * SENT, 128), F32),
+            pltpu.VMEM((8 * SENT, 128), F32),
         ],
-        mib=60,
+        mib=52,
         flops=12_000_000,
         specs=[pl.BlockSpec(memory_space=pltpu.HBM)] * 5,
     )
     got = [swap(x, d) for d, x in enumerate(sent, 1)]
-    near = swap_rows(jnp.where(odd, first, last), 0)
-    late = swap_rows(jnp.where(odd, last, first), 1, True)
-    edge = call(edge_kernel, "edge", ids, (near, late, row_taps, col_weights), rows_of(EDGE))
-    keep, send, edge = call(
-        functools.partial(merge_kernel, share), "merge", ids, [own, *got, edge], rows_of(KEPT, KEPT, EDGE)
+    near = swap_rows(near, 0)
+    own, pair = call(
+        functools.partial(merge_pair_kernel, share), "merge_pair", ids, (own, got[0], near), rows_of(PAIR, PAIR)
+    )
+    anywhere = [pl.BlockSpec(memory_space=pl.ANY)]
+    send, late = call(
+        functools.partial(merge_on_kernel, share),
+        "merge_on",
+        ids,
+        (on, *got, pair, late),
+        (rows_of(KEPT), row),
+        specs=[VMEM] * 4 + anywhere * 2,
+        outs=[VMEM] + anywhere,
+        aliases={6: 1},
     )
     recv = swap(send, 4)
-    own = call(own_kernel, "own", ids, (keep,), jax.ShapeDtypeStruct((18, 384), F32))
+    keep, own, edge = call(
+        functools.partial(merge_own_kernel, share),
+        "merge_own",
+        ids,
+        (own, swap(pair, 2), near, swap_rows(late, 1, True), weights),
+        (rows_of(KEPT), jax.ShapeDtypeStruct((18, 384), F32), rows_of(EDGE)),
+    )
     near = call(
         functools.partial(factor_kernel, count),
         "factor",

time: 81.2 us -> 79.5 us (0.979)
  the two profiles are of different devices: /device:TPU:30 before, /device:TPU:31 now
where the time goes in v4:
time: 79.5 us; the launch traced here: 79 us
  starting transfers between devices  44.8 us (56%)
  waiting for transfers between devices  24 us (30%)
  Pallas kernels  8.49 us (11%)
  local copies, waits for them, and re-layouts  1.6 us (2%)
    ppermute x9, starting transfers between devices, swap(): return lax.ppermute(x, 'mem', [(i, i ^ distance) for i in range(mem)])  33.6 us
    ppermute x9, waiting for transfers between devices, swap(): return lax.ppermute(x, 'mem', [(i, i ^ distance) for i in range(mem)])  18.2 us
    ppermute x2, starting transfers between devices, swap_rows(): lax.ppermute(x, ('mem', 'hor'), [(i * hor + a, (i ^ (4 if a + b == 2 * mi...  11.2 us
    pallas_call x7, Pallas kernels, call(): pl.pallas_call(kernel, out_shape=out, in_specs=[SMEM] + (specs or [VMEM]...  8.49 us
    ppermute x2, waiting for transfers between devices, swap_rows(): lax.ppermute(x, ('mem', 'hor'), [(i * hor + a, (i ^ (4 if a + b == 2 * mi...  5.79 us
    unnamed x6, local copies, waits for them, and re-layouts  1.6 us
  transfers between devices with their start and end apart: 11, of which 6 were waited for; matrix products, arithmetic and copies ran while one was open for 0% of the time, Pallas kernels for 2%

profile of v4, /device:TPU:31, one launch (start us, length us, event | category | flops | bytes accessed | tf_op | source)
XLA Modules:
  0.0 79.0 jit_solution(10097265491720856228)
XLA Ops:
  0.1 0.9 %copy-done.1 = f32[4,72,96]{2,1,0:T(8,128)S(1)} copy-done((f32[4,72,96]{2,1,0:T(8,128)S(1)}, f32[4,72,96]{2,1,0:T(8,128)}, u32[]{:S(2)}) %copy-start.1) | copy-done | bytes 110616
  1.0 0.7 copy-done.2
  1.7 3.2 %first.1 = (f32[232,128]{1,0:T(8,128)S(1)}, f32[464,128]{1,0:T(8,128)S(1)}, f32[696,128]{1,0:T(8,128)S(1)}, f32[232,128]{1,0:T(8,128)S(1)}, f32[232,128]{1,0:T(8...) custom-call(s32[3]{0:T(128)S(1)} %pad_add_fusion.ids, ...), custom_call_target="tpu_custom_call" | custom-call | flops 12000000 | bytes 4554304 | tf_op jit(solution)/shard_map/first/pallas_call | solution.py:30
  4.9 3.5 %collective-permute-start = (f32[696,128]{1,0:T(8,128)S(1)}, f32[696,128]{1,0:T(8,128)S(1)}, u32[]{:S(2)}, u32[]{:S(2)}) collective-permute-start(f32[696,128]{1,0:T(8,128)S(1)} %get-tuple-element.21), channel_id=1, source_target_pairs={{0,64},{64,0},{128,192},{192,128},{256,320},{320,256},{384,448},{4... | collective-permute-start | bytes 1069064 | tf_op jit(solution)/shard_map/ppermute | solution.py:262
  8.4 4.9 %collective-permute-start.3 = (f32[232,128]{1,0:T(8,128)S(1)}, f32[232,128]{1,0:T(8,128)S(1)}, u32[]{:S(2)}, u32[]{:S(2)}) collective-permute-start(f32[232,128]{1,0:T(8,128)S(1)} %get-tuple-element.26), channel_id=1, source_target_pairs={{0,128},{64,192},{128,0},{192,64},{256,384},{320,448},{384,256},{4... | collective-permute-start | bytes 356360 | tf_op jit(solution)/shard_map/ppermute | solution.py:262
  13.3 1.9 %collective-permute-start.4 = (f32[232,128]{1,0:T(8,128)S(1)}, f32[232,128]{1,0:T(8,128)S(1)}, u32[]{:S(2)}, u32[]{:S(2)}) collective-permute-start(f32[232,128]{1,0:T(8,128)S(1)} %get-tuple-element.27), channel_id=1, source_target_pairs={{0,192},{64,128},{128,64},{192,0},{256,448},{320,384},{384,320},{4... | collective-permute-start | bytes 356360 | tf_op jit(solution)/shard_map/ppermute | solution.py:262
  15.3 3.2 %collective-permute-start.1 = (f32[4,96]{1,0:T(4,128)S(1)}, f32[4,96]{1,0:T(4,128)S(1)}, u32[]{:S(2)}, u32[]{:S(2)}) collective-permute-start(f32[4,96]{1,0:T(4,128)S(1)} %get-tuple-element.22), channel_id=1, source_target_pairs={{0,1},{2,3},{4,5},{6,7},{8,9},{10,11},{12,13},{14,15},{16,17},{18,... | collective-permute-start | bytes 4616 | tf_op jit(solution)/shard_map/ppermute | solution.py:267
  18.5 0.8 %collective-permute-done.1.near = f32[4,96]{1,0:T(4,128)S(1)} collective-permute-done((f32[4,96]{1,0:T(4,128)S(1)}, f32[4,96]{1,0:T(4,128)S(1)}, u32[]{:S(2)}, u32[]{:S(2)}) %collective-permute-start.1) | collective-permute-done | bytes 1568 | tf_op jit(solution)/shard_map/ppermute | solution.py:267
  19.9 4.3 %collective-permute-done.4.refs_3_ = f32[232,128]{1,0:T(8,128)S(1)} collective-permute-done((f32[232,128]{1,0:T(8,128)S(1)}, f32[232,128]{1,0:T(8,128)S(1)}, u32[]{:S(2)}, u32[]{:S(2)}) %collective-permute-start.4) | collective-permute-done | bytes 118816 | tf_op jit(solution)/shard_map/ppermute | solution.py:262
  24.1 0.6 merge_on.1
  24.7 8.9 %collective-permute-start.6 = (f32[256,128]{1,0:T(8,128)S(1)}, f32[256,128]{1,0:T(8,128)S(1)}, u32[]{:S(2)}, u32[]{:S(2)}) collective-permute-start(f32[256,128]{1,0:T(8,128)S(1)} %get-tuple-element.32), channel_id=1, source_target_pairs={{0,256},{64,320},{128,384},{192,448},{256,0},{320,64},{384,128},{4... | collective-permute-start | bytes 393224 | tf_op jit(solution)/shard_map/ppermute | solution.py:262
  33.6 3.2 %collective-permute-start.2 = (f32[240,128]{1,0:T(8,128)S(1)}, f32[240,128]{1,0:T(8,128)S(1)}, u32[]{:S(2)}, u32[]{:S(2)}) collective-permute-start(f32[240,128]{1,0:T(8,128)S(1)} %get-tuple-element.24.refs_4_), channel_id=1, source_target_pairs={{0,128},{64,192},{128,0},{192,64},{256,384},{320,448},{384,256},{4... | collective-permute-start | bytes 368648 | tf_op jit(solution)/shard_map/ppermute | solution.py:262
  36.8 8.0 %collective-permute-start.5 = (f32[4,96]{1,0:T(4,128)S(1)}, f32[4,96]{1,0:T(4,128)S(1)}, u32[]{:S(2)}, u32[]{:S(2)}) collective-permute-start(f32[4,96]{1,0:T(4,128)S(1)} %get-tuple-element.29), channel_id=1, source_target_pairs={{1,2},{3,4},{5,6},{7,8},{9,10},{11,12},{13,14},{15,16},{17,18},{19... | collective-permute-start | bytes 4616 | tf_op jit(solution)/shard_map/ppermute | solution.py:267
  44.8 5.0 %collective-permute-done.5.late = f32[4,96]{1,0:T(4,128)S(1)} collective-permute-done((f32[4,96]{1,0:T(4,128)S(1)}, f32[4,96]{1,0:T(4,128)S(1)}, u32[]{:S(2)}, u32[]{:S(2)}) %collective-permute-start.5) | collective-permute-done | bytes 1568 | tf_op jit(solution)/shard_map/ppermute | solution.py:267
  49.8 0.8 %merge_own.1 = (f32[256,128]{1,0:T(8,128)S(1)}, f32[18,384]{1,0:T(8,128)S(1)}, f32[4,128]{1,0:T(4,128)S(1)}) custom-call(s32[3]{0:T(128)S(1)} %pad_add_fusion.ids, f32[240,128]{1,0:T(8,128)S(1)} %get-tuple-element.23.mine, f32[240,128]{1,0:T(8,128)S(1)} %collective-permute-done.2.recv, f32[4,96]{1,0:T(4,128)S(1)} %collective-permute-done.1.near, ...), custom_call_target="tpu_custom_call" | custom-call | flops 200000 | bytes 507904 | tf_op jit(solution)/shard_map/merge_own/pallas_call | solution.py:30
  50.6 0.7 factor.1.a
  51.3 1.9 %collective-permute-start.7 = (f32[112,128]{1,0:T(8,128)S(1)}, f32[112,128]{1,0:T(8,128)S(1)}, u32[]{:S(2)}, u32[]{:S(2)}) collective-permute-start(f32[112,128]{1,0:T(8,128)S(1)} %factor.1.a), channel_id=1, source_target_pairs={{0,256},{64,320},{128,384},{192,448},{256,0},{320,64},{384,128},{4... | collective-permute-start | bytes 172040 | tf_op jit(solution)/shard_map/ppermute | solution.py:262
  53.3 8.5 %collective-permute-done.7.b = f32[112,128]{1,0:T(8,128)S(1)} collective-permute-done((f32[112,128]{1,0:T(8,128)S(1)}, f32[112,128]{1,0:T(8,128)S(1)}, u32[]{:S(2)}, u32[]{:S(2)}) %collective-permute-start.7) | collective-permute-done | bytes 57376 | tf_op jit(solution)/shard_map/ppermute | solution.py:262
  62.4 1.9 %collective-permute-start.10 = (f32[224,128]{1,0:T(8,128)S(1)}, f32[224,128]{1,0:T(8,128)S(1)}, u32[]{:S(2)}, u32[]{:S(2)}) collective-permute-start(f32[224,128]{1,0:T(8,128)S(1)} %join.1.own), channel_id=1, source_target_pairs={{0,192},{64,128},{128,64},{192,0},{256,448},{320,384},{384,320},{4... | collective-permute-start | bytes 344072 | tf_op jit(solution)/shard_map/ppermute | solution.py:262
  64.3 3.0 %collective-permute-start.9 = (f32[224,128]{1,0:T(8,128)S(1)}, f32[224,128]{1,0:T(8,128)S(1)}, u32[]{:S(2)}, u32[]{:S(2)}) collective-permute-start(f32[224,128]{1,0:T(8,128)S(1)} %join.1.own), channel_id=1, source_target_pairs={{0,128},{64,192},{128,0},{192,64},{256,384},{320,448},{384,256},{4... | collective-permute-start | bytes 344072 | tf_op jit(solution)/shard_map/ppermute | solution.py:262
  67.3 4.4 %collective-permute-start.8 = (f32[224,128]{1,0:T(8,128)S(1)}, f32[224,128]{1,0:T(8,128)S(1)}, u32[]{:S(2)}, u32[]{:S(2)}) collective-permute-start(f32[224,128]{1,0:T(8,128)S(1)} %join.1.own), channel_id=1, source_target_pairs={{0,64},{64,0},{128,192},{192,128},{256,320},{320,256},{384,448},{4... | collective-permute-start | bytes 344072 | tf_op jit(solution)/shard_map/ppermute | solution.py:262
  71.7 3.8 %collective-permute-done.9.two = f32[224,128]{1,0:T(8,128)S(1)} collective-permute-done((f32[224,128]{1,0:T(8,128)S(1)}, f32[224,128]{1,0:T(8,128)S(1)}, u32[]{:S(2)}, u32[]{:S(2)}) %collective-permute-start.9) | collective-permute-done | bytes 114720 | tf_op jit(solution)/shard_map/ppermute | solution.py:262
  75.4 1.6 %collective-permute-done.8.one = f32[224,128]{1,0:T(8,128)S(1)} collective-permute-done((f32[224,128]{1,0:T(8,128)S(1)}, f32[224,128]{1,0:T(8,128)S(1)}, u32[]{:S(2)}, u32[]{:S(2)}) %collective-permute-start.8) | collective-permute-done | bytes 114720 | tf_op jit(solution)/shard_map/ppermute | solution.py:262
  77.0 2.0 %output.1 = bf16[10,432,128]{2,1,0:T(8,128)(2,1)} custom-call(s32[3]{0:T(128)S(1)} %pad_add_fusion.ids, f32[224,128]{1,0:T(8,128)S(1)} %join.1.own, f32[224,128]{1,0:T(8,128)S(1)} %collective-permute-done.8.one, f32[224,128]{1,0:T(8,128)S(1)} %collective-permute-done.9.two, f32[224,128]{1,0:T(8,128)S(1)} %collective-permute-done.10.three, ...), custom_call_target="tpu_custom_call" | custom-call | flops 2000000 | bytes 2670592 | tf_op jit(solution)/shard_map/output/pallas_call | solution.py:30
  (12 shorter events, 1.2 us)
Async XLA Ops:
  0.1 0.9 %copy-start.1 = (f32[4,72,96]{2,1,0:T(8,128)S(1)}, f32[4,72,96]{2,1,0:T(8,128)}, u32[]{:S(2)}) copy-start(f32[4,72,96]{2,1,0:T(8,128)} %fine.1) | copy-start | bytes 331780
  1.0 0.7 copy-start.2
  4.9 14.4 %collective-permute-start = (f32[696,128]{1,0:T(8,128)S(1)}, f32[696,128]{1,0:T(8,128)S(1)}, u32[]{:S(2)}, u32[]{:S(2)}) collective-permute-start(f32[696,128]{1,0:T(8,128)S(1)} %get-tuple-element.21), channel_id=1, source_target_pairs={{0,64},{64,0},{128,192},{192,128},{256,320},{320,256},{384,448},{4... | collective-permute-start | bytes 1069064 | tf_op jit(solution)/shard_map/ppermute | solution.py:262
  8.4 11.4 %collective-permute-start.3 = (f32[232,128]{1,0:T(8,128)S(1)}, f32[232,128]{1,0:T(8,128)S(1)}, u32[]{:S(2)}, u32[]{:S(2)}) collective-permute-start(f32[232,128]{1,0:T(8,128)S(1)} %get-tuple-element.26), channel_id=1, source_target_pairs={{0,128},{64,192},{128,0},{192,64},{256,384},{320,448},{384,256},{4... | collective-permute-start | bytes 356360 | tf_op jit(solution)/shard_map/ppermute | solution.py:262
  13.3 10.8 %collective-permute-start.4 = (f32[232,128]{1,0:T(8,128)S(1)}, f32[232,128]{1,0:T(8,128)S(1)}, u32[]{:S(2)}, u32[]{:S(2)}) collective-permute-start(f32[232,128]{1,0:T(8,128)S(1)} %get-tuple-element.27), channel_id=1, source_target_pairs={{0,192},{64,128},{128,64},{192,0},{256,448},{320,384},{384,320},{4... | collective-permute-start | bytes 356360 | tf_op jit(solution)/shard_map/ppermute | solution.py:262
  15.3 4.0 %collective-permute-start.1 = (f32[4,96]{1,0:T(4,128)S(1)}, f32[4,96]{1,0:T(4,128)S(1)}, u32[]{:S(2)}, u32[]{:S(2)}) collective-permute-start(f32[4,96]{1,0:T(4,128)S(1)} %get-tuple-element.22), channel_id=1, source_target_pairs={{0,1},{2,3},{4,5},{6,7},{8,9},{10,11},{12,13},{14,15},{16,17},{18,... | collective-permute-start | bytes 4616 | tf_op jit(solution)/shard_map/ppermute | solution.py:267
  19.3 57.7 %copy-start = (bf16[10,4,36,384]{3,1,2,0:T(4,128)(2,1)S(1)}, bf16[10,4,36,384]{3,1,2,0:T(4,128)(2,1)}, u32[]{:S(2)}) copy-start(bf16[10,4,36,384]{3,1,2,0:T(4,128)(2,1)} %param.9) | copy-start | bytes 3317764
  24.7 25.9 %collective-permute-start.6 = (f32[256,128]{1,0:T(8,128)S(1)}, f32[256,128]{1,0:T(8,128)S(1)}, u32[]{:S(2)}, u32[]{:S(2)}) collective-permute-start(f32[256,128]{1,0:T(8,128)S(1)} %get-tuple-element.32), channel_id=1, source_target_pairs={{0,256},{64,320},{128,384},{192,448},{256,0},{320,64},{384,128},{4... | collective-permute-start | bytes 393224 | tf_op jit(solution)/shard_map/ppermute | solution.py:262
  33.6 16.2 %collective-permute-start.2 = (f32[240,128]{1,0:T(8,128)S(1)}, f32[240,128]{1,0:T(8,128)S(1)}, u32[]{:S(2)}, u32[]{:S(2)}) collective-permute-start(f32[240,128]{1,0:T(8,128)S(1)} %get-tuple-element.24.refs_4_), channel_id=1, source_target_pairs={{0,128},{64,192},{128,0},{192,64},{256,384},{320,448},{384,256},{4... | collective-permute-start | bytes 368648 | tf_op jit(solution)/shard_map/ppermute | solution.py:262
  36.8 13.0 %collective-permute-start.5 = (f32[4,96]{1,0:T(4,128)S(1)}, f32[4,96]{1,0:T(4,128)S(1)}, u32[]{:S(2)}, u32[]{:S(2)}) collective-permute-start(f32[4,96]{1,0:T(4,128)S(1)} %get-tuple-element.29), channel_id=1, source_target_pairs={{1,2},{3,4},{5,6},{7,8},{9,10},{11,12},{13,14},{15,16},{17,18},{19... | collective-permute-start | bytes 4616 | tf_op jit(solution)/shard_map/ppermute | solution.py:267
  51.3 10.5 %collective-permute-start.7 = (f32[112,128]{1,0:T(8,128)S(1)}, f32[112,128]{1,0:T(8,128)S(1)}, u32[]{:S(2)}, u32[]{:S(2)}) collective-permute-start(f32[112,128]{1,0:T(8,128)S(1)} %factor.1.a), channel_id=1, source_target_pairs={{0,256},{64,320},{128,384},{192,448},{256,0},{320,64},{384,128},{4... | collective-permute-start | bytes 172040 | tf_op jit(solution)/shard_map/ppermute | solution.py:262
  62.4 9.3 %collective-permute-start.10 = (f32[224,128]{1,0:T(8,128)S(1)}, f32[224,128]{1,0:T(8,128)S(1)}, u32[]{:S(2)}, u32[]{:S(2)}) collective-permute-start(f32[224,128]{1,0:T(8,128)S(1)} %join.1.own), channel_id=1, source_target_pairs={{0,192},{64,128},{128,64},{192,0},{256,448},{320,384},{384,320},{4... | collective-permute-start | bytes 344072 | tf_op jit(solution)/shard_map/ppermute | solution.py:262
  64.3 11.1 %collective-permute-start.9 = (f32[224,128]{1,0:T(8,128)S(1)}, f32[224,128]{1,0:T(8,128)S(1)}, u32[]{:S(2)}, u32[]{:S(2)}) collective-permute-start(f32[224,128]{1,0:T(8,128)S(1)} %join.1.own), channel_id=1, source_target_pairs={{0,128},{64,192},{128,0},{192,64},{256,384},{320,448},{384,256},{4... | collective-permute-start | bytes 344072 | tf_op jit(solution)/shard_map/ppermute | solution.py:262
  67.3 9.8 %collective-permute-start.8 = (f32[224,128]{1,0:T(8,128)S(1)}, f32[224,128]{1,0:T(8,128)S(1)}, u32[]{:S(2)}, u32[]{:S(2)}) collective-permute-start(f32[224,128]{1,0:T(8,128)S(1)} %join.1.own), channel_id=1, source_target_pairs={{0,64},{64,0},{128,192},{192,128},{256,320},{320,256},{384,448},{4... | collective-permute-start | bytes 344072 | tf_op jit(solution)/shard_map/ppermute | solution.py:262

commit v5 on v4

--- a/solution.py
+++ b/solution.py
@@ -157,23 +157,7 @@
 
 
 def merge_on_kernel(members, ids, *refs):
-    merge(members, refs[:4], refs[6])
-
-
-def merge_own_kernel(members, ids, mine, recv, near, late, weights, keep, wide, edge):
-    total, square = merged(mine, 0, recv, 0, 2 * members)
-    keep[0:HALF, :] = total
-    keep[HALF:STATS, :] = square
-    for s, ref in enumerate((mine, recv)):
-        keep[STATS + 16 * s : STATS + 16 * s + 16, :] = ref[STATS : STATS + 16, :]
-        keep[STATS + 32 + 2 * s : STATS + 34 + 2 * s, :] = ref[STATS + 16 : STATS + 18, :]
-    keep[STATS + 36 : KEPT, :] = jnp.zeros((4, 128), F32)
-    wide[...] = placed_chunk(keep, ids[0])
-    shares = [
-        jnp.dot(rows[...], weights[i], precision=HIGHEST, preferred_element_type=F32)
-        for i, rows in enumerate((near, late))
-    ]
-    edge[...] = shares[0] + pltpu.roll(shares[1], 64, 1)
+    merge(members, refs[3::-1], refs[6])
 
 
 def placed(share, source):
@@ -183,28 +167,38 @@
     return pltpu.roll(share, lax.rem(48 * source + 383, 384), 1)
 
 
-def placed_chunk(ref, device):
+def placed_chunk(ref, device, count):
     wide = jnp.zeros((18, 384), F32)
-    for s in range(4):
+    for s in range(count):
         most = ref[STATS + 8 * s : STATS + 8 * s + 8, :]
-        rest = ref[STATS + 32 + s : STATS + 33 + s, :]
+        rest = ref[STATS + 8 * count + s : STATS + 8 * count + s + 1, :]
         share = jnp.concatenate([most, pltpu.roll(most, 64, 1), rest, pltpu.roll(rest, 64, 1)], axis=0)
         wide = wide + placed(share, device ^ s)
     return wide
 
 
-def factor_kernel(count, ids, mine, recv, own, edge, out, scratch):
-    total, square = merged(mine, 0, recv, 0, count // 2)
+def put_together(one, two, count):
+    diff = one[0] - two[0]
+    return one[0] + two[0], one[1] + two[1] + diff * diff * (0.5 / count)
+
+
+def factor_kernel(count, ids, mine, two, recv, near, late, weights, out, scratch):
+    pair, more, rest = ((ref[0:HALF, :], ref[HALF:STATS, :]) for ref in (mine, two, recv))
+    total, square = put_together(put_together(pair, more, count // 4), rest, count // 2)
     mean = total / count
     spread = jnp.sqrt(square / (count - 1) + 1e-06)
     prior_spread, post_spread = spread[0:ROWS], spread[ROWS:HALF]
     factor = 1.0 + 0.9 * (prior_spread - post_spread) / post_spread
-    wide = own[...] + placed_chunk(recv, ids[0] ^ 4)
+    wide = placed_chunk(mine, ids[0], 2) + placed_chunk(two, ids[0] ^ 2, 2) + placed_chunk(recv, ids[0] ^ 4, 4)
     for ct in range(3):
         scratch[pl.ds(ct, 18, stride=3), :] = wide[:, 128 * ct : 128 * ct + 128]
     out[0:ROWS, :] = factor
     out[ROWS:HALF, :] = mean[0:ROWS] - factor * mean[ROWS:HALF] + scratch[...]
-    out[HALF:GATHER, :] = edge[...]
+    shares = [
+        jnp.dot(rows[...], weights[i], precision=HIGHEST, preferred_element_type=F32)
+        for i, rows in enumerate((near, late))
+    ]
+    out[HALF:GATHER, :] = shares[0] + pltpu.roll(shares[1], 64, 1)
 
 
 def join_kernel(ids, a, b, out):
@@ -306,25 +300,18 @@
         functools.partial(merge_on_kernel, share),
         "merge_on",
         ids,
-        (on, *got, pair, late),
+        (*got[::-1], on, pair, late),
         (rows_of(KEPT), row),
         specs=[VMEM] * 4 + anywhere * 2,
         outs=[VMEM] + anywhere,
         aliases={6: 1},
     )
     recv = swap(send, 4)
-    keep, own, edge = call(
-        functools.partial(merge_own_kernel, share),
-        "merge_own",
-        ids,
-        (own, swap(pair, 2), near, swap_rows(late, 1, True), weights),
-        (rows_of(KEPT), jax.ShapeDtypeStruct((18, 384), F32), rows_of(EDGE)),
-    )
     near = call(
         functools.partial(factor_kernel, count),
         "factor",
         ids,
-        (keep, recv, own, edge),
+        (own, swap(pair, 2), recv, near, swap_rows(late, 1, True), weights),
         rows_of(GATHER),
         [pltpu.VMEM((ROWS, 128), F32)],
     )

time: 79.5 us -> 77 us (0.969)
  waiting for transfers between devices: 24 us -> 16.9 us
  starting transfers between devices: 44.8 us -> 50.1 us
    ppermute x9, waiting for transfers between devices: 18.2 us -> 12.9 us  [swap(): return lax.ppermute(x, 'mem', [(i, i ^ distance) for i in range(mem)])]
    ppermute x9, starting transfers between devices: 33.6 us -> 36.9 us  [swap(): return lax.ppermute(x, 'mem', [(i, i ^ distance) for i in range(mem)])]
    ppermute x2, starting transfers between devices: 11.2 us -> 13.3 us  [swap_rows(): lax.ppermute(x, ('mem', 'hor'), [(i * hor + a, (i ^ (4 if a + b == 2 * mi...]
    ppermute x2, waiting for transfers between devices: 5.79 us -> 3.96 us  [swap_rows(): lax.ppermute(x, ('mem', 'hor'), [(i * hor + a, (i ^ (4 if a + b == 2 * mi...]
    pallas_call x7 -> x6, Pallas kernels: 8.49 us -> 7.77 us  [call(): pl.pallas_call(kernel, out_shape=out, in_specs=[SMEM] + (specs or [VMEM]...]
  transfers between devices with their start and end apart: 11 -> 11, of which waited for: 6 -> 6; matrix products, arithmetic and copies ran while one was open for 0% -> 0% of each run, Pallas kernels for 2% -> 1%
where the time goes in v5:
time: 77 us; the launch traced here: 76.6 us
  starting transfers between devices  50.1 us (65%)
  waiting for transfers between devices  16.9 us (22%)
  Pallas kernels  7.77 us (10%)
  local copies, waits for them, and re-layouts  1.6 us (2%)
    ppermute x9, starting transfers between devices, swap(): return lax.ppermute(x, 'mem', [(i, i ^ distance) for i in range(mem)])  36.9 us
    ppermute x2, starting transfers between devices, swap_rows(): lax.ppermute(x, ('mem', 'hor'), [(i * hor + a, (i ^ (4 if a + b == 2 * mi...  13.3 us
    ppermute x9, waiting for transfers between devices, swap(): return lax.ppermute(x, 'mem', [(i, i ^ distance) for i in range(mem)])  12.9 us
    pallas_call x6, Pallas kernels, call(): pl.pallas_call(kernel, out_shape=out, in_specs=[SMEM] + (specs or [VMEM]...  7.77 us
    ppermute x2, waiting for transfers between devices, swap_rows(): lax.ppermute(x, ('mem', 'hor'), [(i * hor + a, (i ^ (4 if a + b == 2 * mi...  3.96 us
    unnamed x6, local copies, waits for them, and re-layouts  1.6 us
  transfers between devices with their start and end apart: 11, of which 6 were waited for; matrix products, arithmetic and copies ran while one was open for 0% of the time, Pallas kernels for 1%

profile of v5, /device:TPU:31, one launch (start us, length us, event | category | flops | bytes accessed | tf_op | source)
XLA Modules:
  0.0 76.6 jit_solution(9174677331429554747)
XLA Ops:
  0.1 0.9 %copy-done.1 = f32[4,72,96]{2,1,0:T(8,128)S(1)} copy-done((f32[4,72,96]{2,1,0:T(8,128)S(1)}, f32[4,72,96]{2,1,0:T(8,128)}, u32[]{:S(2)}) %copy-start.1) | copy-done | bytes 110616
  1.0 0.7 copy-done.2
  1.7 3.2 %first.1 = (f32[232,128]{1,0:T(8,128)S(1)}, f32[464,128]{1,0:T(8,128)S(1)}, f32[696,128]{1,0:T(8,128)S(1)}, f32[232,128]{1,0:T(8,128)S(1)}, f32[232,128]{1,0:T(8...) custom-call(s32[3]{0:T(128)S(1)} %pad_add_fusion.ids, ...), custom_call_target="tpu_custom_call" | custom-call | flops 12000000 | bytes 4554304 | tf_op jit(solution)/shard_map/first/pallas_call | solution.py:30
  4.9 3.5 %collective-permute-start = (f32[696,128]{1,0:T(8,128)S(1)}, f32[696,128]{1,0:T(8,128)S(1)}, u32[]{:S(2)}, u32[]{:S(2)}) collective-permute-start(f32[696,128]{1,0:T(8,128)S(1)} %get-tuple-element.18), channel_id=1, source_target_pairs={{0,64},{64,0},{128,192},{192,128},{256,320},{320,256},{384,448},{4... | collective-permute-start | bytes 1069064 | tf_op jit(solution)/shard_map/ppermute | solution.py:256
  8.4 4.6 %collective-permute-start.3 = (f32[232,128]{1,0:T(8,128)S(1)}, f32[232,128]{1,0:T(8,128)S(1)}, u32[]{:S(2)}, u32[]{:S(2)}) collective-permute-start(f32[232,128]{1,0:T(8,128)S(1)} %get-tuple-element.22), channel_id=1, source_target_pairs={{0,192},{64,128},{128,64},{192,0},{256,448},{320,384},{384,320},{4... | collective-permute-start | bytes 356360 | tf_op jit(solution)/shard_map/ppermute | solution.py:256
  13.1 2.2 %collective-permute-start.4 = (f32[232,128]{1,0:T(8,128)S(1)}, f32[232,128]{1,0:T(8,128)S(1)}, u32[]{:S(2)}, u32[]{:S(2)}) collective-permute-start(f32[232,128]{1,0:T(8,128)S(1)} %get-tuple-element.23), channel_id=1, source_target_pairs={{0,128},{64,192},{128,0},{192,64},{256,384},{320,448},{384,256},{4... | collective-permute-start | bytes 356360 | tf_op jit(solution)/shard_map/ppermute | solution.py:256
  15.3 3.2 %collective-permute-start.1 = (f32[4,96]{1,0:T(4,128)S(1)}, f32[4,96]{1,0:T(4,128)S(1)}, u32[]{:S(2)}, u32[]{:S(2)}) collective-permute-start(f32[4,96]{1,0:T(4,128)S(1)} %get-tuple-element.19), channel_id=1, source_target_pairs={{0,1},{2,3},{4,5},{6,7},{8,9},{10,11},{12,13},{14,15},{16,17},{18,... | collective-permute-start | bytes 4616 | tf_op jit(solution)/shard_map/ppermute | solution.py:261
  18.5 0.8 %collective-permute-done.1.near = f32[4,96]{1,0:T(4,128)S(1)} collective-permute-done((f32[4,96]{1,0:T(4,128)S(1)}, f32[4,96]{1,0:T(4,128)S(1)}, u32[]{:S(2)}, u32[]{:S(2)}) %collective-permute-start.1) | collective-permute-done | bytes 1568 | tf_op jit(solution)/shard_map/ppermute | solution.py:261
  19.3 0.6 merge_pair.1
  19.9 1.7 %collective-permute-done.3.refs_0_ = f32[232,128]{1,0:T(8,128)S(1)} collective-permute-done((f32[232,128]{1,0:T(8,128)S(1)}, f32[232,128]{1,0:T(8,128)S(1)}, u32[]{:S(2)}, u32[]{:S(2)}) %collective-permute-start.3) | collective-permute-done | bytes 118816 | tf_op jit(solution)/shard_map/ppermute | solution.py:256
  21.5 0.6 merge_on.1
  22.2 8.8 %collective-permute-start.5 = (f32[256,128]{1,0:T(8,128)S(1)}, f32[256,128]{1,0:T(8,128)S(1)}, u32[]{:S(2)}, u32[]{:S(2)}) collective-permute-start(f32[256,128]{1,0:T(8,128)S(1)} %get-tuple-element.26), channel_id=1, source_target_pairs={{0,256},{64,320},{128,384},{192,448},{256,0},{320,64},{384,128},{4... | collective-permute-start | bytes 393224 | tf_op jit(solution)/shard_map/ppermute | solution.py:256
  31.0 3.5 %collective-permute-start.2 = (f32[240,128]{1,0:T(8,128)S(1)}, f32[240,128]{1,0:T(8,128)S(1)}, u32[]{:S(2)}, u32[]{:S(2)}) collective-permute-start(f32[240,128]{1,0:T(8,128)S(1)} %get-tuple-element.21.refs_4_), channel_id=1, source_target_pairs={{0,128},{64,192},{128,0},{192,64},{256,384},{320,448},{384,256},{4... | collective-permute-start | bytes 368648 | tf_op jit(solution)/shard_map/ppermute | solution.py:256
  34.6 10.1 %collective-permute-start.6 = (f32[4,96]{1,0:T(4,128)S(1)}, f32[4,96]{1,0:T(4,128)S(1)}, u32[]{:S(2)}, u32[]{:S(2)}) collective-permute-start(f32[4,96]{1,0:T(4,128)S(1)} %get-tuple-element.27), channel_id=1, source_target_pairs={{1,2},{3,4},{5,6},{7,8},{9,10},{11,12},{13,14},{15,16},{17,18},{19... | collective-permute-start | bytes 4616 | tf_op jit(solution)/shard_map/ppermute | solution.py:261
  44.6 3.2 %collective-permute-done.6.late = f32[4,96]{1,0:T(4,128)S(1)} collective-permute-done((f32[4,96]{1,0:T(4,128)S(1)}, f32[4,96]{1,0:T(4,128)S(1)}, u32[]{:S(2)}, u32[]{:S(2)}) %collective-permute-start.6) | collective-permute-done | bytes 1568 | tf_op jit(solution)/shard_map/ppermute | solution.py:261
  47.8 0.8 %factor.1.a = f32[112,128]{1,0:T(8,128)S(1)} custom-call(s32[3]{0:T(128)S(1)} %pad_add_fusion.ids, f32[240,128]{1,0:T(8,128)S(1)} %get-tuple-element.20.mine, f32[240,128]{1,0:T(8,128)S(1)} %collective-permute-done.2.two, f32[256,128]{1,0:T(8,128)S(1)} %collective-permute-done.5.recv, f32[4,96]{1,0:T(4,128)S(1)} %collective-permute-done.1.near, ...), custom_call_target="tpu_custom_call" | custom-call | flops 200000 | bytes 535552 | tf_op jit(solution)/shard_map/factor/pallas_call | solution.py:30
  48.6 2.1 %collective-permute-start.7 = (f32[112,128]{1,0:T(8,128)S(1)}, f32[112,128]{1,0:T(8,128)S(1)}, u32[]{:S(2)}, u32[]{:S(2)}) collective-permute-start(f32[112,128]{1,0:T(8,128)S(1)} %factor.1.a), channel_id=1, source_target_pairs={{0,256},{64,320},{128,384},{192,448},{256,0},{320,64},{384,128},{4... | collective-permute-start | bytes 172040 | tf_op jit(solution)/shard_map/ppermute | solution.py:256
  50.7 7.4 %collective-permute-done.7.b = f32[112,128]{1,0:T(8,128)S(1)} collective-permute-done((f32[112,128]{1,0:T(8,128)S(1)}, f32[112,128]{1,0:T(8,128)S(1)}, u32[]{:S(2)}, u32[]{:S(2)}) %collective-permute-start.7) | collective-permute-done | bytes 57376 | tf_op jit(solution)/shard_map/ppermute | solution.py:256
  58.6 4.6 %collective-permute-start.10 = (f32[224,128]{1,0:T(8,128)S(1)}, f32[224,128]{1,0:T(8,128)S(1)}, u32[]{:S(2)}, u32[]{:S(2)}) collective-permute-start(f32[224,128]{1,0:T(8,128)S(1)} %join.1.own), channel_id=1, source_target_pairs={{0,192},{64,128},{128,64},{192,0},{256,448},{320,384},{384,320},{4... | collective-permute-start | bytes 344072 | tf_op jit(solution)/shard_map/ppermute | solution.py:256
  63.3 5.5 %collective-permute-start.9 = (f32[224,128]{1,0:T(8,128)S(1)}, f32[224,128]{1,0:T(8,128)S(1)}, u32[]{:S(2)}, u32[]{:S(2)}) collective-permute-start(f32[224,128]{1,0:T(8,128)S(1)} %join.1.own), channel_id=1, source_target_pairs={{0,128},{64,192},{128,0},{192,64},{256,384},{320,448},{384,256},{4... | collective-permute-start | bytes 344072 | tf_op jit(solution)/shard_map/ppermute | solution.py:256
  68.7 1.9 %collective-permute-start.8 = (f32[224,128]{1,0:T(8,128)S(1)}, f32[224,128]{1,0:T(8,128)S(1)}, u32[]{:S(2)}, u32[]{:S(2)}) collective-permute-start(f32[224,128]{1,0:T(8,128)S(1)} %join.1.own), channel_id=1, source_target_pairs={{0,64},{64,0},{128,192},{192,128},{256,320},{320,256},{384,448},{4... | collective-permute-start | bytes 344072 | tf_op jit(solution)/shard_map/ppermute | solution.py:256
  70.7 2.7 %collective-permute-done.9.two = f32[224,128]{1,0:T(8,128)S(1)} collective-permute-done((f32[224,128]{1,0:T(8,128)S(1)}, f32[224,128]{1,0:T(8,128)S(1)}, u32[]{:S(2)}, u32[]{:S(2)}) %collective-permute-start.9) | collective-permute-done | bytes 114720 | tf_op jit(solution)/shard_map/ppermute | solution.py:256
  73.4 1.2 %collective-permute-done.8.one = f32[224,128]{1,0:T(8,128)S(1)} collective-permute-done((f32[224,128]{1,0:T(8,128)S(1)}, f32[224,128]{1,0:T(8,128)S(1)}, u32[]{:S(2)}, u32[]{:S(2)}) %collective-permute-start.8) | collective-permute-done | bytes 114720 | tf_op jit(solution)/shard_map/ppermute | solution.py:256
  74.6 2.0 %output.1 = bf16[10,432,128]{2,1,0:T(8,128)(2,1)} custom-call(s32[3]{0:T(128)S(1)} %pad_add_fusion.ids, f32[224,128]{1,0:T(8,128)S(1)} %join.1.own, f32[224,128]{1,0:T(8,128)S(1)} %collective-permute-done.8.one, f32[224,128]{1,0:T(8,128)S(1)} %collective-permute-done.9.two, f32[224,128]{1,0:T(8,128)S(1)} %collective-permute-done.10.three, ...), custom_call_target="tpu_custom_call" | custom-call | flops 2000000 | bytes 2670592 | tf_op jit(solution)/shard_map/output/pallas_call | solution.py:30
  (11 shorter events, 0.6 us)
Async XLA Ops:
  0.1 0.9 %copy-start.1 = (f32[4,72,96]{2,1,0:T(8,128)S(1)}, f32[4,72,96]{2,1,0:T(8,128)}, u32[]{:S(2)}) copy-start(f32[4,72,96]{2,1,0:T(8,128)} %fine.1) | copy-start | bytes 331780
  1.0 0.7 copy-start.2
  4.9 14.4 %collective-permute-start = (f32[696,128]{1,0:T(8,128)S(1)}, f32[696,128]{1,0:T(8,128)S(1)}, u32[]{:S(2)}, u32[]{:S(2)}) collective-permute-start(f32[696,128]{1,0:T(8,128)S(1)} %get-tuple-element.18), channel_id=1, source_target_pairs={{0,64},{64,0},{128,192},{192,128},{256,320},{320,256},{384,448},{4... | collective-permute-start | bytes 1069064 | tf_op jit(solution)/shard_map/ppermute | solution.py:256
  8.4 13.1 %collective-permute-start.3 = (f32[232,128]{1,0:T(8,128)S(1)}, f32[232,128]{1,0:T(8,128)S(1)}, u32[]{:S(2)}, u32[]{:S(2)}) collective-permute-start(f32[232,128]{1,0:T(8,128)S(1)} %get-tuple-element.22), channel_id=1, source_target_pairs={{0,192},{64,128},{128,64},{192,0},{256,448},{320,384},{384,320},{4... | collective-permute-start | bytes 356360 | tf_op jit(solution)/shard_map/ppermute | solution.py:256
  13.1 8.5 %collective-permute-start.4 = (f32[232,128]{1,0:T(8,128)S(1)}, f32[232,128]{1,0:T(8,128)S(1)}, u32[]{:S(2)}, u32[]{:S(2)}) collective-permute-start(f32[232,128]{1,0:T(8,128)S(1)} %get-tuple-element.23), channel_id=1, source_target_pairs={{0,128},{64,192},{128,0},{192,64},{256,384},{320,448},{384,256},{4... | collective-permute-start | bytes 356360 | tf_op jit(solution)/shard_map/ppermute | solution.py:256
  15.3 4.0 %collective-permute-start.1 = (f32[4,96]{1,0:T(4,128)S(1)}, f32[4,96]{1,0:T(4,128)S(1)}, u32[]{:S(2)}, u32[]{:S(2)}) collective-permute-start(f32[4,96]{1,0:T(4,128)S(1)} %get-tuple-element.19), channel_id=1, source_target_pairs={{0,1},{2,3},{4,5},{6,7},{8,9},{10,11},{12,13},{14,15},{16,17},{18,... | collective-permute-start | bytes 4616 | tf_op jit(solution)/shard_map/ppermute | solution.py:261
  19.3 55.3 %copy-start = (bf16[10,4,36,384]{3,1,2,0:T(4,128)(2,1)S(1)}, bf16[10,4,36,384]{3,1,2,0:T(4,128)(2,1)}, u32[]{:S(2)}) copy-start(bf16[10,4,36,384]{3,1,2,0:T(4,128)(2,1)} %param.9) | copy-start | bytes 3317764
  22.2 25.6 %collective-permute-start.5 = (f32[256,128]{1,0:T(8,128)S(1)}, f32[256,128]{1,0:T(8,128)S(1)}, u32[]{:S(2)}, u32[]{:S(2)}) collective-permute-start(f32[256,128]{1,0:T(8,128)S(1)} %get-tuple-element.26), channel_id=1, source_target_pairs={{0,256},{64,320},{128,384},{192,448},{256,0},{320,64},{384,128},{4... | collective-permute-start | bytes 393224 | tf_op jit(solution)/shard_map/ppermute | solution.py:256
  31.0 16.8 %collective-permute-start.2 = (f32[240,128]{1,0:T(8,128)S(1)}, f32[240,128]{1,0:T(8,128)S(1)}, u32[]{:S(2)}, u32[]{:S(2)}) collective-permute-start(f32[240,128]{1,0:T(8,128)S(1)} %get-tuple-element.21.refs_4_), channel_id=1, source_target_pairs={{0,128},{64,192},{128,0},{192,64},{256,384},{320,448},{384,256},{4... | collective-permute-start | bytes 368648 | tf_op jit(solution)/shard_map/ppermute | solution.py:256
  34.6 13.2 %collective-permute-start.6 = (f32[4,96]{1,0:T(4,128)S(1)}, f32[4,96]{1,0:T(4,128)S(1)}, u32[]{:S(2)}, u32[]{:S(2)}) collective-permute-start(f32[4,96]{1,0:T(4,128)S(1)} %get-tuple-element.27), channel_id=1, source_target_pairs={{1,2},{3,4},{5,6},{7,8},{9,10},{11,12},{13,14},{15,16},{17,18},{19... | collective-permute-start | bytes 4616 | tf_op jit(solution)/shard_map/ppermute | solution.py:261
  48.6 9.5 %collective-permute-start.7 = (f32[112,128]{1,0:T(8,128)S(1)}, f32[112,128]{1,0:T(8,128)S(1)}, u32[]{:S(2)}, u32[]{:S(2)}) collective-permute-start(f32[112,128]{1,0:T(8,128)S(1)} %factor.1.a), channel_id=1, source_target_pairs={{0,256},{64,320},{128,384},{192,448},{256,0},{320,64},{384,128},{4... | collective-permute-start | bytes 172040 | tf_op jit(solution)/shard_map/ppermute | solution.py:256
  58.6 12.1 %collective-permute-start.10 = (f32[224,128]{1,0:T(8,128)S(1)}, f32[224,128]{1,0:T(8,128)S(1)}, u32[]{:S(2)}, u32[]{:S(2)}) collective-permute-start(f32[224,128]{1,0:T(8,128)S(1)} %join.1.own), channel_id=1, source_target_pairs={{0,192},{64,128},{128,64},{192,0},{256,448},{320,384},{384,320},{4... | collective-permute-start | bytes 344072 | tf_op jit(solution)/shard_map/ppermute | solution.py:256
  63.3 10.1 %collective-permute-start.9 = (f32[224,128]{1,0:T(8,128)S(1)}, f32[224,128]{1,0:T(8,128)S(1)}, u32[]{:S(2)}, u32[]{:S(2)}) collective-permute-start(f32[224,128]{1,0:T(8,128)S(1)} %join.1.own), channel_id=1, source_target_pairs={{0,128},{64,192},{128,0},{192,64},{256,384},{320,448},{384,256},{4... | collective-permute-start | bytes 344072 | tf_op jit(solution)/shard_map/ppermute | solution.py:256
  68.7 5.8 %collective-permute-start.8 = (f32[224,128]{1,0:T(8,128)S(1)}, f32[224,128]{1,0:T(8,128)S(1)}, u32[]{:S(2)}, u32[]{:S(2)}) collective-permute-start(f32[224,128]{1,0:T(8,128)S(1)} %join.1.own), channel_id=1, source_target_pairs={{0,64},{64,0},{128,192},{192,128},{256,320},{320,256},{384,448},{4... | collective-permute-start | bytes 344072 | tf_op jit(solution)/shard_map/ppermute | solution.py:256

commit v6 on v5

--- a/solution.py
+++ b/solution.py
@@ -55,17 +55,15 @@
     return jnp.sum(jnp.where(diagonal, taps[t : t + 1, :], 0.0), axis=1, keepdims=True)
 
 
-def first_kernel(ids, prior, post, fine, taps, weights, *refs):
-    outs, (near, late, edge), (members, rows, tap, weight, sems, full, block) = refs[:5], refs[5:8], refs[8:]
+def first_kernel(ids, prior, post, packed, weights, *refs):
+    outs, (near, late, edge), (members, rows, weight, sems, full, block) = refs[:5], refs[5:8], refs[8:]
     m = ids[0]
     copies = [
         pltpu.make_async_copy(src, dst, sems.at[i])
         for i, (src, dst) in enumerate(
             (
-                (fine, rows.at[:, pl.ds(8, 72), :]),
                 (weights.at[pl.ds(pl.multiple_of(96 * m, 32), 96), :], weight.at[0]),
                 (weights.at[pl.ds(pl.multiple_of(96 * (m ^ ids[2]), 32), 96), :], weight.at[1]),
-                (taps, tap),
                 (prior, members.at[0]),
                 (post, members.at[1]),
             )
@@ -73,10 +71,12 @@
     ]
     for copy in copies:
         copy.start()
-    for copy in copies[:4]:
+    for copy in copies[:2]:
         copy.wait()
+    tap = jnp.concatenate([packed[t, 72:73, 0:36] for t in range(4)], axis=0)
     odd = ids[1] & 1
     for level in range(4):
+        rows[level, 8:80, :] = packed[level, 0:72, 0:96]
         first, last = rows[level, 8:9, :], rows[level, 79:80, :]
         near[level : level + 1, :] = jnp.where(odd == 1, first, last)
         late[level : level + 1, :] = jnp.where(odd == 1, last, first)
@@ -97,18 +97,19 @@
             block[at : at + 8, :] = part[row : row + 8] + pltpu.roll(part[row + 8 : row + 16], 64, 1)
             block[at + 8 : at + 9, :] = part[row + 16 : row + 17] + pltpu.roll(part[row + 17 : row + 18], 64, 1)
             block[at + 9 : at + 16, :] = jnp.zeros((7, 128), F32)
-    step = 144
+    step = 16
     for which in range(2):
-        copies[4 + which].wait()
+        copies[2 + which].wait()
         count = members.shape[1]
         for at in range(0, 432, step):
-            total = members[which, 0, at : at + step, :].astype(F32)
-            for i in range(1, count):
-                total = total + members[which, i, at : at + step, :].astype(F32)
+            values = [members[which, i, at : at + step, :].astype(F32) for i in range(count)]
+            total = values[0]
+            for value in values[1:]:
+                total = total + value
             mean = total / count
             square = jnp.zeros_like(total)
-            for i in range(count):
-                dev = members[which, i, at : at + step, :].astype(F32) - mean
+            for value in values:
+                dev = value - mean
                 square = square + dev * dev
             full[which, at : at + step, :] = total
             full[2 + which, at : at + step, :] = square
@@ -271,24 +272,25 @@
     prior, posterior = viewed(prior), viewed(posterior)
 
     row = jax.ShapeDtypeStruct((4, 96), F32)
+    packed = jnp.pad(fine_increment, ((0, 0), (0, 8), (0, 32)))
+    packed = packed + jnp.pad(row_taps[:, None, :], ((0, 0), (72, 7), (0, 92)))
     on, own, *sent, near, late, weights = call(
         first_kernel,
         "first",
         ids,
-        (prior, posterior, fine_increment, row_taps, col_weights),
+        (prior, posterior, packed, col_weights),
         rows_of(SENT, 2 * SENT, 3 * SENT, SENT, SENT) + (row, row, jax.ShapeDtypeStruct((2, 96, 128), F32)),
         [
             pltpu.VMEM((2, share, 432, 128), jnp.bfloat16),
             pltpu.VMEM((4, 88, 96), F32),
-            pltpu.VMEM((4, 36), F32),
             pltpu.VMEM((2, 96, 384), F32),
-            pltpu.SemaphoreType.DMA((6,)),
+            pltpu.SemaphoreType.DMA((4,)),
             pltpu.VMEM((4, 432, 128), F32),
             pltpu.VMEM((8 * SENT, 128), F32),
         ],
         mib=52,
         flops=12_000_000,
-        specs=[pl.BlockSpec(memory_space=pltpu.HBM)] * 5,
+        specs=[pl.BlockSpec(memory_space=pltpu.HBM)] * 2 + [VMEM, pl.BlockSpec(memory_space=pltpu.HBM)],
     )
     got = [swap(x, d) for d, x in enumerate(sent, 1)]
     near = swap_rows(near, 0)

time: 77 us -> 76.1 us (0.988)
  local copies, waits for them, and re-layouts: 1.6 us -> 0.01 us
  other arithmetic: 0.08 us -> 1.02 us
    unnamed x6 -> x2, local copies, waits for them, and re-layouts: 1.6 us -> 0.01 us
    add x0 -> x1, other arithmetic: none -> 0.94 us  [on_device(): packed = packed + jnp.pad(row_taps[:, None, :], ((0, 0), (72, 7), (0, 92)))]
where the time goes in v6:
time: 76.1 us; the launch traced here: 75.7 us
  starting transfers between devices  50.1 us (66%)
  waiting for transfers between devices  16.9 us (22%)
  Pallas kernels  7.52 us (10%)
  other arithmetic  1.02 us (1%)
    ppermute x9, starting transfers between devices, swap(): return lax.ppermute(x, 'mem', [(i, i ^ distance) for i in range(mem)])  36.8 us
    ppermute x2, starting transfers between devices, swap_rows(): lax.ppermute(x, ('mem', 'hor'), [(i * hor + a, (i ^ (4 if a + b == 2 * mi...  13.3 us
    ppermute x9, waiting for transfers between devices, swap(): return lax.ppermute(x, 'mem', [(i, i ^ distance) for i in range(mem)])  13 us
    pallas_call x6, Pallas kernels, call(): pl.pallas_call(kernel, out_shape=out, in_specs=[SMEM] + (specs or [VMEM]...  7.52 us
    ppermute x2, waiting for transfers between devices, swap_rows(): lax.ppermute(x, ('mem', 'hor'), [(i * hor + a, (i ^ (4 if a + b == 2 * mi...  3.96 us
  transfers between devices with their start and end apart: 11, of which 6 were waited for; matrix products, arithmetic and copies ran while one was open for 0% of the time, Pallas kernels for 1%

profile of v6, /device:TPU:31, one launch (start us, length us, event | category | flops | bytes accessed | tf_op | source)
XLA Modules:
  0.0 75.7 jit_solution(7648116030401288209)
XLA Ops:
  0.0 0.9 %pad_add_fusion.packed = f32[4,80,128]{2,1,0:T(8,128)S(1)} fusion(f32[4,1,36]{2,1,0:T(1,128)} %bitcast.24, f32[4,72,96]{2,1,0:T(8,128)} %param.5), kind=kLoop, calls=%fused_computation | loop fusion | flops 40960 | bytes 275008 | tf_op jit(solution)/shard_map/add | solution.py:276
  1.0 3.0 %first.1 = (f32[232,128]{1,0:T(8,128)S(1)}, f32[464,128]{1,0:T(8,128)S(1)}, f32[696,128]{1,0:T(8,128)S(1)}, f32[232,128]{1,0:T(8,128)S(1)}, f32[232,128]{1,0:T(8...) custom-call(s32[3]{0:T(128)S(1)} %pad_add_fusion.1.ids, ...), custom_call_target="tpu_custom_call" | custom-call | flops 12000000 | bytes 4606976 | tf_op jit(solution)/shard_map/first/pallas_call | solution.py:30
  4.0 3.5 %collective-permute-start = (f32[696,128]{1,0:T(8,128)S(1)}, f32[696,128]{1,0:T(8,128)S(1)}, u32[]{:S(2)}, u32[]{:S(2)}) collective-permute-start(f32[696,128]{1,0:T(8,128)S(1)} %get-tuple-element.18), channel_id=1, source_target_pairs={{0,64},{64,0},{128,192},{192,128},{256,320},{320,256},{384,448},{4... | collective-permute-start | bytes 1069064 | tf_op jit(solution)/shard_map/ppermute | solution.py:257
  7.6 4.6 %collective-permute-start.3 = (f32[232,128]{1,0:T(8,128)S(1)}, f32[232,128]{1,0:T(8,128)S(1)}, u32[]{:S(2)}, u32[]{:S(2)}) collective-permute-start(f32[232,128]{1,0:T(8,128)S(1)} %get-tuple-element.22), channel_id=1, source_target_pairs={{0,192},{64,128},{128,64},{192,0},{256,448},{320,384},{384,320},{4... | collective-permute-start | bytes 356360 | tf_op jit(solution)/shard_map/ppermute | solution.py:257
  12.2 2.2 %collective-permute-start.4 = (f32[232,128]{1,0:T(8,128)S(1)}, f32[232,128]{1,0:T(8,128)S(1)}, u32[]{:S(2)}, u32[]{:S(2)}) collective-permute-start(f32[232,128]{1,0:T(8,128)S(1)} %get-tuple-element.23), channel_id=1, source_target_pairs={{0,128},{64,192},{128,0},{192,64},{256,384},{320,448},{384,256},{4... | collective-permute-start | bytes 356360 | tf_op jit(solution)/shard_map/ppermute | solution.py:257
  14.4 3.2 %collective-permute-start.1 = (f32[4,96]{1,0:T(4,128)S(1)}, f32[4,96]{1,0:T(4,128)S(1)}, u32[]{:S(2)}, u32[]{:S(2)}) collective-permute-start(f32[4,96]{1,0:T(4,128)S(1)} %get-tuple-element.19), channel_id=1, source_target_pairs={{0,1},{2,3},{4,5},{6,7},{8,9},{10,11},{12,13},{14,15},{16,17},{18,... | collective-permute-start | bytes 4616 | tf_op jit(solution)/shard_map/ppermute | solution.py:262
  17.6 0.8 %collective-permute-done.1.near = f32[4,96]{1,0:T(4,128)S(1)} collective-permute-done((f32[4,96]{1,0:T(4,128)S(1)}, f32[4,96]{1,0:T(4,128)S(1)}, u32[]{:S(2)}, u32[]{:S(2)}) %collective-permute-start.1) | collective-permute-done | bytes 1568 | tf_op jit(solution)/shard_map/ppermute | solution.py:262
  18.4 0.6 merge_pair.1
  19.0 1.7 %collective-permute-done.3.refs_0_ = f32[232,128]{1,0:T(8,128)S(1)} collective-permute-done((f32[232,128]{1,0:T(8,128)S(1)}, f32[232,128]{1,0:T(8,128)S(1)}, u32[]{:S(2)}, u32[]{:S(2)}) %collective-permute-start.3) | collective-permute-done | bytes 118816 | tf_op jit(solution)/shard_map/ppermute | solution.py:257
  20.7 0.6 merge_on.1
  21.3 8.8 %collective-permute-start.5 = (f32[256,128]{1,0:T(8,128)S(1)}, f32[256,128]{1,0:T(8,128)S(1)}, u32[]{:S(2)}, u32[]{:S(2)}) collective-permute-start(f32[256,128]{1,0:T(8,128)S(1)} %get-tuple-element.26), channel_id=1, source_target_pairs={{0,256},{64,320},{128,384},{192,448},{256,0},{320,64},{384,128},{4... | collective-permute-start | bytes 393224 | tf_op jit(solution)/shard_map/ppermute | solution.py:257
  30.1 3.5 %collective-permute-start.2 = (f32[240,128]{1,0:T(8,128)S(1)}, f32[240,128]{1,0:T(8,128)S(1)}, u32[]{:S(2)}, u32[]{:S(2)}) collective-permute-start(f32[240,128]{1,0:T(8,128)S(1)} %get-tuple-element.21.refs_4_), channel_id=1, source_target_pairs={{0,128},{64,192},{128,0},{192,64},{256,384},{320,448},{384,256},{4... | collective-permute-start | bytes 368648 | tf_op jit(solution)/shard_map/ppermute | solution.py:257
  33.7 10.1 %collective-permute-start.6 = (f32[4,96]{1,0:T(4,128)S(1)}, f32[4,96]{1,0:T(4,128)S(1)}, u32[]{:S(2)}, u32[]{:S(2)}) collective-permute-start(f32[4,96]{1,0:T(4,128)S(1)} %get-tuple-element.27), channel_id=1, source_target_pairs={{1,2},{3,4},{5,6},{7,8},{9,10},{11,12},{13,14},{15,16},{17,18},{19... | collective-permute-start | bytes 4616 | tf_op jit(solution)/shard_map/ppermute | solution.py:262
  43.8 3.2 %collective-permute-done.6.late = f32[4,96]{1,0:T(4,128)S(1)} collective-permute-done((f32[4,96]{1,0:T(4,128)S(1)}, f32[4,96]{1,0:T(4,128)S(1)}, u32[]{:S(2)}, u32[]{:S(2)}) %collective-permute-start.6) | collective-permute-done | bytes 1568 | tf_op jit(solution)/shard_map/ppermute | solution.py:262
  46.9 0.8 %factor.1.a = f32[112,128]{1,0:T(8,128)S(1)} custom-call(s32[3]{0:T(128)S(1)} %pad_add_fusion.1.ids, f32[240,128]{1,0:T(8,128)S(1)} %get-tuple-element.20.mine, f32[240,128]{1,0:T(8,128)S(1)} %collective-permute-done.2.two, f32[256,128]{1,0:T(8,128)S(1)} %collective-permute-done.5.recv, f32[4,96]{1,0:T(4,128)S(1)} %collective-permute-done.1.near, ...), custom_call_target="tpu_custom_call" | custom-call | flops 200000 | bytes 535552 | tf_op jit(solution)/shard_map/factor/pallas_call | solution.py:30
  47.7 2.1 %collective-permute-start.7 = (f32[112,128]{1,0:T(8,128)S(1)}, f32[112,128]{1,0:T(8,128)S(1)}, u32[]{:S(2)}, u32[]{:S(2)}) collective-permute-start(f32[112,128]{1,0:T(8,128)S(1)} %factor.1.a), channel_id=1, source_target_pairs={{0,256},{64,320},{128,384},{192,448},{256,0},{320,64},{384,128},{4... | collective-permute-start | bytes 172040 | tf_op jit(solution)/shard_map/ppermute | solution.py:257
  49.8 7.4 %collective-permute-done.7.b = f32[112,128]{1,0:T(8,128)S(1)} collective-permute-done((f32[112,128]{1,0:T(8,128)S(1)}, f32[112,128]{1,0:T(8,128)S(1)}, u32[]{:S(2)}, u32[]{:S(2)}) %collective-permute-start.7) | collective-permute-done | bytes 57376 | tf_op jit(solution)/shard_map/ppermute | solution.py:257
  57.2 0.5 join.1.own
  57.7 4.6 %collective-permute-start.10 = (f32[224,128]{1,0:T(8,128)S(1)}, f32[224,128]{1,0:T(8,128)S(1)}, u32[]{:S(2)}, u32[]{:S(2)}) collective-permute-start(f32[224,128]{1,0:T(8,128)S(1)} %join.1.own), channel_id=1, source_target_pairs={{0,192},{64,128},{128,64},{192,0},{256,448},{320,384},{384,320},{4... | collective-permute-start | bytes 344072 | tf_op jit(solution)/shard_map/ppermute | solution.py:257
  62.4 5.5 %collective-permute-start.9 = (f32[224,128]{1,0:T(8,128)S(1)}, f32[224,128]{1,0:T(8,128)S(1)}, u32[]{:S(2)}, u32[]{:S(2)}) collective-permute-start(f32[224,128]{1,0:T(8,128)S(1)} %join.1.own), channel_id=1, source_target_pairs={{0,128},{64,192},{128,0},{192,64},{256,384},{320,448},{384,256},{4... | collective-permute-start | bytes 344072 | tf_op jit(solution)/shard_map/ppermute | solution.py:257
  67.9 1.9 %collective-permute-start.8 = (f32[224,128]{1,0:T(8,128)S(1)}, f32[224,128]{1,0:T(8,128)S(1)}, u32[]{:S(2)}, u32[]{:S(2)}) collective-permute-start(f32[224,128]{1,0:T(8,128)S(1)} %join.1.own), channel_id=1, source_target_pairs={{0,64},{64,0},{128,192},{192,128},{256,320},{320,256},{384,448},{4... | collective-permute-start | bytes 344072 | tf_op jit(solution)/shard_map/ppermute | solution.py:257
  69.8 2.7 %collective-permute-done.9.two = f32[224,128]{1,0:T(8,128)S(1)} collective-permute-done((f32[224,128]{1,0:T(8,128)S(1)}, f32[224,128]{1,0:T(8,128)S(1)}, u32[]{:S(2)}, u32[]{:S(2)}) %collective-permute-start.9) | collective-permute-done | bytes 114720 | tf_op jit(solution)/shard_map/ppermute | solution.py:257
  72.5 1.2 %collective-permute-done.8.one = f32[224,128]{1,0:T(8,128)S(1)} collective-permute-done((f32[224,128]{1,0:T(8,128)S(1)}, f32[224,128]{1,0:T(8,128)S(1)}, u32[]{:S(2)}, u32[]{:S(2)}) %collective-permute-start.8) | collective-permute-done | bytes 114720 | tf_op jit(solution)/shard_map/ppermute | solution.py:257
  73.7 2.0 %output.1 = bf16[10,432,128]{2,1,0:T(8,128)(2,1)} custom-call(s32[3]{0:T(128)S(1)} %pad_add_fusion.1.ids, f32[224,128]{1,0:T(8,128)S(1)} %join.1.own, f32[224,128]{1,0:T(8,128)S(1)} %collective-permute-done.8.one, f32[224,128]{1,0:T(8,128)S(1)} %collective-permute-done.9.two, f32[224,128]{1,0:T(8,128)S(1)} %collective-permute-done.10.three, ...), custom_call_target="tpu_custom_call" | custom-call | flops 2000000 | bytes 2670592 | tf_op jit(solution)/shard_map/output/pallas_call | solution.py:30
  (8 shorter events, 0.1 us)
Async XLA Ops:
  4.0 14.4 %collective-permute-start = (f32[696,128]{1,0:T(8,128)S(1)}, f32[696,128]{1,0:T(8,128)S(1)}, u32[]{:S(2)}, u32[]{:S(2)}) collective-permute-start(f32[696,128]{1,0:T(8,128)S(1)} %get-tuple-element.18), channel_id=1, source_target_pairs={{0,64},{64,0},{128,192},{192,128},{256,320},{320,256},{384,448},{4... | collective-permute-start | bytes 1069064 | tf_op jit(solution)/shard_map/ppermute | solution.py:257
  7.6 13.1 %collective-permute-start.3 = (f32[232,128]{1,0:T(8,128)S(1)}, f32[232,128]{1,0:T(8,128)S(1)}, u32[]{:S(2)}, u32[]{:S(2)}) collective-permute-start(f32[232,128]{1,0:T(8,128)S(1)} %get-tuple-element.22), channel_id=1, source_target_pairs={{0,192},{64,128},{128,64},{192,0},{256,448},{320,384},{384,320},{4... | collective-permute-start | bytes 356360 | tf_op jit(solution)/shard_map/ppermute | solution.py:257
  12.2 8.5 %collective-permute-start.4 = (f32[232,128]{1,0:T(8,128)S(1)}, f32[232,128]{1,0:T(8,128)S(1)}, u32[]{:S(2)}, u32[]{:S(2)}) collective-permute-start(f32[232,128]{1,0:T(8,128)S(1)} %get-tuple-element.23), channel_id=1, source_target_pairs={{0,128},{64,192},{128,0},{192,64},{256,384},{320,448},{384,256},{4... | collective-permute-start | bytes 356360 | tf_op jit(solution)/shard_map/ppermute | solution.py:257
  14.4 4.0 %collective-permute-start.1 = (f32[4,96]{1,0:T(4,128)S(1)}, f32[4,96]{1,0:T(4,128)S(1)}, u32[]{:S(2)}, u32[]{:S(2)}) collective-permute-start(f32[4,96]{1,0:T(4,128)S(1)} %get-tuple-element.19), channel_id=1, source_target_pairs={{0,1},{2,3},{4,5},{6,7},{8,9},{10,11},{12,13},{14,15},{16,17},{18,... | collective-permute-start | bytes 4616 | tf_op jit(solution)/shard_map/ppermute | solution.py:262
  18.4 55.3 %copy-start = (bf16[10,4,36,384]{3,1,2,0:T(4,128)(2,1)S(1)}, bf16[10,4,36,384]{3,1,2,0:T(4,128)(2,1)}, u32[]{:S(2)}) copy-start(bf16[10,4,36,384]{3,1,2,0:T(4,128)(2,1)} %param.9) | copy-start | bytes 3317764
  21.3 25.6 %collective-permute-start.5 = (f32[256,128]{1,0:T(8,128)S(1)}, f32[256,128]{1,0:T(8,128)S(1)}, u32[]{:S(2)}, u32[]{:S(2)}) collective-permute-start(f32[256,128]{1,0:T(8,128)S(1)} %get-tuple-element.26), channel_id=1, source_target_pairs={{0,256},{64,320},{128,384},{192,448},{256,0},{320,64},{384,128},{4... | collective-permute-start | bytes 393224 | tf_op jit(solution)/shard_map/ppermute | solution.py:257
  30.1 16.8 %collective-permute-start.2 = (f32[240,128]{1,0:T(8,128)S(1)}, f32[240,128]{1,0:T(8,128)S(1)}, u32[]{:S(2)}, u32[]{:S(2)}) collective-permute-start(f32[240,128]{1,0:T(8,128)S(1)} %get-tuple-element.21.refs_4_), channel_id=1, source_target_pairs={{0,128},{64,192},{128,0},{192,64},{256,384},{320,448},{384,256},{4... | collective-permute-start | bytes 368648 | tf_op jit(solution)/shard_map/ppermute | solution.py:257
  33.7 13.2 %collective-permute-start.6 = (f32[4,96]{1,0:T(4,128)S(1)}, f32[4,96]{1,0:T(4,128)S(1)}, u32[]{:S(2)}, u32[]{:S(2)}) collective-permute-start(f32[4,96]{1,0:T(4,128)S(1)} %get-tuple-element.27), channel_id=1, source_target_pairs={{1,2},{3,4},{5,6},{7,8},{9,10},{11,12},{13,14},{15,16},{17,18},{19... | collective-permute-start | bytes 4616 | tf_op jit(solution)/shard_map/ppermute | solution.py:262
  47.7 9.4 %collective-permute-start.7 = (f32[112,128]{1,0:T(8,128)S(1)}, f32[112,128]{1,0:T(8,128)S(1)}, u32[]{:S(2)}, u32[]{:S(2)}) collective-permute-start(f32[112,128]{1,0:T(8,128)S(1)} %factor.1.a), channel_id=1, source_target_pairs={{0,256},{64,320},{128,384},{192,448},{256,0},{320,64},{384,128},{4... | collective-permute-start | bytes 172040 | tf_op jit(solution)/shard_map/ppermute | solution.py:257
  57.7 12.1 %collective-permute-start.10 = (f32[224,128]{1,0:T(8,128)S(1)}, f32[224,128]{1,0:T(8,128)S(1)}, u32[]{:S(2)}, u32[]{:S(2)}) collective-permute-start(f32[224,128]{1,0:T(8,128)S(1)} %join.1.own), channel_id=1, source_target_pairs={{0,192},{64,128},{128,64},{192,0},{256,448},{320,384},{384,320},{4... | collective-permute-start | bytes 344072 | tf_op jit(solution)/shard_map/ppermute | solution.py:257
  62.4 10.1 %collective-permute-start.9 = (f32[224,128]{1,0:T(8,128)S(1)}, f32[224,128]{1,0:T(8,128)S(1)}, u32[]{:S(2)}, u32[]{:S(2)}) collective-permute-start(f32[224,128]{1,0:T(8,128)S(1)} %join.1.own), channel_id=1, source_target_pairs={{0,128},{64,192},{128,0},{192,64},{256,384},{320,448},{384,256},{4... | collective-permute-start | bytes 344072 | tf_op jit(solution)/shard_map/ppermute | solution.py:257
  67.9 5.8 %collective-permute-start.8 = (f32[224,128]{1,0:T(8,128)S(1)}, f32[224,128]{1,0:T(8,128)S(1)}, u32[]{:S(2)}, u32[]{:S(2)}) collective-permute-start(f32[224,128]{1,0:T(8,128)S(1)} %join.1.own), channel_id=1, source_target_pairs={{0,64},{64,0},{128,192},{192,128},{256,320},{320,256},{384,448},{4... | collective-permute-start | bytes 344072 | tf_op jit(solution)/shard_map/ppermute | solution.py:257

commit v7 on v6

--- a/solution.py
+++ b/solution.py
@@ -31,7 +31,7 @@
         kernel,
         out_shape=out,
         in_specs=[SMEM] + (specs or [VMEM] * len(args)),
-        out_specs=tuple(outs or (VMEM,) * len(out)) if many else VMEM,
+        out_specs=tuple(outs or (VMEM,) * len(out)) if many else (outs or VMEM),
         scratch_shapes=list(scratch),
         input_output_aliases=aliases or {},
         compiler_params=pltpu.CompilerParams(vmem_limit_bytes=mib * 2**20),
@@ -158,7 +158,7 @@
 
 
 def merge_on_kernel(members, ids, *refs):
-    merge(members, refs[3::-1], refs[6])
+    merge(members, refs[3::-1], refs[5])
 
 
 def placed(share, source):
@@ -208,7 +208,7 @@
     out[size : 2 * size, :] = b[...]
 
 
-def output_kernel(ids, own, one, two, three, post, out, block, factor, base):
+def output_kernel(ids, own, one, two, three, post, out, block, factor, base, result, sems):
     near = jnp.zeros((EDGE, 384), F32)
     late = near
     for d, ref in enumerate((own, one, two, three)):
@@ -230,12 +230,18 @@
     for ct in range(3):
         for at, part in ((4 * ct, above), (420 + 4 * ct, below)):
             base[at : at + 4, :] = base[at : at + 4, :] + part[:, 128 * ct : 128 * ct + 128]
-    step = 144
+    step, members = 48, post.shape[0]
+    copies = []
     for at in range(0, 432, step):
         scale = factor[at : at + step, :]
         shift = base[at : at + step, :]
-        for i in range(post.shape[0]):
-            out[i, at : at + step, :] = (shift + scale * post[i, at : at + step, :].astype(F32)).astype(jnp.bfloat16)
+        for i in range(members):
+            result[i, at : at + step, :] = (shift + scale * post[i, at : at + step, :].astype(F32)).astype(jnp.bfloat16)
+        part = (slice(None), pl.ds(at, step))
+        copies.append(pltpu.make_async_copy(result.at[part], out.at[part], sems.at[at // step]))
+        copies[-1].start()
+    for copy in copies:
+        copy.wait()
 
 
 def viewed(x):
@@ -298,15 +304,13 @@
         functools.partial(merge_pair_kernel, share), "merge_pair", ids, (own, got[0], near), rows_of(PAIR, PAIR)
     )
     anywhere = [pl.BlockSpec(memory_space=pl.ANY)]
-    send, late = call(
+    send = call(
         functools.partial(merge_on_kernel, share),
         "merge_on",
         ids,
-        (*got[::-1], on, pair, late),
-        (rows_of(KEPT), row),
-        specs=[VMEM] * 4 + anywhere * 2,
-        outs=[VMEM] + anywhere,
-        aliases={6: 1},
+        (*got[::-1], on, pair),
+        rows_of(KEPT),
+        specs=[VMEM] * 4 + anywhere,
     )
     recv = swap(send, 4)
     near = call(
@@ -325,9 +329,12 @@
         ids,
         (*gathered, posterior),
         jax.ShapeDtypeStruct(posterior.shape, jnp.bfloat16),
-        [pltpu.VMEM((8 * GATHER, 128), F32)] + [pltpu.VMEM((432, 128), F32)] * 2,
+        [pltpu.VMEM((8 * GATHER, 128), F32)]
+        + [pltpu.VMEM((432, 128), F32)] * 2
+        + [pltpu.VMEM(posterior.shape, jnp.bfloat16), pltpu.SemaphoreType.DMA((9,))],
         mib=10,
         flops=2_000_000,
+        outs=pl.BlockSpec(memory_space=pltpu.HBM),
     )
     out = out.reshape(share, 36, 3, 4, 128).transpose(0, 1, 3, 2, 4)
     return out.reshape(share, 36, 4, 384).transpose(0, 2, 1, 3)

time: 76.1 us -> 76.1 us (level)
  no operation moved by 1% of the time
where the time goes in v7:
time: 76.1 us; the launch traced here: 75.7 us
  starting transfers between devices  50.1 us (66%)
  waiting for transfers between devices  16.9 us (22%)
  Pallas kernels  7.51 us (10%)
  other arithmetic  1.02 us (1%)
    ppermute x9, starting transfers between devices, swap(): return lax.ppermute(x, 'mem', [(i, i ^ distance) for i in range(mem)])  36.8 us
    ppermute x2, starting transfers between devices, swap_rows(): lax.ppermute(x, ('mem', 'hor'), [(i * hor + a, (i ^ (4 if a + b == 2 * mi...  13.3 us
    ppermute x9, waiting for transfers between devices, swap(): return lax.ppermute(x, 'mem', [(i, i ^ distance) for i in range(mem)])  12.9 us
    pallas_call x6, Pallas kernels, call(): pl.pallas_call(kernel, out_shape=out, in_specs=[SMEM] + (specs or [VMEM]...  7.51 us
    ppermute x2, waiting for transfers between devices, swap_rows(): lax.ppermute(x, ('mem', 'hor'), [(i * hor + a, (i ^ (4 if a + b == 2 * mi...  3.96 us
  transfers between devices with their start and end apart: 11, of which 6 were waited for; matrix products, arithmetic and copies ran while one was open for 0% of the time, Pallas kernels for 1%

profile of v7, /device:TPU:31, one launch (start us, length us, event | category | flops | bytes accessed | tf_op | source)
XLA Modules:
  0.0 75.7 jit_solution(17004142564865692768)
XLA Ops:
  0.0 0.9 %pad_add_fusion.packed = f32[4,80,128]{2,1,0:T(8,128)S(1)} fusion(f32[4,1,36]{2,1,0:T(1,128)} %bitcast.24, f32[4,72,96]{2,1,0:T(8,128)} %param.5), kind=kLoop, calls=%fused_computation | loop fusion | flops 40960 | bytes 275008 | tf_op jit(solution)/shard_map/add | solution.py:282
  1.0 3.0 %first.1 = (f32[232,128]{1,0:T(8,128)S(1)}, f32[464,128]{1,0:T(8,128)S(1)}, f32[696,128]{1,0:T(8,128)S(1)}, f32[232,128]{1,0:T(8,128)S(1)}, f32[232,128]{1,0:T(8...) custom-call(s32[3]{0:T(128)S(1)} %pad_add_fusion.1.ids, ...), custom_call_target="tpu_custom_call" | custom-call | flops 12000000 | bytes 4606976 | tf_op jit(solution)/shard_map/first/pallas_call | solution.py:30
  4.0 3.5 %collective-permute-start = (f32[696,128]{1,0:T(8,128)S(1)}, f32[696,128]{1,0:T(8,128)S(1)}, u32[]{:S(2)}, u32[]{:S(2)}) collective-permute-start(f32[696,128]{1,0:T(8,128)S(1)} %get-tuple-element.16), channel_id=1, source_target_pairs={{0,64},{64,0},{128,192},{192,128},{256,320},{320,256},{384,448},{4... | collective-permute-start | bytes 1069064 | tf_op jit(solution)/shard_map/ppermute | solution.py:263
  7.6 4.6 %collective-permute-start.3 = (f32[232,128]{1,0:T(8,128)S(1)}, f32[232,128]{1,0:T(8,128)S(1)}, u32[]{:S(2)}, u32[]{:S(2)}) collective-permute-start(f32[232,128]{1,0:T(8,128)S(1)} %get-tuple-element.20), channel_id=1, source_target_pairs={{0,192},{64,128},{128,64},{192,0},{256,448},{320,384},{384,320},{4... | collective-permute-start | bytes 356360 | tf_op jit(solution)/shard_map/ppermute | solution.py:263
  12.2 2.2 %collective-permute-start.4 = (f32[232,128]{1,0:T(8,128)S(1)}, f32[232,128]{1,0:T(8,128)S(1)}, u32[]{:S(2)}, u32[]{:S(2)}) collective-permute-start(f32[232,128]{1,0:T(8,128)S(1)} %get-tuple-element.21), channel_id=1, source_target_pairs={{0,128},{64,192},{128,0},{192,64},{256,384},{320,448},{384,256},{4... | collective-permute-start | bytes 356360 | tf_op jit(solution)/shard_map/ppermute | solution.py:263
  14.4 3.2 %collective-permute-start.1 = (f32[4,96]{1,0:T(4,128)S(1)}, f32[4,96]{1,0:T(4,128)S(1)}, u32[]{:S(2)}, u32[]{:S(2)}) collective-permute-start(f32[4,96]{1,0:T(4,128)S(1)} %get-tuple-element.17), channel_id=1, source_target_pairs={{0,1},{2,3},{4,5},{6,7},{8,9},{10,11},{12,13},{14,15},{16,17},{18,... | collective-permute-start | bytes 4616 | tf_op jit(solution)/shard_map/ppermute | solution.py:268
  17.6 0.8 %collective-permute-done.1.near = f32[4,96]{1,0:T(4,128)S(1)} collective-permute-done((f32[4,96]{1,0:T(4,128)S(1)}, f32[4,96]{1,0:T(4,128)S(1)}, u32[]{:S(2)}, u32[]{:S(2)}) %collective-permute-start.1) | collective-permute-done | bytes 1568 | tf_op jit(solution)/shard_map/ppermute | solution.py:268
  18.4 0.6 merge_pair.1
  19.0 1.7 %collective-permute-done.3.refs_0_ = f32[232,128]{1,0:T(8,128)S(1)} collective-permute-done((f32[232,128]{1,0:T(8,128)S(1)}, f32[232,128]{1,0:T(8,128)S(1)}, u32[]{:S(2)}, u32[]{:S(2)}) %collective-permute-start.3) | collective-permute-done | bytes 118816 | tf_op jit(solution)/shard_map/ppermute | solution.py:263
  20.7 0.6 merge_on.1
  21.3 8.8 %collective-permute-start.5 = (f32[256,128]{1,0:T(8,128)S(1)}, f32[256,128]{1,0:T(8,128)S(1)}, u32[]{:S(2)}, u32[]{:S(2)}) collective-permute-start(f32[256,128]{1,0:T(8,128)S(1)} %merge_on.1), channel_id=1, source_target_pairs={{0,256},{64,320},{128,384},{192,448},{256,0},{320,64},{384,128},{4... | collective-permute-start | bytes 393224 | tf_op jit(solution)/shard_map/ppermute | solution.py:263
  30.1 3.5 %collective-permute-start.2 = (f32[240,128]{1,0:T(8,128)S(1)}, f32[240,128]{1,0:T(8,128)S(1)}, u32[]{:S(2)}, u32[]{:S(2)}) collective-permute-start(f32[240,128]{1,0:T(8,128)S(1)} %get-tuple-element.19.refs_4_), channel_id=1, source_target_pairs={{0,128},{64,192},{128,0},{192,64},{256,384},{320,448},{384,256},{4... | collective-permute-start | bytes 368648 | tf_op jit(solution)/shard_map/ppermute | solution.py:263
  33.7 10.1 %collective-permute-start.6 = (f32[4,96]{1,0:T(4,128)S(1)}, f32[4,96]{1,0:T(4,128)S(1)}, u32[]{:S(2)}, u32[]{:S(2)}) collective-permute-start(f32[4,96]{1,0:T(4,128)S(1)} %get-tuple-element.23), channel_id=1, source_target_pairs={{1,2},{3,4},{5,6},{7,8},{9,10},{11,12},{13,14},{15,16},{17,18},{19... | collective-permute-start | bytes 4616 | tf_op jit(solution)/shard_map/ppermute | solution.py:268
  43.8 3.2 %collective-permute-done.6.late = f32[4,96]{1,0:T(4,128)S(1)} collective-permute-done((f32[4,96]{1,0:T(4,128)S(1)}, f32[4,96]{1,0:T(4,128)S(1)}, u32[]{:S(2)}, u32[]{:S(2)}) %collective-permute-start.6) | collective-permute-done | bytes 1568 | tf_op jit(solution)/shard_map/ppermute | solution.py:268
  46.9 0.8 %factor.1.a = f32[112,128]{1,0:T(8,128)S(1)} custom-call(s32[3]{0:T(128)S(1)} %pad_add_fusion.1.ids, f32[240,128]{1,0:T(8,128)S(1)} %get-tuple-element.18.mine, f32[240,128]{1,0:T(8,128)S(1)} %collective-permute-done.2.two, f32[256,128]{1,0:T(8,128)S(1)} %collective-permute-done.5.recv, f32[4,96]{1,0:T(4,128)S(1)} %collective-permute-done.1.near, ...), custom_call_target="tpu_custom_call" | custom-call | flops 200000 | bytes 535552 | tf_op jit(solution)/shard_map/factor/pallas_call | solution.py:30
  47.7 2.1 %collective-permute-start.7 = (f32[112,128]{1,0:T(8,128)S(1)}, f32[112,128]{1,0:T(8,128)S(1)}, u32[]{:S(2)}, u32[]{:S(2)}) collective-permute-start(f32[112,128]{1,0:T(8,128)S(1)} %factor.1.a), channel_id=1, source_target_pairs={{0,256},{64,320},{128,384},{192,448},{256,0},{320,64},{384,128},{4... | collective-permute-start | bytes 172040 | tf_op jit(solution)/shard_map/ppermute | solution.py:263
  49.8 7.4 %collective-permute-done.7.b = f32[112,128]{1,0:T(8,128)S(1)} collective-permute-done((f32[112,128]{1,0:T(8,128)S(1)}, f32[112,128]{1,0:T(8,128)S(1)}, u32[]{:S(2)}, u32[]{:S(2)}) %collective-permute-start.7) | collective-permute-done | bytes 57376 | tf_op jit(solution)/shard_map/ppermute | solution.py:263
  57.2 0.5 join.1.own
  57.7 4.6 %collective-permute-start.10 = (f32[224,128]{1,0:T(8,128)S(1)}, f32[224,128]{1,0:T(8,128)S(1)}, u32[]{:S(2)}, u32[]{:S(2)}) collective-permute-start(f32[224,128]{1,0:T(8,128)S(1)} %join.1.own), channel_id=1, source_target_pairs={{0,192},{64,128},{128,64},{192,0},{256,448},{320,384},{384,320},{4... | collective-permute-start | bytes 344072 | tf_op jit(solution)/shard_map/ppermute | solution.py:263
  62.4 5.5 %collective-permute-start.9 = (f32[224,128]{1,0:T(8,128)S(1)}, f32[224,128]{1,0:T(8,128)S(1)}, u32[]{:S(2)}, u32[]{:S(2)}) collective-permute-start(f32[224,128]{1,0:T(8,128)S(1)} %join.1.own), channel_id=1, source_target_pairs={{0,128},{64,192},{128,0},{192,64},{256,384},{320,448},{384,256},{4... | collective-permute-start | bytes 344072 | tf_op jit(solution)/shard_map/ppermute | solution.py:263
  67.9 1.9 %collective-permute-start.8 = (f32[224,128]{1,0:T(8,128)S(1)}, f32[224,128]{1,0:T(8,128)S(1)}, u32[]{:S(2)}, u32[]{:S(2)}) collective-permute-start(f32[224,128]{1,0:T(8,128)S(1)} %join.1.own), channel_id=1, source_target_pairs={{0,64},{64,0},{128,192},{192,128},{256,320},{320,256},{384,448},{4... | collective-permute-start | bytes 344072 | tf_op jit(solution)/shard_map/ppermute | solution.py:263
  69.8 2.7 %collective-permute-done.9.two = f32[224,128]{1,0:T(8,128)S(1)} collective-permute-done((f32[224,128]{1,0:T(8,128)S(1)}, f32[224,128]{1,0:T(8,128)S(1)}, u32[]{:S(2)}, u32[]{:S(2)}) %collective-permute-start.9) | collective-permute-done | bytes 114720 | tf_op jit(solution)/shard_map/ppermute | solution.py:263
  72.5 1.2 %collective-permute-done.8.one = f32[224,128]{1,0:T(8,128)S(1)} collective-permute-done((f32[224,128]{1,0:T(8,128)S(1)}, f32[224,128]{1,0:T(8,128)S(1)}, u32[]{:S(2)}, u32[]{:S(2)}) %collective-permute-start.8) | collective-permute-done | bytes 114720 | tf_op jit(solution)/shard_map/ppermute | solution.py:263
  73.7 2.0 %output.1 = bf16[10,432,128]{2,1,0:T(8,128)(2,1)} custom-call(s32[3]{0:T(128)S(1)} %pad_add_fusion.1.ids, f32[224,128]{1,0:T(8,128)S(1)} %join.1.own, f32[224,128]{1,0:T(8,128)S(1)} %collective-permute-done.8.one, f32[224,128]{1,0:T(8,128)S(1)} %collective-permute-done.9.two, f32[224,128]{1,0:T(8,128)S(1)} %collective-permute-done.10.three, ...), custom_call_target="tpu_custom_call" | custom-call | flops 2000000 | bytes 2670592 | tf_op jit(solution)/shard_map/output/pallas_call | solution.py:30
  (8 shorter events, 0.1 us)
Async XLA Ops:
  4.0 14.4 %collective-permute-start = (f32[696,128]{1,0:T(8,128)S(1)}, f32[696,128]{1,0:T(8,128)S(1)}, u32[]{:S(2)}, u32[]{:S(2)}) collective-permute-start(f32[696,128]{1,0:T(8,128)S(1)} %get-tuple-element.16), channel_id=1, source_target_pairs={{0,64},{64,0},{128,192},{192,128},{256,320},{320,256},{384,448},{4... | collective-permute-start | bytes 1069064 | tf_op jit(solution)/shard_map/ppermute | solution.py:263
  7.6 13.1 %collective-permute-start.3 = (f32[232,128]{1,0:T(8,128)S(1)}, f32[232,128]{1,0:T(8,128)S(1)}, u32[]{:S(2)}, u32[]{:S(2)}) collective-permute-start(f32[232,128]{1,0:T(8,128)S(1)} %get-tuple-element.20), channel_id=1, source_target_pairs={{0,192},{64,128},{128,64},{192,0},{256,448},{320,384},{384,320},{4... | collective-permute-start | bytes 356360 | tf_op jit(solution)/shard_map/ppermute | solution.py:263
  12.2 8.5 %collective-permute-start.4 = (f32[232,128]{1,0:T(8,128)S(1)}, f32[232,128]{1,0:T(8,128)S(1)}, u32[]{:S(2)}, u32[]{:S(2)}) collective-permute-start(f32[232,128]{1,0:T(8,128)S(1)} %get-tuple-element.21), channel_id=1, source_target_pairs={{0,128},{64,192},{128,0},{192,64},{256,384},{320,448},{384,256},{4... | collective-permute-start | bytes 356360 | tf_op jit(solution)/shard_map/ppermute | solution.py:263
  14.4 4.0 %collective-permute-start.1 = (f32[4,96]{1,0:T(4,128)S(1)}, f32[4,96]{1,0:T(4,128)S(1)}, u32[]{:S(2)}, u32[]{:S(2)}) collective-permute-start(f32[4,96]{1,0:T(4,128)S(1)} %get-tuple-element.17), channel_id=1, source_target_pairs={{0,1},{2,3},{4,5},{6,7},{8,9},{10,11},{12,13},{14,15},{16,17},{18,... | collective-permute-start | bytes 4616 | tf_op jit(solution)/shard_map/ppermute | solution.py:268
  18.4 55.3 %copy-start = (bf16[10,4,36,384]{3,1,2,0:T(4,128)(2,1)S(1)}, bf16[10,4,36,384]{3,1,2,0:T(4,128)(2,1)}, u32[]{:S(2)}) copy-start(bf16[10,4,36,384]{3,1,2,0:T(4,128)(2,1)} %param.9) | copy-start | bytes 3317764
  21.3 25.6 %collective-permute-start.5 = (f32[256,128]{1,0:T(8,128)S(1)}, f32[256,128]{1,0:T(8,128)S(1)}, u32[]{:S(2)}, u32[]{:S(2)}) collective-permute-start(f32[256,128]{1,0:T(8,128)S(1)} %merge_on.1), channel_id=1, source_target_pairs={{0,256},{64,320},{128,384},{192,448},{256,0},{320,64},{384,128},{4... | collective-permute-start | bytes 393224 | tf_op jit(solution)/shard_map/ppermute | solution.py:263
  30.1 16.8 %collective-permute-start.2 = (f32[240,128]{1,0:T(8,128)S(1)}, f32[240,128]{1,0:T(8,128)S(1)}, u32[]{:S(2)}, u32[]{:S(2)}) collective-permute-start(f32[240,128]{1,0:T(8,128)S(1)} %get-tuple-element.19.refs_4_), channel_id=1, source_target_pairs={{0,128},{64,192},{128,0},{192,64},{256,384},{320,448},{384,256},{4... | collective-permute-start | bytes 368648 | tf_op jit(solution)/shard_map/ppermute | solution.py:263
  33.7 13.2 %collective-permute-start.6 = (f32[4,96]{1,0:T(4,128)S(1)}, f32[4,96]{1,0:T(4,128)S(1)}, u32[]{:S(2)}, u32[]{:S(2)}) collective-permute-start(f32[4,96]{1,0:T(4,128)S(1)} %get-tuple-element.23), channel_id=1, source_target_pairs={{1,2},{3,4},{5,6},{7,8},{9,10},{11,12},{13,14},{15,16},{17,18},{19... | collective-permute-start | bytes 4616 | tf_op jit(solution)/shard_map/ppermute | solution.py:268
  47.7 9.4 %collective-permute-start.7 = (f32[112,128]{1,0:T(8,128)S(1)}, f32[112,128]{1,0:T(8,128)S(1)}, u32[]{:S(2)}, u32[]{:S(2)}) collective-permute-start(f32[112,128]{1,0:T(8,128)S(1)} %factor.1.a), channel_id=1, source_target_pairs={{0,256},{64,320},{128,384},{192,448},{256,0},{320,64},{384,128},{4... | collective-permute-start | bytes 172040 | tf_op jit(solution)/shard_map/ppermute | solution.py:263
  57.7 12.1 %collective-permute-start.10 = (f32[224,128]{1,0:T(8,128)S(1)}, f32[224,128]{1,0:T(8,128)S(1)}, u32[]{:S(2)}, u32[]{:S(2)}) collective-permute-start(f32[224,128]{1,0:T(8,128)S(1)} %join.1.own), channel_id=1, source_target_pairs={{0,192},{64,128},{128,64},{192,0},{256,448},{320,384},{384,320},{4... | collective-permute-start | bytes 344072 | tf_op jit(solution)/shard_map/ppermute | solution.py:263
  62.4 10.1 %collective-permute-start.9 = (f32[224,128]{1,0:T(8,128)S(1)}, f32[224,128]{1,0:T(8,128)S(1)}, u32[]{:S(2)}, u32[]{:S(2)}) collective-permute-start(f32[224,128]{1,0:T(8,128)S(1)} %join.1.own), channel_id=1, source_target_pairs={{0,128},{64,192},{128,0},{192,64},{256,384},{320,448},{384,256},{4... | collective-permute-start | bytes 344072 | tf_op jit(solution)/shard_map/ppermute | solution.py:263
  67.9 5.8 %collective-permute-start.8 = (f32[224,128]{1,0:T(8,128)S(1)}, f32[224,128]{1,0:T(8,128)S(1)}, u32[]{:S(2)}, u32[]{:S(2)}) collective-permute-start(f32[224,128]{1,0:T(8,128)S(1)} %join.1.own), channel_id=1, source_target_pairs={{0,64},{64,0},{128,192},{192,128},{256,320},{320,256},{384,448},{4... | collective-permute-start | bytes 344072 | tf_op jit(solution)/shard_map/ppermute | solution.py:263

commit v8 on v7

--- a/solution.py
+++ b/solution.py
@@ -64,12 +64,11 @@
             (
                 (weights.at[pl.ds(pl.multiple_of(96 * m, 32), 96), :], weight.at[0]),
                 (weights.at[pl.ds(pl.multiple_of(96 * (m ^ ids[2]), 32), 96), :], weight.at[1]),
-                (prior, members.at[0]),
-                (post, members.at[1]),
+                *[(ref.at[pl.ds(i, 5)], members.at[j, pl.ds(i, 5)]) for j, ref in ((0, prior), (1, post)) for i in (0, 5)],
             )
         )
     ]
-    for copy in copies:
+    for copy in copies[2:] + copies[:2]:
         copy.start()
     for copy in copies[:2]:
         copy.wait()
@@ -99,7 +98,8 @@
             block[at + 9 : at + 16, :] = jnp.zeros((7, 128), F32)
     step = 16
     for which in range(2):
-        copies[2 + which].wait()
+        copies[2 + 2 * which].wait()
+        copies[3 + 2 * which].wait()
         count = members.shape[1]
         for at in range(0, 432, step):
             values = [members[which, i, at : at + step, :].astype(F32) for i in range(count)]
@@ -290,7 +290,7 @@
             pltpu.VMEM((2, share, 432, 128), jnp.bfloat16),
             pltpu.VMEM((4, 88, 96), F32),
             pltpu.VMEM((2, 96, 384), F32),
-            pltpu.SemaphoreType.DMA((4,)),
+            pltpu.SemaphoreType.DMA((6,)),
             pltpu.VMEM((4, 432, 128), F32),
             pltpu.VMEM((8 * SENT, 128), F32),
         ],

time: 76.1 us -> 77.2 us (1.014)
  waiting for transfers between devices: 16.9 us -> 18.5 us
  starting transfers between devices: 50.1 us -> 49 us
    ppermute x9, waiting for transfers between devices: 12.9 us -> 14 us  [swap(): return lax.ppermute(x, 'mem', [(i, i ^ distance) for i in range(mem)])]
where the time goes in v8:
time: 77.2 us; the launch traced here: 76.8 us
  starting transfers between devices  49 us (63%)
  waiting for transfers between devices  18.5 us (24%)
  Pallas kernels  8.16 us (11%)
  other arithmetic  1.02 us (1%)
    ppermute x9, starting transfers between devices, swap(): return lax.ppermute(x, 'mem', [(i, i ^ distance) for i in range(mem)])  36.2 us
    ppermute x9, waiting for transfers between devices, swap(): return lax.ppermute(x, 'mem', [(i, i ^ distance) for i in range(mem)])  14 us
    ppermute x2, starting transfers between devices, swap_rows(): lax.ppermute(x, ('mem', 'hor'), [(i * hor + a, (i ^ (4 if a + b == 2 * mi...  12.7 us
    pallas_call x6, Pallas kernels, call(): pl.pallas_call(kernel, out_shape=out, in_specs=[SMEM] + (specs or [VMEM]...  8.16 us
    ppermute x2, waiting for transfers between devices, swap_rows(): lax.ppermute(x, ('mem', 'hor'), [(i * hor + a, (i ^ (4 if a + b == 2 * mi...  4.43 us
  transfers between devices with their start and end apart: 11, of which 6 were waited for; matrix products, arithmetic and copies ran while one was open for 0% of the time, Pallas kernels for 1%

profile of v8, /device:TPU:31, one launch (start us, length us, event | category | flops | bytes accessed | tf_op | source)
XLA Modules:
  0.0 76.8 jit_solution(13301266842538233982)
XLA Ops:
  0.0 0.9 %pad_add_fusion.packed = f32[4,80,128]{2,1,0:T(8,128)S(1)} fusion(f32[4,1,36]{2,1,0:T(1,128)} %bitcast.24, f32[4,72,96]{2,1,0:T(8,128)} %param.5), kind=kLoop, calls=%fused_computation | loop fusion | flops 40960 | bytes 275008 | tf_op jit(solution)/shard_map/add | solution.py:282
  1.0 3.6 %first.1 = (f32[232,128]{1,0:T(8,128)S(1)}, f32[464,128]{1,0:T(8,128)S(1)}, f32[696,128]{1,0:T(8,128)S(1)}, f32[232,128]{1,0:T(8,128)S(1)}, f32[232,128]{1,0:T(8...) custom-call(s32[3]{0:T(128)S(1)} %pad_add_fusion.1.ids, ...), custom_call_target="tpu_custom_call" | custom-call | flops 12000000 | bytes 4606976 | tf_op jit(solution)/shard_map/first/pallas_call | solution.py:30
  4.7 3.5 %collective-permute-start = (f32[696,128]{1,0:T(8,128)S(1)}, f32[696,128]{1,0:T(8,128)S(1)}, u32[]{:S(2)}, u32[]{:S(2)}) collective-permute-start(f32[696,128]{1,0:T(8,128)S(1)} %get-tuple-element.16), channel_id=1, source_target_pairs={{0,64},{64,0},{128,192},{192,128},{256,320},{320,256},{384,448},{4... | collective-permute-start | bytes 1069064 | tf_op jit(solution)/shard_map/ppermute | solution.py:263
  8.2 4.6 %collective-permute-start.3 = (f32[232,128]{1,0:T(8,128)S(1)}, f32[232,128]{1,0:T(8,128)S(1)}, u32[]{:S(2)}, u32[]{:S(2)}) collective-permute-start(f32[232,128]{1,0:T(8,128)S(1)} %get-tuple-element.20), channel_id=1, source_target_pairs={{0,192},{64,128},{128,64},{192,0},{256,448},{320,384},{384,320},{4... | collective-permute-start | bytes 356360 | tf_op jit(solution)/shard_map/ppermute | solution.py:263
  12.8 2.2 %collective-permute-start.4 = (f32[232,128]{1,0:T(8,128)S(1)}, f32[232,128]{1,0:T(8,128)S(1)}, u32[]{:S(2)}, u32[]{:S(2)}) collective-permute-start(f32[232,128]{1,0:T(8,128)S(1)} %get-tuple-element.21), channel_id=1, source_target_pairs={{0,128},{64,192},{128,0},{192,64},{256,384},{320,448},{384,256},{4... | collective-permute-start | bytes 356360 | tf_op jit(solution)/shard_map/ppermute | solution.py:263
  15.0 3.1 %collective-permute-start.1 = (f32[4,96]{1,0:T(4,128)S(1)}, f32[4,96]{1,0:T(4,128)S(1)}, u32[]{:S(2)}, u32[]{:S(2)}) collective-permute-start(f32[4,96]{1,0:T(4,128)S(1)} %get-tuple-element.17), channel_id=1, source_target_pairs={{0,1},{2,3},{4,5},{6,7},{8,9},{10,11},{12,13},{14,15},{16,17},{18,... | collective-permute-start | bytes 4616 | tf_op jit(solution)/shard_map/ppermute | solution.py:268
  18.2 0.8 %collective-permute-done.1.near = f32[4,96]{1,0:T(4,128)S(1)} collective-permute-done((f32[4,96]{1,0:T(4,128)S(1)}, f32[4,96]{1,0:T(4,128)S(1)}, u32[]{:S(2)}, u32[]{:S(2)}) %collective-permute-start.1) | collective-permute-done | bytes 1568 | tf_op jit(solution)/shard_map/ppermute | solution.py:268
  19.0 0.6 merge_pair.1
  19.6 1.8 %collective-permute-done.3.refs_0_ = f32[232,128]{1,0:T(8,128)S(1)} collective-permute-done((f32[232,128]{1,0:T(8,128)S(1)}, f32[232,128]{1,0:T(8,128)S(1)}, u32[]{:S(2)}, u32[]{:S(2)}) %collective-permute-start.3) | collective-permute-done | bytes 118816 | tf_op jit(solution)/shard_map/ppermute | solution.py:263
  21.4 0.6 merge_on.1
  22.0 8.8 %collective-permute-start.5 = (f32[256,128]{1,0:T(8,128)S(1)}, f32[256,128]{1,0:T(8,128)S(1)}, u32[]{:S(2)}, u32[]{:S(2)}) collective-permute-start(f32[256,128]{1,0:T(8,128)S(1)} %merge_on.1), channel_id=1, source_target_pairs={{0,256},{64,320},{128,384},{192,448},{256,0},{320,64},{384,128},{4... | collective-permute-start | bytes 393224 | tf_op jit(solution)/shard_map/ppermute | solution.py:263
  30.8 3.9 %collective-permute-start.2 = (f32[240,128]{1,0:T(8,128)S(1)}, f32[240,128]{1,0:T(8,128)S(1)}, u32[]{:S(2)}, u32[]{:S(2)}) collective-permute-start(f32[240,128]{1,0:T(8,128)S(1)} %get-tuple-element.19.refs_4_), channel_id=1, source_target_pairs={{0,128},{64,192},{128,0},{192,64},{256,384},{320,448},{384,256},{4... | collective-permute-start | bytes 368648 | tf_op jit(solution)/shard_map/ppermute | solution.py:263
  34.8 9.6 %collective-permute-start.6 = (f32[4,96]{1,0:T(4,128)S(1)}, f32[4,96]{1,0:T(4,128)S(1)}, u32[]{:S(2)}, u32[]{:S(2)}) collective-permute-start(f32[4,96]{1,0:T(4,128)S(1)} %get-tuple-element.23), channel_id=1, source_target_pairs={{1,2},{3,4},{5,6},{7,8},{9,10},{11,12},{13,14},{15,16},{17,18},{19... | collective-permute-start | bytes 4616 | tf_op jit(solution)/shard_map/ppermute | solution.py:268
  44.4 3.6 %collective-permute-done.6.late = f32[4,96]{1,0:T(4,128)S(1)} collective-permute-done((f32[4,96]{1,0:T(4,128)S(1)}, f32[4,96]{1,0:T(4,128)S(1)}, u32[]{:S(2)}, u32[]{:S(2)}) %collective-permute-start.6) | collective-permute-done | bytes 1568 | tf_op jit(solution)/shard_map/ppermute | solution.py:268
  48.0 0.8 %factor.1.a = f32[112,128]{1,0:T(8,128)S(1)} custom-call(s32[3]{0:T(128)S(1)} %pad_add_fusion.1.ids, f32[240,128]{1,0:T(8,128)S(1)} %get-tuple-element.18.mine, f32[240,128]{1,0:T(8,128)S(1)} %collective-permute-done.2.two, f32[256,128]{1,0:T(8,128)S(1)} %collective-permute-done.5.recv, f32[4,96]{1,0:T(4,128)S(1)} %collective-permute-done.1.near, ...), custom_call_target="tpu_custom_call" | custom-call | flops 200000 | bytes 535552 | tf_op jit(solution)/shard_map/factor/pallas_call | solution.py:30
  48.8 1.9 %collective-permute-start.7 = (f32[112,128]{1,0:T(8,128)S(1)}, f32[112,128]{1,0:T(8,128)S(1)}, u32[]{:S(2)}, u32[]{:S(2)}) collective-permute-start(f32[112,128]{1,0:T(8,128)S(1)} %factor.1.a), channel_id=1, source_target_pairs={{0,256},{64,320},{128,384},{192,448},{256,0},{320,64},{384,128},{4... | collective-permute-start | bytes 172040 | tf_op jit(solution)/shard_map/ppermute | solution.py:263
  50.7 7.6 %collective-permute-done.7.b = f32[112,128]{1,0:T(8,128)S(1)} collective-permute-done((f32[112,128]{1,0:T(8,128)S(1)}, f32[112,128]{1,0:T(8,128)S(1)}, u32[]{:S(2)}, u32[]{:S(2)}) %collective-permute-start.7) | collective-permute-done | bytes 57376 | tf_op jit(solution)/shard_map/ppermute | solution.py:263
  58.3 0.5 join.1.own
  58.8 4.2 %collective-permute-start.10 = (f32[224,128]{1,0:T(8,128)S(1)}, f32[224,128]{1,0:T(8,128)S(1)}, u32[]{:S(2)}, u32[]{:S(2)}) collective-permute-start(f32[224,128]{1,0:T(8,128)S(1)} %join.1.own), channel_id=1, source_target_pairs={{0,192},{64,128},{128,64},{192,0},{256,448},{320,384},{384,320},{4... | collective-permute-start | bytes 344072 | tf_op jit(solution)/shard_map/ppermute | solution.py:263
  63.1 5.1 %collective-permute-start.9 = (f32[224,128]{1,0:T(8,128)S(1)}, f32[224,128]{1,0:T(8,128)S(1)}, u32[]{:S(2)}, u32[]{:S(2)}) collective-permute-start(f32[224,128]{1,0:T(8,128)S(1)} %join.1.own), channel_id=1, source_target_pairs={{0,128},{64,192},{128,0},{192,64},{256,384},{320,448},{384,256},{4... | collective-permute-start | bytes 344072 | tf_op jit(solution)/shard_map/ppermute | solution.py:263
  68.2 1.9 %collective-permute-start.8 = (f32[224,128]{1,0:T(8,128)S(1)}, f32[224,128]{1,0:T(8,128)S(1)}, u32[]{:S(2)}, u32[]{:S(2)}) collective-permute-start(f32[224,128]{1,0:T(8,128)S(1)} %join.1.own), channel_id=1, source_target_pairs={{0,64},{64,0},{128,192},{192,128},{256,320},{320,256},{384,448},{4... | collective-permute-start | bytes 344072 | tf_op jit(solution)/shard_map/ppermute | solution.py:263
  70.1 3.6 %collective-permute-done.9.two = f32[224,128]{1,0:T(8,128)S(1)} collective-permute-done((f32[224,128]{1,0:T(8,128)S(1)}, f32[224,128]{1,0:T(8,128)S(1)}, u32[]{:S(2)}, u32[]{:S(2)}) %collective-permute-start.9) | collective-permute-done | bytes 114720 | tf_op jit(solution)/shard_map/ppermute | solution.py:263
  73.7 1.1 %collective-permute-done.8.one = f32[224,128]{1,0:T(8,128)S(1)} collective-permute-done((f32[224,128]{1,0:T(8,128)S(1)}, f32[224,128]{1,0:T(8,128)S(1)}, u32[]{:S(2)}, u32[]{:S(2)}) %collective-permute-start.8) | collective-permute-done | bytes 114720 | tf_op jit(solution)/shard_map/ppermute | solution.py:263
  74.8 2.0 %output.1 = bf16[10,432,128]{2,1,0:T(8,128)(2,1)} custom-call(s32[3]{0:T(128)S(1)} %pad_add_fusion.1.ids, f32[224,128]{1,0:T(8,128)S(1)} %join.1.own, f32[224,128]{1,0:T(8,128)S(1)} %collective-permute-done.8.one, f32[224,128]{1,0:T(8,128)S(1)} %collective-permute-done.9.two, f32[224,128]{1,0:T(8,128)S(1)} %collective-permute-done.10.three, ...), custom_call_target="tpu_custom_call" | custom-call | flops 2000000 | bytes 2670592 | tf_op jit(solution)/shard_map/output/pallas_call | solution.py:30
  (8 shorter events, 0.1 us)
Async XLA Ops:
  4.7 14.3 %collective-permute-start = (f32[696,128]{1,0:T(8,128)S(1)}, f32[696,128]{1,0:T(8,128)S(1)}, u32[]{:S(2)}, u32[]{:S(2)}) collective-permute-start(f32[696,128]{1,0:T(8,128)S(1)} %get-tuple-element.16), channel_id=1, source_target_pairs={{0,64},{64,0},{128,192},{192,128},{256,320},{320,256},{384,448},{4... | collective-permute-start | bytes 1069064 | tf_op jit(solution)/shard_map/ppermute | solution.py:263
  8.2 13.2 %collective-permute-start.3 = (f32[232,128]{1,0:T(8,128)S(1)}, f32[232,128]{1,0:T(8,128)S(1)}, u32[]{:S(2)}, u32[]{:S(2)}) collective-permute-start(f32[232,128]{1,0:T(8,128)S(1)} %get-tuple-element.20), channel_id=1, source_target_pairs={{0,192},{64,128},{128,64},{192,0},{256,448},{320,384},{384,320},{4... | collective-permute-start | bytes 356360 | tf_op jit(solution)/shard_map/ppermute | solution.py:263
  12.8 8.5 %collective-permute-start.4 = (f32[232,128]{1,0:T(8,128)S(1)}, f32[232,128]{1,0:T(8,128)S(1)}, u32[]{:S(2)}, u32[]{:S(2)}) collective-permute-start(f32[232,128]{1,0:T(8,128)S(1)} %get-tuple-element.21), channel_id=1, source_target_pairs={{0,128},{64,192},{128,0},{192,64},{256,384},{320,448},{384,256},{4... | collective-permute-start | bytes 356360 | tf_op jit(solution)/shard_map/ppermute | solution.py:263
  15.0 4.0 %collective-permute-start.1 = (f32[4,96]{1,0:T(4,128)S(1)}, f32[4,96]{1,0:T(4,128)S(1)}, u32[]{:S(2)}, u32[]{:S(2)}) collective-permute-start(f32[4,96]{1,0:T(4,128)S(1)} %get-tuple-element.17), channel_id=1, source_target_pairs={{0,1},{2,3},{4,5},{6,7},{8,9},{10,11},{12,13},{14,15},{16,17},{18,... | collective-permute-start | bytes 4616 | tf_op jit(solution)/shard_map/ppermute | solution.py:268
  19.0 55.8 %copy-start = (bf16[10,4,36,384]{3,1,2,0:T(4,128)(2,1)S(1)}, bf16[10,4,36,384]{3,1,2,0:T(4,128)(2,1)}, u32[]{:S(2)}) copy-start(bf16[10,4,36,384]{3,1,2,0:T(4,128)(2,1)} %param.9) | copy-start | bytes 3317764
  22.0 26.0 %collective-permute-start.5 = (f32[256,128]{1,0:T(8,128)S(1)}, f32[256,128]{1,0:T(8,128)S(1)}, u32[]{:S(2)}, u32[]{:S(2)}) collective-permute-start(f32[256,128]{1,0:T(8,128)S(1)} %merge_on.1), channel_id=1, source_target_pairs={{0,256},{64,320},{128,384},{192,448},{256,0},{320,64},{384,128},{4... | collective-permute-start | bytes 393224 | tf_op jit(solution)/shard_map/ppermute | solution.py:263
  30.8 17.2 %collective-permute-start.2 = (f32[240,128]{1,0:T(8,128)S(1)}, f32[240,128]{1,0:T(8,128)S(1)}, u32[]{:S(2)}, u32[]{:S(2)}) collective-permute-start(f32[240,128]{1,0:T(8,128)S(1)} %get-tuple-element.19.refs_4_), channel_id=1, source_target_pairs={{0,128},{64,192},{128,0},{192,64},{256,384},{320,448},{384,256},{4... | collective-permute-start | bytes 368648 | tf_op jit(solution)/shard_map/ppermute | solution.py:263
  34.8 13.2 %collective-permute-start.6 = (f32[4,96]{1,0:T(4,128)S(1)}, f32[4,96]{1,0:T(4,128)S(1)}, u32[]{:S(2)}, u32[]{:S(2)}) collective-permute-start(f32[4,96]{1,0:T(4,128)S(1)} %get-tuple-element.23), channel_id=1, source_target_pairs={{1,2},{3,4},{5,6},{7,8},{9,10},{11,12},{13,14},{15,16},{17,18},{19... | collective-permute-start | bytes 4616 | tf_op jit(solution)/shard_map/ppermute | solution.py:268
  48.8 9.5 %collective-permute-start.7 = (f32[112,128]{1,0:T(8,128)S(1)}, f32[112,128]{1,0:T(8,128)S(1)}, u32[]{:S(2)}, u32[]{:S(2)}) collective-permute-start(f32[112,128]{1,0:T(8,128)S(1)} %factor.1.a), channel_id=1, source_target_pairs={{0,256},{64,320},{128,384},{192,448},{256,0},{320,64},{384,128},{4... | collective-permute-start | bytes 172040 | tf_op jit(solution)/shard_map/ppermute | solution.py:263
  58.8 11.2 %collective-permute-start.10 = (f32[224,128]{1,0:T(8,128)S(1)}, f32[224,128]{1,0:T(8,128)S(1)}, u32[]{:S(2)}, u32[]{:S(2)}) collective-permute-start(f32[224,128]{1,0:T(8,128)S(1)} %join.1.own), channel_id=1, source_target_pairs={{0,192},{64,128},{128,64},{192,0},{256,448},{320,384},{384,320},{4... | collective-permute-start | bytes 344072 | tf_op jit(solution)/shard_map/ppermute | solution.py:263
  63.1 10.6 %collective-permute-start.9 = (f32[224,128]{1,0:T(8,128)S(1)}, f32[224,128]{1,0:T(8,128)S(1)}, u32[]{:S(2)}, u32[]{:S(2)}) collective-permute-start(f32[224,128]{1,0:T(8,128)S(1)} %join.1.own), channel_id=1, source_target_pairs={{0,128},{64,192},{128,0},{192,64},{256,384},{320,448},{384,256},{4... | collective-permute-start | bytes 344072 | tf_op jit(solution)/shard_map/ppermute | solution.py:263
  68.2 6.6 %collective-permute-start.8 = (f32[224,128]{1,0:T(8,128)S(1)}, f32[224,128]{1,0:T(8,128)S(1)}, u32[]{:S(2)}, u32[]{:S(2)}) collective-permute-start(f32[224,128]{1,0:T(8,128)S(1)} %join.1.own), channel_id=1, source_target_pairs={{0,64},{64,0},{128,192},{192,128},{256,320},{320,256},{384,448},{4... | collective-permute-start | bytes 344072 | tf_op jit(solution)/shard_map/ppermute | solution.py:263
